TPU v7x, 32 devices: a whole 2x2x4 slice. The times are simulated.
32 devices in a mesh: list: 8 (over y, x, core), rep: 4 (over z).
Axes of the slice: x: 2, y: 2, z: 4, core: 2. Of those that a mesh axis runs over, the one named last changes fastest.
Arguments:
- memory_rows: bfloat16 [8192, 1024], P(('list', 'rep'))
- list_owner: int32 [8192, 1], P(('list', 'rep')), may hold values from 0 to 7; in each aligned block of 256 rows (0 to 255, 256 to 511, ...) at most 128 rows name the same one
- list_slot: int32 [8192], P(('list', 'rep')), may hold values from 0 to 2047
- pq_codes: int32 [8192, 16], P(('list', 'rep')), may hold values from 0 to 255
- valid_rows: int32 [32], P(('list', 'rep')), may hold values from 128 to 256
- centroids: bfloat16 [16384, 1024], P('list'), may hold values from -3 to 3
- codebook: float32 [16, 256, 64], replicated
Outputs:
- new_codebook: float32 [16, 256, 64], P('rep')
- row_error: float32 [8192], P(('list', 'rep'))
Inputs may be any that keep to these rules, and one draw needn't show every extreme that they name: `list_owner`: the rows of one device name one index of list at most 128 times, and some device's rows name one exactly 128 times.
All inputs are finite; a program needn't handle non-finite values.
Results may differ from a plain program's by a relative error of at most 0.0038.
Values may be sent and summed in bfloat16 or wider, within the bound.
No kernel may reach another device: no remote copies, remote signals or barrier semaphores. Data moves between devices by JAX's collectives and lax.ppermute only.
A program may use at most 128 MiB of HBM per device.

v0:
```python
import jax
import jax.numpy as jnp
from jax import lax
from jax.sharding import PartitionSpec as P

prior_weight = 4.0


def code_statistics(residual, pq_codes, is_live, codebook):
    row_count = residual.shape[0]
    subspaces = codebook.shape[0]
    code_count = codebook.shape[1]
    width_sub = codebook.shape[2]
    residual = jnp.where(is_live[:, None], residual, 0.0)
    recon = codebook[jnp.arange(subspaces)[None, :], pq_codes].reshape(
        row_count, subspaces * width_sub
    )
    row_error = jnp.where(is_live, jnp.mean((residual - recon) ** 2, axis=1), 0.0)
    rounded = (
        residual.astype(jnp.bfloat16).reshape(row_count, subspaces, width_sub).transpose(1, 0, 2)
    )
    codes_major = pq_codes.T

    def per_subspace(item):
        code_col, part_rows = item
        onehot = ((code_col[:, None] == jnp.arange(code_count)[None, :]) & is_live[:, None]).astype(
            jnp.bfloat16
        )
        sums_one = lax.dot_general(
            onehot, part_rows, (((0,), (0,)), ((), ())), preferred_element_type=jnp.float32
        )
        counts_one = jnp.sum(onehot.astype(jnp.float32), axis=0)
        return (sums_one, counts_one)

    sums, counts = lax.map(per_subspace, (codes_major, rounded))
    return (row_error, sums, counts)


def body(memory_rows, list_owner, list_slot, pq_codes, valid_rows, centroids, codebook):
    row_count = memory_rows.shape[0]
    width = memory_rows.shape[1]
    list_count = centroids.shape[0]
    owners = lax.axis_size("list")
    capacity = 4 * row_count // owners
    is_valid = jnp.arange(row_count) < valid_rows[0]
    target = list_owner[:, 0]
    onehot_dest = ((target[:, None] == jnp.arange(owners)[None, :]) & is_valid[:, None]).astype(
        jnp.int32
    )
    before = jnp.cumsum(onehot_dest, axis=0) - onehot_dest
    slot_rank = jnp.sum(before * onehot_dest, axis=1)
    position = jnp.where(is_valid, target * capacity + slot_rank, owners * capacity)
    taken = jnp.clip(position, 0, owners * capacity - 1)
    total_slots = owners * capacity
    send_rows = (
        jnp.zeros((total_slots, width), jnp.bfloat16).at[position].set(memory_rows, mode="drop")
    )
    send_slot = jnp.full((total_slots,), -1, jnp.int32).at[position].set(list_slot, mode="drop")
    send_codes = (
        jnp.zeros((total_slots, pq_codes.shape[1]), jnp.int32)
        .at[position]
        .set(pq_codes, mode="drop")
    )
    got_rows, got_slot, got_codes = (
        lax.all_to_all(
            send_rows.reshape(owners, capacity, width),
            "list",
            split_axis=0,
            concat_axis=0,
            tiled=True,
        ),
        lax.all_to_all(
            send_slot.reshape(owners, capacity), "list", split_axis=0, concat_axis=0, tiled=True
        ),
        lax.all_to_all(
            send_codes.reshape(owners, capacity, pq_codes.shape[1]),
            "list",
            split_axis=0,
            concat_axis=0,
            tiled=True,
        ),
    )
    got_rows = got_rows.reshape(total_slots, width)
    got_slot = got_slot.reshape(total_slots)
    got_codes = got_codes.reshape(total_slots, pq_codes.shape[1])
    is_live = got_slot >= 0
    centre = centroids[jnp.clip(got_slot, 0, list_count - 1)].astype(jnp.float32)
    residual = got_rows.astype(jnp.float32) - centre
    slot_error, sums, counts = code_statistics(residual, got_codes, is_live, codebook)
    returned = lax.all_to_all(
        slot_error.reshape(owners, capacity), "list", split_axis=0, concat_axis=0, tiled=True
    )
    row_error = jnp.where(is_valid, returned.reshape(total_slots)[taken], 0.0)
    subspaces = codebook.shape[0]
    replicas = lax.axis_size("rep")
    share = subspaces // replicas
    first_sub = lax.axis_index("rep") * share
    sums_all, counts_all = lax.psum((sums, counts), ("list", "rep"))
    sums_mine = lax.dynamic_slice_in_dim(sums_all, first_sub, share, 0)
    counts_mine = lax.dynamic_slice_in_dim(counts_all, first_sub, share, 0)
    old_mine = lax.dynamic_slice_in_dim(codebook, first_sub, share, 0)
    new_codebook = (sums_mine + prior_weight * old_mine) / (counts_mine[:, :, None] + prior_weight)
    return (new_codebook, row_error)


def solution(mesh):
    in_specs = (
        P(("list", "rep"), None),
        P(("list", "rep"), None),
        P(("list", "rep")),
        P(("list", "rep"), None),
        P(("list", "rep")),
        P("list", None),
        P(),
    )
    out_specs = (P("rep", None, None), P(("list", "rep")))
    return jax.shard_map(body, mesh=mesh, in_specs=in_specs, out_specs=out_specs, check_vma=False)
```

profile of v0, /device:TPU:0, one launch (start us, length us, event | category | flops | bytes accessed | tf_op | source)
XLA Modules:
  0.0 415.8 jit_solution(5310605735617684223)
XLA Ops:
  10.9 2.1 scatter_custom_fusion.1
  13.0 5.2 %all-to-all-start.1 = ((s32[8,1,128]{2,1,0:T(1,128)}), s32[8,1,128]{2,1,0:T(1,128)S(1)}, u32[]{:S(2)}, u32[]{:S(2)}) async-start(s32[8,1,128]{2,1,0:T(1,128)} %bitcast.13), calls=%async_computation.1 | async-start | bytes 8192 | tf_op jit(solution)/shard_map/all_to_all | solution.py:72
  19.0 1.3 scatter_custom_fusion
  21.1 1.8 all-to-all-done.1
  22.9 3.4 all-to-all-start
  26.2 3.8 scatter_custom_fusion.2
  30.0 1.2 all-to-all-done
  31.2 4.3 %all-to-all-start.2 = ((bf16[8,128,1024]{2,1,0:T(8,128)(2,1)}), bf16[8,128,1024]{2,1,0:T(8,128)(2,1)}, u32[]{:S(2)}, u32[]{:S(2)}) async-start(bf16[8,128,1024]{2,1,0:T(8,128)(2,1)} %bitcast.16), calls=%async_computation.2 | async-start | bytes 4194304 | tf_op jit(solution)/shard_map/all_to_all | solution.py:65
  36.4 8.8 %gather_fusion = bf16[1024,1024]{1,0:T(8,128)(2,1)} fusion(bf16[2048,1024]{1,0:T(8,128)(2,1)} %param.14, s32[1024]{0:T(1024)S(1)} %broadcast_clamp_fusion), kind=kCustom, calls=%fused_computation | custom fusion | bytes 4198400 | tf_op jit(solution)/shard_map/gather | solution.py:87
  45.2 4.1 copy.41
  49.3 4.0 convert_element_type.53
  53.9 176.0 %gather_fusion.1 = f32[16384,64]{1,0:T(8,128)} fusion(f32[16,256,64]{2,1,0:T(8,128)S(1)} %copy.45, s32[16384]{0:T(1024)S(1)} %reshape.188), kind=kCustom, calls=%fused_computation.1 | custom fusion | bytes 8519680 | tf_op jit(solution)/shard_map/gather | solution.py:15
  229.9 7.6 %gather.13 = f32[8,128,1024]{2,1,0:T(8,128)} reshape(f32[16384,64]{1,0:T(8,128)} %gather_fusion.1) | data formatting | bytes 8388608 | tf_op jit(solution)/shard_map/gather | solution.py:15
  237.5 4.3 %copy.39 = f32[8,128,1024]{1,0,2:T(8,128)} copy(bf16[8,128,1024]{2,1,0:T(8,128)(2,1)} %all-to-all-done.2) | data formatting | bytes 6291456 | tf_op jit(solution)/shard_map/convert_element_type | solution.py:88
  241.8 4.9 %reshape.177 = f32[1024,16,64]{0,2,1:T(8,128)} reshape(f32[8,128,1024]{1,0,2:T(8,128)} %copy.39) | data formatting | bytes 8388608 | tf_op jit(solution)/shard_map/convert_element_type | solution.py:88
  246.7 4.6 %fusion.9 = bf16[16,1024,64]{1,2,0:T(8,128)(2,1)S(1)} fusion(f32[1024,16,64]{0,2,1:T(8,128)} %reshape.177, f32[1024,16,64]{0,2,1:T(8,128)} %bitcast.70, pred[1024]{0:T(1024)(128)(4,1)S(1)} %fusion.25), kind=kLoop, calls=%fused_computation.20 | loop fusion | flops 3145728 | bytes 10486784 | tf_op jit(solution)/shard_map/transpose | solution.py:20
  251.3 24.5 %while.12 = (s32[]{:T(128)}, f32[16,256,64]{1,2,0:T(8,128)}, f32[16,256]{1,0:T(8,128)S(1)}, s32[16,1024]{1,0:T(8,128)S(1)}, pred[1024]{0:T(1024)(128)(4,1)S(1)},...) while((s32[]{:T(128)}, f32[16,256,64]{1,2,0:T(8,128)}, f32[16,256]{1,0:T(8,128)S(1)}, ...), condition=%wide.region_8.9_spmd, body=%wide.region_6.8_spmd.sunk | while | flops 35389184 | bytes 219237 | solution.py:35
  251.3 1.1 fusion.32
  275.8 5.0 %multiply_reduce_fusion = f32[8,128]{1,0:T(8,128)S(1)} fusion(f32[8,128,1024]{2,1,0:T(8,128)} %gather.13, f32[8,128,1024]{2,1,0:T(8,128)} %bitcast.69, pred[8,128]{1,0:T(8,128)(4,1)S(1)} %fusion.24, bf16[8,128,1024]{2,1,0:T(8,128)(2,1)} %all-to-all-done.2), kind=kLoop, calls=%fused_computation.18 | loop fusion | flops 6290432 | bytes 10490880 | tf_op jit(solution)/shard_map/reduce_sum | solution.py:18
  281.5 3.9 all-to-all-start.3
  285.3 41.1 %psum.15 = f32[16,256]{1,0:T(8,128)S(1)} all-reduce(f32[16,256]{1,0:T(8,128)S(1)} %get-tuple-element.36), channel_id=1, replica_groups=mesh['list'=8,'rep'=4] {'list','rep'}, use_global_device_ids=true, to_apply=%region_10.11 | all-reduce | flops 4096 | bytes 32768 | tf_op jit(solution)/shard_map/psum | solution.py:98
  326.4 1.4 gather_fusion.2
  328.4 78.8 %all-reduce.2.cloned.1.call-done = f32[16,256,64]{1,2,0:T(8,128)} async-done(((f32[16,256,64]{1,2,0:T(8,128)}), f32[16,256,64]{1,2,0:T(8,128)}) %all-reduce.2.cloned.1.call-update) | async-done | bytes 1048592 | tf_op jit(solution)/shard_map/psum | solution.py:98
  407.2 1.8 add_divide_fusion
  (99 shorter events, 30.0 us)
Async XLA Ops:
  7.2 28.6 %copy-start = (f32[16,256,64]{1,2,0:T(8,128)S(1)}, f32[16,256,64]{1,2,0:T(8,128)}, u32[]{:S(2)}) copy-start(f32[16,256,64]{1,2,0:T(8,128)} %param.15) | copy-start | bytes 3145732
  13.0 9.8 %all-to-all-start.1 = ((s32[8,1,128]{2,1,0:T(1,128)}), s32[8,1,128]{2,1,0:T(1,128)S(1)}, u32[]{:S(2)}, u32[]{:S(2)}) async-start(s32[8,1,128]{2,1,0:T(1,128)} %bitcast.13), calls=%async_computation.1 | async-start | bytes 8192 | tf_op jit(solution)/shard_map/all_to_all | solution.py:72
  22.9 8.3 %all-to-all-start = ((s32[8,128,16]{1,2,0:T(8,128)}), s32[8,128,16]{1,2,0:T(8,128)S(1)}, u32[]{:S(2)}, u32[]{:S(2)}) async-start(s32[8,128,16]{1,2,0:T(8,128)} %copy.36), calls=%async_computation | async-start | bytes 131072 | tf_op jit(solution)/shard_map/all_to_all | solution.py:75
  31.2 206.3 %all-to-all-start.2 = ((bf16[8,128,1024]{2,1,0:T(8,128)(2,1)}), bf16[8,128,1024]{2,1,0:T(8,128)(2,1)}, u32[]{:S(2)}, u32[]{:S(2)}) async-start(bf16[8,128,1024]{2,1,0:T(8,128)(2,1)} %bitcast.16), calls=%async_computation.2 | async-start | bytes 4194304 | tf_op jit(solution)/shard_map/all_to_all | solution.py:65
  35.5 371.6 %all-reduce.2.cloned.1.call-start = ((), (), s32[]{:S(2)}) async-start(), calls=%async_computation.4 | async-start | bytes 2097152 | tf_op jit(solution)/shard_map/psum | solution.py:98
  281.5 45.0 %all-to-all-start.3 = ((f32[8,1,128]{2,1,0:T(1,128)}), f32[8,1,128]{2,1,0:T(1,128)S(1)}, u32[]{:S(2)}, u32[]{:S(2)}) async-start(f32[8,1,128]{2,1,0:T(1,128)} %bitcast.25), calls=%async_computation.3 | async-start | bytes 8192 | tf_op jit(solution)/shard_map/all_to_all | solution.py:90
Sparse Core Ops, SparseCore 0:
  275.9 131.1 all-reduce.1
where the time goes:
time: 417 us; the launch traced here: 416 us
  local copies, waits for them, and re-layouts  218 us (52%)
  waiting for transfers between devices  81.8 us (20%)
  blocking collectives  41.1 us (10%)
  other arithmetic  25 us (6%)
  matrix products  17.6 us (4%)
  starting transfers between devices  16.9 us (4%)
  between operations  15 us (4%)
    gather x2, local copies, waits for them, and re-layouts, code_statistics(): codebook[jnp.arange(subspaces)[None, :], pq_codes]  184 us
    psum x1, waiting for transfers between devices, body(): sums_all, counts_all = lax.psum((sums, counts), ('list', 'rep'))  78.8 us
    psum x1, blocking collectives, body(): sums_all, counts_all = lax.psum((sums, counts), ('list', 'rep'))  41.1 us
    dot_general x16, matrix products, per_subspace(): lax.dot_general(onehot, part_rows, (((0,), (0,)), ((), ())), preferred_el...  17.6 us
    convert_element_type x2, local copies, waits for them, and re-layouts, body(): residual = got_rows.astype(jnp.float32) - centre  9.2 us
    gather x1, local copies, waits for them, and re-layouts, body(): centroids[jnp.clip(got_slot, 0, list_count - 1)].astype(jnp.float32)  8.75 us
  transfers between devices with their start and end apart: 5, of which 3 were waited for; matrix products, arithmetic and copies ran while one was open for 52% of the time, Pallas kernels for 0%

commit v1 on v0

v1 whole, which is shorter than its diff:
```python
import functools

import jax
import jax.numpy as jnp
from jax import lax
from jax.experimental import pallas as pl
from jax.experimental.pallas import tpu as pltpu
from jax.sharding import PartitionSpec as P

prior_weight = 4.0
F32, BF16, I32 = jnp.float32, jnp.bfloat16, jnp.int32
VMEM = pl.BlockSpec(memory_space=pltpu.VMEM)
SMEM = pl.BlockSpec(memory_space=pltpu.SMEM)
NT = (((1,), (1,)), ((), ()))
extra = 16


def mask_bf16(mask):
    return jnp.where(mask, 1.0, 0.0).astype(BF16)


def dot(a, b):
    return jnp.dot(a, b, preferred_element_type=F32)


def dot_nt(a, b):
    return lax.dot_general(a, b, NT, preferred_element_type=F32)


def pack_kernel(owners, replicas, capacity, place, valid, rows, owner, slot, codes, *outs):
    pieces = outs[:owners]
    blocks = outs[owners : owners + replicas]
    requests, position_out = outs[owners + replicas :]
    row_count, width = rows.shape
    me, rep = place[0], place[1]
    lane = lax.broadcasted_iota(I32, (1, row_count), 1)
    live = lane < valid[0]
    target = jnp.where(live, owner[...], -1)
    hit = jnp.where(lax.broadcasted_iota(I32, (owners, row_count), 0) == target, 1.0, 0.0)
    earlier = mask_bf16(
        lax.broadcasted_iota(I32, (row_count, row_count), 0)
        < lax.broadcasted_iota(I32, (row_count, row_count), 1)
    )
    before = dot(hit.astype(BF16), earlier)
    rank = jnp.sum(hit * before, axis=0, keepdims=True).astype(I32)
    position = jnp.where(live, target * capacity + rank, -1)
    position_out[...] = position

    code_rows = codes[...].astype(F32)
    high = (slot[...] // 256).astype(F32)
    low = (slot[...] % 256).astype(F32)
    which = lax.broadcasted_iota(I32, (extra, row_count), 0)
    tail = jnp.where(which == 0, high, jnp.where(which == 1, low, jnp.where(which == 2, 1.0, 0.0)))
    info = jnp.concatenate([code_rows, tail], axis=0).astype(BF16)
    within = lax.broadcasted_iota(I32, (capacity, row_count), 0)
    for step in range(owners):
        dest = jnp.bitwise_xor(me, step)
        place_at = mask_bf16(within == position - dest * capacity)
        pieces[step][...] = dot(place_at, rows[...]).astype(BF16)
        asked = dot_nt(info, place_at).astype(BF16)
        for r in range(replicas):
            requests[dest * replicas + r] = asked

    share = width // replicas
    live_codes = jnp.where(live, code_rows, 256.0).astype(BF16)
    subs = codes.shape[0]
    for step in range(replicas):
        group = jnp.bitwise_xor(rep, step)
        start = pl.multiple_of(group * share, share)
        blocks[step][0:row_count, :] = rows[:, pl.ds(start, share)]
        for part in range(row_count // share):
            blocks[step][row_count + part * subs : row_count + (part + 1) * subs, :] = live_codes[
                :, part * share : (part + 1) * share
            ]


def sums_kernel(owners, replicas, chunk, subs, place, centres, requests, *refs):
    blocks = refs[:replicas]
    keep, send, total, turned = refs[replicas:]
    lists, share = centres.shape
    sources, request_rows, capacity = requests.shape
    group_subs, _, code_count = total.shape
    width_sub = share // group_subs
    rep = place[1]
    turned[...] = centres[...].T
    span = chunk * capacity

    def pick(rows_in):
        at = lax.broadcasted_iota(I32, (8, rows_in), 0)
        col = lax.broadcasted_iota(I32, (8, rows_in), 1)
        return mask_bf16((col == rep * group_subs + at) & (at < group_subs))

    pick_asked = pick(request_rows)
    pick_local = pick(subs)
    code_iota = lax.broadcasted_iota(I32, (code_count, span), 0)
    low_iota = lax.broadcasted_iota(I32, (256, span), 0)
    total[...] = jnp.zeros_like(total)

    @pl.loop(0, sources // chunk)
    def _(index):
        asked = jnp.concatenate([requests[index * chunk + j] for j in range(chunk)], axis=1)
        codes = dot(pick_asked, asked).astype(I32)
        asked32 = asked[subs : subs + extra].astype(F32)
        high = asked32[0:1].astype(I32)
        low = asked32[1:2].astype(I32)
        live = asked32[2:3] > 0.5
        low_hit = mask_bf16(low_iota == jnp.where(live, low, -1))
        slot_hit = jnp.concatenate(
            [low_hit * mask_bf16(high == h) for h in range(lists // 256)], axis=0
        )
        gathered = dot(turned[...], slot_hit).astype(BF16)
        for m in range(group_subs):
            code_hit = mask_bf16(code_iota == codes[m : m + 1])
            total[m, 0:width_sub] -= dot_nt(
                gathered[m * width_sub : (m + 1) * width_sub], code_hit
            )

    row_count = (blocks[0].shape[0] * share) // (share + subs)
    local_iota = lax.broadcasted_iota(I32, (code_count, row_count), 0)
    ones = jnp.ones((16, row_count), BF16)
    half = group_subs // 2
    mine = jnp.bitwise_and(place[0], 1)
    hits = []
    for block in blocks:
        columns = block[0:row_count, :].T
        local = jnp.concatenate(
            [
                block[row_count + p * subs : row_count + (p + 1) * subs, :]
                for p in range(row_count // share)
            ],
            axis=1,
        )
        codes = dot(pick_local, local).astype(I32)
        hits.append((columns, codes))
    for m in range(group_subs):
        sums = total[m, 0:width_sub]
        counts = jnp.zeros((16, code_count), F32)
        for columns, codes in hits:
            code_hit = mask_bf16(local_iota == codes[m : m + 1])
            sums += dot_nt(columns[m * width_sub : (m + 1) * width_sub], code_hit)
            counts += dot_nt(ones, code_hit)

        def store(out):
            out[m % half, 0:width_sub] = sums
            out[m % half, width_sub : width_sub + 8] = counts[0:8]

        pl.when(mine == m // half)(functools.partial(store, keep))
        pl.when(mine != m // half)(functools.partial(store, send))


def target_kernel(subs, place, requests, centres, book, out):
    lists = centres.shape[0]
    width_sub, code_count = book.shape[1:]
    chunk, _, capacity = requests.shape
    span = chunk * capacity
    asked = jnp.concatenate([requests[j] for j in range(chunk)], axis=1).astype(F32)
    turned = asked.T.astype(I32)
    slots = turned[:, subs : subs + 1] * 256 + turned[:, subs + 1 : subs + 2]
    slot_hit = mask_bf16(lax.broadcasted_iota(I32, (span, lists), 1) == slots)
    centre = dot(slot_hit, centres[...])
    code_iota = lax.broadcasted_iota(I32, (span, code_count), 1)
    empty = jnp.zeros((width_sub, code_count), BF16)
    for pair in range(subs // 2):
        hits, highs, lows = [], [], []
        for m in (2 * pair, 2 * pair + 1):
            hits.append(mask_bf16(code_iota == turned[:, m : m + 1]))
            high = book[m].astype(BF16)
            highs.append(high)
            lows.append((book[m] - high.astype(F32)).astype(BF16))
        table = jnp.concatenate(
            [
                jnp.concatenate([highs[0], empty], axis=1),
                jnp.concatenate([empty, highs[1]], axis=1),
                jnp.concatenate([lows[0], empty], axis=1),
                jnp.concatenate([empty, lows[1]], axis=1),
            ],
            axis=0,
        )
        recon = dot_nt(jnp.concatenate(hits, axis=1), table)
        lanes = 2 * width_sub
        out[:, pair * lanes : (pair + 1) * lanes] = (
            centre[:, pair * lanes : (pair + 1) * lanes] + recon[:, :lanes] + recon[:, lanes:]
        )


def error_kernel(owners, place, targets, *refs):
    pieces, out = refs[:owners], refs[owners]
    capacity, width = pieces[0].shape
    for step in range(owners):
        source = jnp.bitwise_xor(place[0], step)
        start = pl.multiple_of(source * capacity, capacity)
        partial = jnp.zeros((capacity, 128), F32)
        for column in range(0, width, 128):
            gap = (
                pieces[step][:, column : column + 128].astype(F32)
                - targets[pl.ds(start, capacity), column : column + 128]
            )
            partial += gap * gap
        out[source] = jnp.sum(partial.T, axis=0, keepdims=True) * (1.0 / width)


def unpack_kernel(returned, position, out):
    owners, _, capacity = returned.shape
    row_count = position.shape[1]
    table = jnp.concatenate([returned[o] for o in range(owners)], axis=0).T
    within = lax.broadcasted_iota(I32, (capacity, row_count), 0)
    found = jnp.zeros((capacity, row_count), F32)
    for o in range(owners):
        found += jnp.where(within == position[...] - o * capacity, table[:, o : o + 1], 0.0)
    out[...] = jnp.sum(found, axis=0, keepdims=True)


def refresh_kernel(place, own, other, book, out):
    half, _, code_count = own.shape
    width_sub = book.shape[1]
    mine = jnp.bitwise_and(place[0], 1)
    for index, part in ((mine, own), (1 - mine, other)):
        for i in range(half):
            m = index * half + i
            sums, counts = part[i, 0:width_sub], part[i, width_sub : width_sub + 1]
            out[m] = (sums + prior_weight * book[m]) / (counts + prior_weight)


def swap(array, axis, step):
    count = lax.axis_size(axis)
    return lax.ppermute(array, axis, [(i, i ^ step) for i in range(count)])


def struct(*shape, dtype=F32):
    return jax.ShapeDtypeStruct(shape, dtype)


def params(mib):
    return pltpu.CompilerParams(vmem_limit_bytes=mib << 20)


def cost(flops, size):
    return pl.CostEstimate(flops=int(flops), bytes_accessed=int(size), transcendentals=0)


def body(memory_rows, list_owner, list_slot, pq_codes, valid_rows, centroids, codebook):
    row_count, width = memory_rows.shape
    lists = centroids.shape[0]
    subs, code_count, width_sub = codebook.shape
    owners, replicas = lax.axis_size("list"), lax.axis_size("rep")
    capacity = max(128, 4 * row_count // owners)
    share = width // replicas
    group_subs = subs // replicas
    request_rows = subs + extra
    devices = owners * replicas
    place = jnp.stack([lax.axis_index("list"), lax.axis_index("rep")]).astype(I32)
    book = jnp.transpose(codebook, (0, 2, 1))

    packed = pl.pallas_call(
        functools.partial(pack_kernel, owners, replicas, capacity),
        in_specs=[SMEM, SMEM] + [VMEM] * 4,
        out_specs=[VMEM] * (owners + replicas + 2),
        out_shape=[struct(capacity, width, dtype=BF16)] * owners
        + [struct(row_count + subs * row_count // share, share, dtype=BF16)] * replicas
        + [
            struct(devices, request_rows, capacity, dtype=BF16),
            struct(1, row_count, dtype=I32),
        ],
        compiler_params=params(40),
        cost_estimate=cost(2 * owners * capacity * row_count * width, 4 << 20),
        name="pack",
    )(
        place,
        valid_rows,
        memory_rows,
        list_owner.reshape(1, row_count),
        list_slot.reshape(1, row_count),
        pq_codes.T,
    )
    pieces = packed[:owners]
    blocks = packed[owners : owners + replicas]
    requests, position = packed[owners + replicas :]

    requests = lax.all_to_all(requests, ("list", "rep"), 0, 0, tiled=True)
    got_blocks = [blocks[0]] + [swap(blocks[s], "rep", s) for s in range(1, replicas)]
    got_pieces = [pieces[0]] + [swap(pieces[s], "list", s) for s in range(1, owners)]

    chunk = 8
    half_shape = struct(group_subs // 2, width_sub + 8, code_count)
    keep, send = pl.pallas_call(
        functools.partial(sums_kernel, owners, replicas, chunk, subs),
        grid_spec=pltpu.PrefetchScalarGridSpec(
            num_scalar_prefetch=1,
            grid=(1,),
            in_specs=[
                pl.BlockSpec((lists, share), lambda i, at: (0, at[1])),
                pl.BlockSpec((devices, request_rows, capacity), lambda i, at: (0, 0, 0)),
            ]
            + [pl.BlockSpec(b.shape, lambda i, at: (0, 0)) for b in got_blocks],
            out_specs=[pl.BlockSpec(half_shape.shape, lambda i, at: (0, 0, 0))] * 2,
            scratch_shapes=[
                pltpu.VMEM((group_subs, width_sub, code_count), F32),
                pltpu.VMEM((share, lists), BF16),
            ],
        ),
        out_shape=[half_shape] * 2,
        compiler_params=params(48),
        cost_estimate=cost(2 * devices * capacity * lists * share, 2 << 20),
        name="sums",
    )(place, centroids, requests, *got_blocks)

    own = keep + swap(send, "list", 1)
    others = [swap(own, "list", s) for s in range(2, owners, 2)]
    own = functools.reduce(jnp.add, others, own)
    other = swap(own, "list", 1)
    new_codebook = pl.pallas_call(
        refresh_kernel,
        grid_spec=pltpu.PrefetchScalarGridSpec(
            num_scalar_prefetch=1,
            grid=(1,),
            in_specs=[
                pl.BlockSpec(half_shape.shape, lambda i, at: (0, 0, 0)),
                pl.BlockSpec(half_shape.shape, lambda i, at: (0, 0, 0)),
                pl.BlockSpec((group_subs, width_sub, code_count), lambda i, at: (at[1], 0, 0)),
            ],
            out_specs=pl.BlockSpec((group_subs, width_sub, code_count), lambda i, at: (0, 0, 0)),
        ),
        out_shape=struct(group_subs, width_sub, code_count),
        cost_estimate=cost(1 << 20, 1 << 20),
        name="refresh",
    )(place, own, other, book)

    group = 4
    targets = pl.pallas_call(
        functools.partial(target_kernel, subs),
        grid_spec=pltpu.PrefetchScalarGridSpec(
            num_scalar_prefetch=1,
            grid=(owners // group,),
            in_specs=[
                pl.BlockSpec(
                    (group, None, request_rows, capacity), lambda i, at: (i, at[1], 0, 0)
                ),
                pl.BlockSpec((lists, width), lambda i, at: (0, 0)),
                pl.BlockSpec((subs, width_sub, code_count), lambda i, at: (0, 0, 0)),
            ],
            out_specs=pl.BlockSpec((group * capacity, width), lambda i, at: (i, 0)),
        ),
        out_shape=struct(owners * capacity, width),
        compiler_params=params(48),
        cost_estimate=cost(2 * owners * capacity * lists * width, 9 << 20),
        name="targets",
    )(place, requests.reshape(owners, replicas, request_rows, capacity), centroids, book)

    errors = pl.pallas_call(
        functools.partial(error_kernel, owners),
        in_specs=[SMEM] + [VMEM] * (owners + 1),
        out_specs=VMEM,
        out_shape=struct(owners, 1, capacity),
        compiler_params=params(48),
        cost_estimate=cost(4 * owners * capacity * width, 6 << 20),
        name="errors",
    )(place, targets, *got_pieces)
    returned = lax.all_to_all(errors, "list", 0, 0, tiled=True)
    row_error = pl.pallas_call(
        unpack_kernel,
        in_specs=[VMEM] * 2,
        out_specs=VMEM,
        out_shape=struct(1, row_count),
        name="unpack",
    )(returned, position)
    return (jnp.transpose(new_codebook, (0, 2, 1)), row_error.reshape(row_count))


def solution(mesh):
    in_specs = (
        P(("list", "rep"), None),
        P(("list", "rep"), None),
        P(("list", "rep")),
        P(("list", "rep"), None),
        P(("list", "rep")),
        P("list", None),
        P(),
    )
    out_specs = (P("rep", None, None), P(("list", "rep")))
    return jax.shard_map(body, mesh=mesh, in_specs=in_specs, out_specs=out_specs, check_vma=False)
```

time: 417 us -> 102 us (0.24)
  local copies, waits for them, and re-layouts: 218 us -> 13.2 us
  waiting for transfers between devices: 81.8 us -> 28.2 us
  blocking collectives: 41.1 us -> 7.51 us
  Pallas kernels: 0 us -> 29.8 us
  other arithmetic: 25 us -> 0.79 us
  matrix products: 17.6 us -> 0 us
  between operations: 15 us -> 1.38 us
    gather x4 -> x0, local copies, waits for them, and re-layouts: 194 us -> none  [the longest x2 184 us: code_statistics(): codebook[jnp.arange(subspaces)[None, :], pq_codes]]
    psum x1 -> x0, waiting for transfers between devices: 78.8 us -> none  [body(): sums_all, counts_all = lax.psum((sums, counts), ('list', 'rep'))]
    psum x1 -> x0, blocking collectives: 41.1 us -> none  [body(): sums_all, counts_all = lax.psum((sums, counts), ('list', 'rep'))]
    pallas_call x0 -> x6, Pallas kernels: none -> 29.8 us  [the longest x1 10.3 us: body(): pl.pallas_call(functools.partial(target_kernel, subs), grid_spec=pltpu.Pr...]
    ppermute x0 -> x15, waiting for transfers between devices: none -> 28.2 us  [swap(): return lax.ppermute(array, axis, [(i, i ^ step) for i in range(count)])]
    dot_general x16 -> x0, matrix products: 17.6 us -> none  [per_subspace(): lax.dot_general(onehot, part_rows, (((0,), (0,)), ((), ())), preferred_el...]
    ppermute x0 -> x15, starting transfers between devices: none -> 13.6 us  [swap(): return lax.ppermute(array, axis, [(i, i ^ step) for i in range(count)])]
    convert_element_type x3 -> x0, local copies, waits for them, and re-layouts: 13.3 us -> none  [the longest x2 9.2 us: body(): residual = got_rows.astype(jnp.float32) - centre]
  transfers between devices with their start and end apart: 5 -> 16, of which waited for: 3 -> 7; matrix products, arithmetic and copies ran while one was open for 52% -> 1% of each run, Pallas kernels for 0% -> 15%
where the time goes in v1:
time: 102 us
  Pallas kernels  29.8 us (29%)
  waiting for transfers between devices  28.2 us (28%)
  starting transfers between devices  20.9 us (20%)
  local copies, waits for them, and re-layouts  13.2 us (13%)
  blocking collectives  7.51 us (7%)
  between operations  1.38 us (1%)
    ppermute x15, waiting for transfers between devices, swap(): return lax.ppermute(array, axis, [(i, i ^ step) for i in range(count)])  28.2 us
    ppermute x15, starting transfers between devices, swap(): return lax.ppermute(array, axis, [(i, i ^ step) for i in range(count)])  13.6 us
    unnamed x32, local copies, waits for them, and re-layouts  13.2 us
    pallas_call x1, Pallas kernels, body(): pl.pallas_call(functools.partial(target_kernel, subs), grid_spec=pltpu.Pr...  10.3 us
    pallas_call x1, Pallas kernels, body(): pl.pallas_call(functools.partial(sums_kernel, owners, replicas, chunk, su...  10.2 us
    all_to_all x1, blocking collectives, body(): returned = lax.all_to_all(errors, 'list', 0, 0, tiled=True)  7.51 us
    all_to_all x1, starting transfers between devices, body(): requests = lax.all_to_all(requests, ('list', 'rep'), 0, 0, tiled=True)  7.3 us
    pallas_call x1, Pallas kernels, body(): pl.pallas_call(functools.partial(error_kernel, owners), in_specs=[SMEM] +...  2.85 us
  transfers between devices with their start and end apart: 16, of which 7 were waited for; matrix products, arithmetic and copies ran while one was open for 1% of the time, Pallas kernels for 15%

profile of v1, /device:TPU:0, one launch (start us, length us, event | category | flops | bytes accessed | tf_op | source)
XLA Modules:
  0.0 101.8 jit_solution(4765856844306845556)
XLA Ops:
  4.5 2.3 %pack.1 = (bf16[128,1024]{1,0:T(8,128)(2,1)S(1)}, bf16[128,1024]{1,0:T(8,128)(2,1)S(1)}, bf16[128,1024]{1,0:T(8,128)(2,1)S(1)}, bf16[128,1024]{1,0:T(8,128)(2,1)...) custom-call(s32[2]{0:T(128)S(1)} %pad_add_fusion.place, ...), custom_call_target="tpu_custom_call" | custom-call | flops 536870912 | bytes 4194304 | tf_op jit(solution)/shard_map/pack/pallas_call | solution.py:254
  8.0 7.3 %all-to-all-start = ((bf16[32,32,128]{2,1,0:T(8,128)(2,1)}), bf16[32,32,128]{2,1,0:T(8,128)(2,1)S(1)}, u32[]{:S(2)}, u32[]{:S(2)}) async-start(bf16[32,32,128]{2,1,0:T(8,128)(2,1)} %get-tuple-element.18), calls=%async_computation | async-start | bytes 524288 | tf_op jit(solution)/shard_map/all_to_all | solution.py:279
  15.3 1.8 %collective-permute-start = (bf16[272,256]{1,0:T(8,128)(2,1)S(1)}, bf16[272,256]{1,0:T(8,128)(2,1)S(1)}, u32[]{:S(2)}, u32[]{:S(2)}) collective-permute-start(bf16[272,256]{1,0:T(8,128)(2,1)S(1)} %get-tuple-element.20), channel_id=1, source_target_pairs={{0,1},{1,0},{2,3},{3,2},{4,5},{5,4},{6,7},{7,6},{8,9},{9,8},{10,11... | collective-permute-start | bytes 417800 | tf_op jit(solution)/shard_map/ppermute | solution.py:226
  17.1 2.4 %collective-permute-start.1 = (bf16[272,256]{1,0:T(8,128)(2,1)S(1)}, bf16[272,256]{1,0:T(8,128)(2,1)S(1)}, u32[]{:S(2)}, u32[]{:S(2)}) collective-permute-start(bf16[272,256]{1,0:T(8,128)(2,1)S(1)} %get-tuple-element.21), channel_id=1, source_target_pairs={{0,2},{1,3},{2,0},{3,1},{4,6},{5,7},{6,4},{7,5},{8,10},{9,11},{10,... | collective-permute-start | bytes 417800 | tf_op jit(solution)/shard_map/ppermute | solution.py:226
  19.7 8.2 %collective-permute-done.refs_1_ = bf16[272,256]{1,0:T(8,128)(2,1)S(1)} collective-permute-done((bf16[272,256]{1,0:T(8,128)(2,1)S(1)}, bf16[272,256]{1,0:T(8,128)(2,1)S(1)}, u32[]{:S(2)}, u32[]{:S(2)}) %collective-permute-start) | collective-permute-done | bytes 139296 | tf_op jit(solution)/shard_map/ppermute | solution.py:226
  27.9 6.2 %collective-permute-done.1.refs_2_ = bf16[272,256]{1,0:T(8,128)(2,1)S(1)} collective-permute-done((bf16[272,256]{1,0:T(8,128)(2,1)S(1)}, bf16[272,256]{1,0:T(8,128)(2,1)S(1)}, u32[]{:S(2)}, u32[]{:S(2)}) %collective-permute-start.1) | collective-permute-done | bytes 139296 | tf_op jit(solution)/shard_map/ppermute | solution.py:226
  35.4 2.2 %copy-done.4 = bf16[2048,1024]{1,0:T(8,128)(2,1)S(1)} copy-done((bf16[2048,1024]{1,0:T(8,128)(2,1)S(1)}, bf16[2048,1024]{1,0:T(8,128)(2,1)}, u32[]{:S(2)}) %copy-start.4) | copy-done | bytes 4194328
  40.3 10.2 %sums.1 = (f32[2,72,256]{2,1,0:T(8,128)S(1)}, f32[2,72,256]{2,1,0:T(8,128)S(1)}) custom-call(s32[2]{0:T(128)S(1)} %pad_add_fusion.place, bf16[2048,1024]{1,0:T(8,128)(2,1)S(1)} %copy-done.4, bf16[32,32,128]{2,1,0:T(8,128)(2,1)S(1)} %all-to-all-done.requests, bf16[272,256]{1,0:T(8,128)(2,1)S(1)} %copy-done.14, ...), custom_call_target="tpu_custom_call" | custom-call | flops 4294967296 | bytes 2097152 | tf_op jit(solution)/shard_map/sums/pallas_call | solution.py:285
  50.6 1.4 %collective-permute-done.3 = f32[2,72,256]{2,1,0:T(8,128)S(1)} collective-permute-done((f32[2,72,256]{2,1,0:T(8,128)S(1)}, f32[2,72,256]{2,1,0:T(8,128)S(1)}, u32[]{:S(2)}, u32[]{:S(2)}) %collective-permute-start.3) | collective-permute-done | bytes 147488 | tf_op jit(solution)/shard_map/ppermute | solution.py:226
  52.0 2.5 %collective-permute-start.6 = (f32[2,72,256]{2,1,0:T(8,128)S(1)}, f32[2,72,256]{2,1,0:T(8,128)S(1)}, u32[]{:S(2)}, u32[]{:S(2)}) collective-permute-start(f32[2,72,256]{2,1,0:T(8,128)S(1)} %add.12), channel_id=1, source_target_pairs={{0,24},{4,28},{8,16},{12,20},{16,8},{20,12},{24,0},{28,4},{1,25},{... | collective-permute-start | bytes 442376 | tf_op jit(solution)/shard_map/ppermute | solution.py:226
  55.6 1.5 %collective-permute-start.9 = (bf16[128,1024]{1,0:T(8,128)(2,1)S(1)}, bf16[128,1024]{1,0:T(8,128)(2,1)S(1)}, u32[]{:S(2)}, u32[]{:S(2)}) collective-permute-start(bf16[128,1024]{1,0:T(8,128)(2,1)S(1)} %get-tuple-element.27), channel_id=1, source_target_pairs={{0,8},{4,12},{8,0},{12,4},{16,24},{20,28},{24,16},{28,20},{1,9},{5... | collective-permute-start | bytes 786440 | tf_op jit(solution)/shard_map/ppermute | solution.py:226
  57.0 2.5 %collective-permute-done.6 = f32[2,72,256]{2,1,0:T(8,128)S(1)} collective-permute-done((f32[2,72,256]{2,1,0:T(8,128)S(1)}, f32[2,72,256]{2,1,0:T(8,128)S(1)}, u32[]{:S(2)}, u32[]{:S(2)}) %collective-permute-start.6) | collective-permute-done | bytes 147488 | tf_op jit(solution)/shard_map/ppermute | solution.py:226
  59.6 2.5 %collective-permute-done.5 = f32[2,72,256]{2,1,0:T(8,128)S(1)} collective-permute-done((f32[2,72,256]{2,1,0:T(8,128)S(1)}, f32[2,72,256]{2,1,0:T(8,128)S(1)}, u32[]{:S(2)}, u32[]{:S(2)}) %collective-permute-start.5) | collective-permute-done | bytes 147488 | tf_op jit(solution)/shard_map/ppermute | solution.py:226
  62.0 1.5 %collective-permute-start.11 = (bf16[128,1024]{1,0:T(8,128)(2,1)S(1)}, bf16[128,1024]{1,0:T(8,128)(2,1)S(1)}, u32[]{:S(2)}, u32[]{:S(2)}) collective-permute-start(bf16[128,1024]{1,0:T(8,128)(2,1)S(1)} %get-tuple-element.29), channel_id=1, source_target_pairs={{0,16},{4,20},{8,24},{12,28},{16,0},{20,4},{24,8},{28,12},{1,17},{... | collective-permute-start | bytes 786440 | tf_op jit(solution)/shard_map/ppermute | solution.py:226
  64.2 1.4 %collective-permute-start.13 = (bf16[128,1024]{1,0:T(8,128)(2,1)S(1)}, bf16[128,1024]{1,0:T(8,128)(2,1)S(1)}, u32[]{:S(2)}, u32[]{:S(2)}) collective-permute-start(bf16[128,1024]{1,0:T(8,128)(2,1)S(1)} %get-tuple-element.31), channel_id=1, source_target_pairs={{0,24},{4,28},{8,16},{12,20},{16,8},{20,12},{24,0},{28,4},{1,25},{... | collective-permute-start | bytes 786440 | tf_op jit(solution)/shard_map/ppermute | solution.py:226
  65.7 2.8 %collective-permute-done.9.refs_2_ = bf16[128,1024]{1,0:T(8,128)(2,1)S(1)} collective-permute-done((bf16[128,1024]{1,0:T(8,128)(2,1)S(1)}, bf16[128,1024]{1,0:T(8,128)(2,1)S(1)}, u32[]{:S(2)}, u32[]{:S(2)}) %collective-permute-start.9) | collective-permute-done | bytes 262176 | tf_op jit(solution)/shard_map/ppermute | solution.py:226
  68.5 4.6 %collective-permute-done.10.refs_3_ = bf16[128,1024]{1,0:T(8,128)(2,1)S(1)} collective-permute-done((bf16[128,1024]{1,0:T(8,128)(2,1)S(1)}, bf16[128,1024]{1,0:T(8,128)(2,1)S(1)}, u32[]{:S(2)}, u32[]{:S(2)}) %collective-permute-start.10) | collective-permute-done | bytes 262176 | tf_op jit(solution)/shard_map/ppermute | solution.py:226
  73.1 1.1 %collective-permute-start.7 = (f32[2,72,256]{2,1,0:T(8,128)}, f32[2,72,256]{2,1,0:T(8,128)S(1)}, u32[]{:S(2)}, u32[]{:S(2)}) collective-permute-start(f32[2,72,256]{2,1,0:T(8,128)} %add_add_fusion.own), channel_id=1, source_target_pairs={{0,4},{4,0},{8,12},{12,8},{16,20},{20,16},{24,28},{28,24},{1,5},{5... | collective-permute-start | bytes 442376 | tf_op jit(solution)/shard_map/ppermute | solution.py:226
  74.3 10.3 %targets.1 = f32[1024,1024]{1,0:T(8,128)S(1)} custom-call(s32[2]{0:T(128)S(1)} %pad_add_fusion.place, bf16[8,4,32,128]{3,2,1,0:T(8,128)(2,1)S(1)} %bitcast.11, bf16[2048,1024]{1,0:T(8,128)(2,1)} %centres.3, f32[16,64,256]{2,1,0:T(8,128)S(1)} %bitcast.10), custom_call_target="tpu_custom_call" | custom-call | flops 4294967296 | bytes 9437184 | tf_op jit(solution)/shard_map/targets/pallas_call | solution.py:329
  84.6 1.9 %copy-done = f32[1024,1024]{1,0:T(8,128)} copy-done((f32[1024,1024]{1,0:T(8,128)}, f32[1024,1024]{1,0:T(8,128)S(1)}, u32[]{:S(2)}) %copy-start) | copy-done | bytes 4194328
  86.6 2.9 %errors.1 = f32[8,1,128]{2,1,0:T(1,128)S(1)} custom-call(s32[2]{0:T(128)S(1)} %pad_add_fusion.place, f32[1024,1024]{1,0:T(8,128)} %copy-done, bf16[128,1024]{1,0:T(8,128)(2,1)S(1)} %get-tuple-element.25.refs_0_, bf16[128,1024]{1,0:T(8,128)(2,1)S(1)} %collective-permute-done.8.refs_1_, bf16[128,1024]{1,0:T(8,128)(2,1)S(1)} %collective-permute-done.9.refs_2_, ...), custom_call_target="tpu_custom_call" | custom-call | flops 4194304 | bytes 6291456 | tf_op jit(solution)/shard_map/errors/pallas_call | solution.py:349
  89.5 7.5 %all_to_all.10.returned = f32[8,1,128]{2,1,0:T(1,128)} all-to-all(f32[8,1,128]{2,1,0:T(1,128)S(1)} %errors.1), channel_id=1, replica_groups=mesh['list'=8,'rep'=4] {'list'}, dimensions={0} | all-to-all | bytes 8192 | tf_op jit(solution)/shard_map/all_to_all | solution.py:358
  97.0 1.6 %unpack.1 = f32[1,256]{1,0:T(1,128)} custom-call(f32[8,1,128]{2,1,0:T(1,128)} %all_to_all.10.returned, s32[1,256]{1,0:T(1,128)} %copy-done.3), custom_call_target="tpu_custom_call" | custom-call | tf_op jit(solution)/shard_map/unpack/pallas_call | solution.py:359
  99.3 2.5 %refresh.1 = f32[4,64,256]{2,1,0:T(8,128)} custom-call(s32[2]{0:T(128)} %copy-done.2, f32[2,72,256]{2,1,0:T(8,128)} %add_add_fusion.own, f32[2,72,256]{2,1,0:T(8,128)} %copy-done.15, f32[16,64,256]{2,1,0:T(8,128)} %bitcast.9), custom_call_target="tpu_custom_call" | custom-call | flops 1048576 | bytes 1048576 | tf_op jit(solution)/shard_map/refresh/pallas_call | solution.py:311
  (50 shorter events, 11.2 us)
Async XLA Ops:
  1.4 85.2 %copy-start.2 = (s32[2]{0:T(128)}, s32[2]{0:T(128)S(1)}, u32[]{:S(2)}) copy-start(s32[2]{0:T(128)S(1)} %pad_add_fusion.place) | copy-start | bytes 28
  1.4 1.0 %copy-start.5 = (bf16[256,1024]{1,0:T(8,128)(2,1)S(1)}, bf16[256,1024]{1,0:T(8,128)(2,1)}, u32[]{:S(2)}) copy-start(bf16[256,1024]{1,0:T(8,128)(2,1)} %rows.1) | copy-start | bytes 1572868
  8.0 27.4 %all-to-all-start = ((bf16[32,32,128]{2,1,0:T(8,128)(2,1)}), bf16[32,32,128]{2,1,0:T(8,128)(2,1)S(1)}, u32[]{:S(2)}, u32[]{:S(2)}) async-start(bf16[32,32,128]{2,1,0:T(8,128)(2,1)} %get-tuple-element.18), calls=%async_computation | async-start | bytes 524288 | tf_op jit(solution)/shard_map/all_to_all | solution.py:279
  15.3 12.6 %collective-permute-start = (bf16[272,256]{1,0:T(8,128)(2,1)S(1)}, bf16[272,256]{1,0:T(8,128)(2,1)S(1)}, u32[]{:S(2)}, u32[]{:S(2)}) collective-permute-start(bf16[272,256]{1,0:T(8,128)(2,1)S(1)} %get-tuple-element.20), channel_id=1, source_target_pairs={{0,1},{1,0},{2,3},{3,2},{4,5},{5,4},{6,7},{7,6},{8,9},{9,8},{10,11... | collective-permute-start | bytes 417800 | tf_op jit(solution)/shard_map/ppermute | solution.py:226
  17.1 17.0 %collective-permute-start.1 = (bf16[272,256]{1,0:T(8,128)(2,1)S(1)}, bf16[272,256]{1,0:T(8,128)(2,1)S(1)}, u32[]{:S(2)}, u32[]{:S(2)}) collective-permute-start(bf16[272,256]{1,0:T(8,128)(2,1)S(1)} %get-tuple-element.21), channel_id=1, source_target_pairs={{0,2},{1,3},{2,0},{3,1},{4,6},{5,7},{6,4},{7,5},{8,10},{9,11},{10,... | collective-permute-start | bytes 417800 | tf_op jit(solution)/shard_map/ppermute | solution.py:226
  19.5 15.2 %collective-permute-start.2 = (bf16[272,256]{1,0:T(8,128)(2,1)S(1)}, bf16[272,256]{1,0:T(8,128)(2,1)S(1)}, u32[]{:S(2)}, u32[]{:S(2)}) collective-permute-start(bf16[272,256]{1,0:T(8,128)(2,1)S(1)} %get-tuple-element.22), channel_id=1, source_target_pairs={{0,3},{1,2},{2,1},{3,0},{4,7},{5,6},{6,5},{7,4},{8,11},{9,10},{10,... | collective-permute-start | bytes 417800 | tf_op jit(solution)/shard_map/ppermute | solution.py:226
  35.4 2.2 %copy-start.4 = (bf16[2048,1024]{1,0:T(8,128)(2,1)S(1)}, bf16[2048,1024]{1,0:T(8,128)(2,1)}, u32[]{:S(2)}) copy-start(bf16[2048,1024]{1,0:T(8,128)(2,1)} %centres.3) | copy-start | bytes 12582916
  37.6 0.9 copy-start.7
  38.5 0.9 copy-start.9
  39.4 0.9 copy-start.14
  40.3 33.9 %copy-start.1 = (f32[16,256,64]{1,2,0:T(8,128)S(1)}, f32[16,256,64]{1,2,0:T(8,128)}, u32[]{:S(2)}) copy-start(f32[16,256,64]{1,2,0:T(8,128)} %param.13) | copy-start | bytes 3145732
  50.6 1.4 %collective-permute-start.3 = (f32[2,72,256]{2,1,0:T(8,128)S(1)}, f32[2,72,256]{2,1,0:T(8,128)S(1)}, u32[]{:S(2)}, u32[]{:S(2)}) collective-permute-start(f32[2,72,256]{2,1,0:T(8,128)S(1)} %get-tuple-element.24), channel_id=1, source_target_pairs={{0,4},{4,0},{8,12},{12,8},{16,20},{20,16},{24,28},{28,24},{1,5},{5... | collective-permute-start | bytes 442376 | tf_op jit(solution)/shard_map/ppermute | solution.py:226
  52.0 7.6 %collective-permute-start.6 = (f32[2,72,256]{2,1,0:T(8,128)S(1)}, f32[2,72,256]{2,1,0:T(8,128)S(1)}, u32[]{:S(2)}, u32[]{:S(2)}) collective-permute-start(f32[2,72,256]{2,1,0:T(8,128)S(1)} %add.12), channel_id=1, source_target_pairs={{0,24},{4,28},{8,16},{12,20},{16,8},{20,12},{24,0},{28,4},{1,25},{... | collective-permute-start | bytes 442376 | tf_op jit(solution)/shard_map/ppermute | solution.py:226
  54.5 7.6 %collective-permute-start.5 = (f32[2,72,256]{2,1,0:T(8,128)S(1)}, f32[2,72,256]{2,1,0:T(8,128)S(1)}, u32[]{:S(2)}, u32[]{:S(2)}) collective-permute-start(f32[2,72,256]{2,1,0:T(8,128)S(1)} %add.12), channel_id=1, source_target_pairs={{0,16},{4,20},{8,24},{12,28},{16,0},{20,4},{24,8},{28,12},{1,17},{... | collective-permute-start | bytes 442376 | tf_op jit(solution)/shard_map/ppermute | solution.py:226
  55.0 8.5 %collective-permute-start.4 = (f32[2,72,256]{2,1,0:T(8,128)S(1)}, f32[2,72,256]{2,1,0:T(8,128)S(1)}, u32[]{:S(2)}, u32[]{:S(2)}) collective-permute-start(f32[2,72,256]{2,1,0:T(8,128)S(1)} %add.12), channel_id=1, source_target_pairs={{0,8},{4,12},{8,0},{12,4},{16,24},{20,28},{24,16},{28,20},{1,9},{5... | collective-permute-start | bytes 442376 | tf_op jit(solution)/shard_map/ppermute | solution.py:226
  55.6 8.6 %collective-permute-start.8 = (bf16[128,1024]{1,0:T(8,128)(2,1)S(1)}, bf16[128,1024]{1,0:T(8,128)(2,1)S(1)}, u32[]{:S(2)}, u32[]{:S(2)}) collective-permute-start(bf16[128,1024]{1,0:T(8,128)(2,1)S(1)} %get-tuple-element.26), channel_id=1, source_target_pairs={{0,4},{4,0},{8,12},{12,8},{16,20},{20,16},{24,28},{28,24},{1,5},{5... | collective-permute-start | bytes 786440 | tf_op jit(solution)/shard_map/ppermute | solution.py:226
  55.6 12.9 %collective-permute-start.9 = (bf16[128,1024]{1,0:T(8,128)(2,1)S(1)}, bf16[128,1024]{1,0:T(8,128)(2,1)S(1)}, u32[]{:S(2)}, u32[]{:S(2)}) collective-permute-start(bf16[128,1024]{1,0:T(8,128)(2,1)S(1)} %get-tuple-element.27), channel_id=1, source_target_pairs={{0,8},{4,12},{8,0},{12,4},{16,24},{20,28},{24,16},{28,20},{1,9},{5... | collective-permute-start | bytes 786440 | tf_op jit(solution)/shard_map/ppermute | solution.py:226
  59.6 13.6 %collective-permute-start.10 = (bf16[128,1024]{1,0:T(8,128)(2,1)S(1)}, bf16[128,1024]{1,0:T(8,128)(2,1)S(1)}, u32[]{:S(2)}, u32[]{:S(2)}) collective-permute-start(bf16[128,1024]{1,0:T(8,128)(2,1)S(1)} %get-tuple-element.28), channel_id=1, source_target_pairs={{0,12},{4,8},{8,4},{12,0},{16,28},{20,24},{24,20},{28,16},{1,13},{... | collective-permute-start | bytes 786440 | tf_op jit(solution)/shard_map/ppermute | solution.py:226
  62.0 24.5 %collective-permute-start.11 = (bf16[128,1024]{1,0:T(8,128)(2,1)S(1)}, bf16[128,1024]{1,0:T(8,128)(2,1)S(1)}, u32[]{:S(2)}, u32[]{:S(2)}) collective-permute-start(bf16[128,1024]{1,0:T(8,128)(2,1)S(1)} %get-tuple-element.29), channel_id=1, source_target_pairs={{0,16},{4,20},{8,24},{12,28},{16,0},{20,4},{24,8},{28,12},{1,17},{... | collective-permute-start | bytes 786440 | tf_op jit(solution)/shard_map/ppermute | solution.py:226
  63.5 23.0 %collective-permute-start.12 = (bf16[128,1024]{1,0:T(8,128)(2,1)S(1)}, bf16[128,1024]{1,0:T(8,128)(2,1)S(1)}, u32[]{:S(2)}, u32[]{:S(2)}) collective-permute-start(bf16[128,1024]{1,0:T(8,128)(2,1)S(1)} %get-tuple-element.30), channel_id=1, source_target_pairs={{0,20},{4,16},{8,28},{12,24},{16,4},{20,0},{24,12},{28,8},{1,21},{... | collective-permute-start | bytes 786440 | tf_op jit(solution)/shard_map/ppermute | solution.py:226
  64.2 22.3 %collective-permute-start.13 = (bf16[128,1024]{1,0:T(8,128)(2,1)S(1)}, bf16[128,1024]{1,0:T(8,128)(2,1)S(1)}, u32[]{:S(2)}, u32[]{:S(2)}) collective-permute-start(bf16[128,1024]{1,0:T(8,128)(2,1)S(1)} %get-tuple-element.31), channel_id=1, source_target_pairs={{0,24},{4,28},{8,16},{12,20},{16,8},{20,12},{24,0},{28,4},{1,25},{... | collective-permute-start | bytes 786440 | tf_op jit(solution)/shard_map/ppermute | solution.py:226
  68.5 18.1 %collective-permute-start.14 = (bf16[128,1024]{1,0:T(8,128)(2,1)S(1)}, bf16[128,1024]{1,0:T(8,128)(2,1)S(1)}, u32[]{:S(2)}, u32[]{:S(2)}) collective-permute-start(bf16[128,1024]{1,0:T(8,128)(2,1)S(1)} %get-tuple-element.32), channel_id=1, source_target_pairs={{0,28},{4,24},{8,20},{12,16},{16,12},{20,8},{24,4},{28,0},{1,29},{... | collective-permute-start | bytes 786440 | tf_op jit(solution)/shard_map/ppermute | solution.py:226
  73.1 25.5 %collective-permute-start.7 = (f32[2,72,256]{2,1,0:T(8,128)}, f32[2,72,256]{2,1,0:T(8,128)S(1)}, u32[]{:S(2)}, u32[]{:S(2)}) collective-permute-start(f32[2,72,256]{2,1,0:T(8,128)} %add_add_fusion.own), channel_id=1, source_target_pairs={{0,4},{4,0},{8,12},{12,8},{16,20},{20,16},{24,28},{28,24},{1,5},{5... | collective-permute-start | bytes 442376 | tf_op jit(solution)/shard_map/ppermute | solution.py:226
  84.6 2.0 %copy-start = (f32[1024,1024]{1,0:T(8,128)}, f32[1024,1024]{1,0:T(8,128)S(1)}, u32[]{:S(2)}) copy-start(f32[1024,1024]{1,0:T(8,128)S(1)} %targets.1) | copy-start | bytes 12582916
  (8 other events, 5.3 us)

commit v2 on v1

v2 whole, which is shorter than its diff:
```python
import functools

import jax
import jax.numpy as jnp
from jax import lax
from jax.experimental import pallas as pl
from jax.experimental.pallas import tpu as pltpu
from jax.sharding import PartitionSpec as P

prior_weight = 4.0
F32, BF16, I32 = jnp.float32, jnp.bfloat16, jnp.int32
VMEM = pl.BlockSpec(memory_space=pltpu.VMEM)
SMEM = pl.BlockSpec(memory_space=pltpu.SMEM)
NT = (((1,), (1,)), ((), ()))
request_rows = 16


def mask_bf16(mask):
    return jnp.where(mask, 1.0, 0.0).astype(BF16)


def dot(a, b):
    return jnp.dot(a, b, preferred_element_type=F32)


def dot_nt(a, b):
    return lax.dot_general(a, b, NT, preferred_element_type=F32)


def pack_kernel(owners, replicas, capacity, place, valid, rows, owner, slot, codes, *outs):
    blocks = outs[:replicas]
    requests, position_out = outs[replicas:]
    row_count, width = rows.shape
    rep = place[1]
    lane = lax.broadcasted_iota(I32, (1, row_count), 1)
    live = lane < valid[0]
    target = jnp.where(live, owner[...], -1)
    hit = jnp.where(lax.broadcasted_iota(I32, (owners, row_count), 0) == target, 1.0, 0.0)
    earlier = mask_bf16(
        lax.broadcasted_iota(I32, (row_count, row_count), 0)
        < lax.broadcasted_iota(I32, (row_count, row_count), 1)
    )
    before = dot(hit.astype(BF16), earlier)
    rank = jnp.sum(hit * before, axis=0, keepdims=True).astype(I32)
    position = jnp.where(live, target * capacity + rank, -1)
    position_out[...] = position

    code_rows = codes[...].astype(F32)
    subs = code_rows.shape[0]
    group_subs = subs // replicas
    high = (slot[...] // 256).astype(F32)
    low = (slot[...] % 256).astype(F32)
    which = lax.broadcasted_iota(I32, (request_rows - group_subs, row_count), 0)
    tail = jnp.where(which == 0, high, jnp.where(which == 1, low, jnp.where(which == 2, 1.0, 0.0)))
    info = jnp.concatenate(
        [
            part
            for g in range(replicas)
            for part in (code_rows[g * group_subs : (g + 1) * group_subs], tail)
        ],
        axis=0,
    ).astype(BF16)
    within = lax.broadcasted_iota(I32, (capacity, row_count), 0)
    for dest in range(owners):
        place_at = mask_bf16(within == position - dest * capacity)
        asked = dot_nt(info, place_at).astype(BF16)
        for g in range(replicas):
            requests[dest * replicas + g] = asked[g * request_rows : (g + 1) * request_rows]

    share = width // replicas
    live_codes = jnp.where(live, code_rows, 256.0).astype(BF16)
    for step in range(replicas):
        group = jnp.bitwise_xor(rep, step)
        start = pl.multiple_of(group * share, share)
        blocks[step][0:row_count, :] = rows[:, pl.ds(start, share)]
        for part in range(row_count // share):
            blocks[step][row_count + part * subs : row_count + (part + 1) * subs, :] = live_codes[
                :, part * share : (part + 1) * share
            ]


def pick(group, group_subs, rows_in):
    at = lax.broadcasted_iota(I32, (8, rows_in), 0)
    col = lax.broadcasted_iota(I32, (8, rows_in), 1)
    return mask_bf16((col == group * group_subs + at) & (at < group_subs))


def centre_sums_kernel(chunk, place, centres, requests, total, turned):
    lists, share = centres.shape
    sources, _, capacity = requests.shape
    group_subs, width_sub, code_count = total.shape
    turned[...] = centres[...].T
    span = chunk * capacity
    code_iota = lax.broadcasted_iota(I32, (code_count, span), 0)
    low_iota = lax.broadcasted_iota(I32, (256, span), 0)
    total[...] = jnp.zeros_like(total)

    @pl.loop(0, sources // chunk)
    def _(index):
        asked = jnp.concatenate([requests[index * chunk + j] for j in range(chunk)], axis=1)
        asked = asked.astype(F32).astype(I32)
        codes = asked[0:group_subs]
        high, low, live = (asked[group_subs + i : group_subs + i + 1] for i in range(3))
        low_hit = mask_bf16(low_iota == jnp.where(live > 0, low, -1))
        slot_hit = jnp.concatenate(
            [low_hit * mask_bf16(high == h) for h in range(lists // 256)], axis=0
        )
        gathered = dot(turned[...], slot_hit).astype(BF16)
        for m in range(group_subs):
            code_hit = mask_bf16(code_iota == codes[m : m + 1])
            total[m] += dot_nt(gathered[m * width_sub : (m + 1) * width_sub], code_hit)


def row_sums_kernel(replicas, subs, place, centre_sums, book, *refs):
    blocks = refs[:replicas]
    keep, send = refs[replicas:]
    group_subs, width_sub, code_count = centre_sums.shape
    share = width_sub * group_subs
    pick_local = pick(place[1], group_subs, subs)
    row_count = (blocks[0].shape[0] * share) // (share + subs)
    local_iota = lax.broadcasted_iota(I32, (code_count, row_count), 0)
    ones = jnp.ones((16, row_count), BF16)
    prior = jnp.where(place[0] == 0, prior_weight, 0.0)
    half = group_subs // 2
    mine = jnp.bitwise_and(place[0], 1)
    hits = []
    for block in blocks:
        columns = block[0:row_count, :].T
        local = jnp.concatenate(
            [
                block[row_count + p * subs : row_count + (p + 1) * subs, :]
                for p in range(row_count // share)
            ],
            axis=1,
        )
        codes = dot(pick_local, local).astype(I32)
        hits.append((columns, codes))
    for m in range(group_subs):
        sums = prior * book[m] - centre_sums[m]
        counts = jnp.full((16, code_count), prior, F32)
        for columns, codes in hits:
            code_hit = mask_bf16(local_iota == codes[m : m + 1])
            sums += dot_nt(columns[m * width_sub : (m + 1) * width_sub], code_hit)
            counts += dot_nt(ones, code_hit)

        def store(out):
            out[m % half, 0:width_sub] = sums
            out[m % half, width_sub : width_sub + 8] = counts[0:8]

        pl.when(mine == m // half)(functools.partial(store, keep))
        pl.when(mine != m // half)(functools.partial(store, send))


def gather_kernel(group_subs, place, requests, centres, out):
    lists = centres.shape[0]
    chunk, _, capacity = requests.shape
    span = chunk * capacity
    asked = jnp.concatenate([requests[j] for j in range(chunk)], axis=1).astype(F32)
    turned = asked.T.astype(I32)
    slots = turned[:, group_subs : group_subs + 1] * 256 + turned[:, group_subs + 1 : group_subs + 2]
    slot_hit = mask_bf16(lax.broadcasted_iota(I32, (span, lists), 1) == slots)
    out[...] = dot(slot_hit, centres[...]).astype(BF16)


def offset_kernel(rows, codes, book, out):
    subs, width_sub, code_count = book.shape
    row_count = rows.shape[0]
    turned = codes[...].astype(F32).T.astype(I32)
    code_iota = lax.broadcasted_iota(I32, (row_count, code_count), 1)
    empty = jnp.zeros((width_sub, code_count), BF16)
    for pair in range(subs // 2):
        hits, highs, lows = [], [], []
        for m in (2 * pair, 2 * pair + 1):
            hits.append(mask_bf16(code_iota == turned[:, m : m + 1]))
            high = book[m].astype(BF16)
            highs.append(high)
            lows.append((book[m] - high.astype(F32)).astype(BF16))
        table = jnp.concatenate(
            [
                jnp.concatenate([highs[0], empty], axis=1),
                jnp.concatenate([empty, highs[1]], axis=1),
                jnp.concatenate([lows[0], empty], axis=1),
                jnp.concatenate([empty, lows[1]], axis=1),
            ],
            axis=0,
        )
        recon = dot_nt(jnp.concatenate(hits, axis=1), table)
        lanes = 2 * width_sub
        span = slice(pair * lanes, (pair + 1) * lanes)
        out[:, span] = rows[:, span].astype(F32) - (recon[:, :lanes] + recon[:, lanes:])


def error_kernel(valid, position, offsets, centres, out):
    slots, width = centres.shape
    row_count = offsets.shape[0]
    column_at = jnp.broadcast_to(position[...].astype(F32), (8, row_count)).T.astype(I32)[:, 0:1]
    hit = mask_bf16(lax.broadcasted_iota(I32, (row_count, slots), 1) == column_at)
    partial = jnp.zeros((row_count, 128), F32)
    for start in range(0, width, 256):
        gap = offsets[:, start : start + 256] - dot(hit, centres[:, start : start + 256])
        square = gap * gap
        partial += square[:, :128] + square[:, 128:]
    error = jnp.sum(partial.T, axis=0, keepdims=True) * (1.0 / width)
    lane = lax.broadcasted_iota(I32, (1, row_count), 1)
    out[...] = jnp.where(lane < valid[0], error, 0.0)


def swap(array, axis, step):
    count = lax.axis_size(axis)
    return lax.ppermute(array, axis, [(i, i ^ step) for i in range(count)])


def struct(*shape, dtype=F32):
    return jax.ShapeDtypeStruct(shape, dtype)


def params(mib):
    return pltpu.CompilerParams(vmem_limit_bytes=mib << 20)


def cost(flops, size):
    return pl.CostEstimate(flops=int(flops), bytes_accessed=int(size), transcendentals=0)


def body(memory_rows, list_owner, list_slot, pq_codes, valid_rows, centroids, codebook):
    row_count, width = memory_rows.shape
    lists = centroids.shape[0]
    subs, code_count, width_sub = codebook.shape
    owners, replicas = lax.axis_size("list"), lax.axis_size("rep")
    capacity = max(128, 4 * row_count // owners)
    share = width // replicas
    group_subs = subs // replicas
    devices = owners * replicas
    place = jnp.stack([lax.axis_index("list"), lax.axis_index("rep")]).astype(I32)
    book = jnp.transpose(codebook, (0, 2, 1))

    codes = pq_codes.T

    packed = pl.pallas_call(
        functools.partial(pack_kernel, owners, replicas, capacity),
        in_specs=[SMEM, SMEM] + [VMEM] * 4,
        out_specs=[VMEM] * (replicas + 2),
        out_shape=[struct(row_count + subs * row_count // share, share, dtype=BF16)] * replicas
        + [
            struct(devices, request_rows, capacity, dtype=BF16),
            struct(1, row_count, dtype=I32),
        ],
        compiler_params=params(60),
        cost_estimate=cost(1 << 20, 1 << 20),
        name="pack",
    )(
        place,
        valid_rows,
        memory_rows,
        list_owner.reshape(1, row_count),
        list_slot.reshape(1, row_count),
        codes,
    )
    blocks = packed[:replicas]
    requests, position = packed[replicas:]

    requests = lax.all_to_all(requests, ("list", "rep"), 0, 0, tiled=True)
    got_blocks = [blocks[0]] + [swap(blocks[s], "rep", s) for s in range(1, replicas)]

    group = 4
    gathered = pl.pallas_call(
        functools.partial(gather_kernel, group_subs),
        grid_spec=pltpu.PrefetchScalarGridSpec(
            num_scalar_prefetch=1,
            grid=(owners // group,),
            in_specs=[
                pl.BlockSpec(
                    (group, None, request_rows, capacity), lambda i, at: (i, at[1], 0, 0)
                ),
                pl.BlockSpec((lists, width), lambda i, at: (0, 0)),
            ],
            out_specs=pl.BlockSpec((group * capacity, width), lambda i, at: (i, 0)),
        ),
        out_shape=struct(owners * capacity, width, dtype=BF16),
        compiler_params=params(48),
        cost_estimate=cost(2 * owners * capacity * lists * width, 6 << 20),
        name="gather",
    )(place, requests.reshape(owners, replicas, request_rows, capacity), centroids)
    centres = lax.all_to_all(
        gathered.reshape(owners, capacity, width), "list", 0, 0, tiled=True
    ).reshape(owners * capacity, width)

    chunk = 8
    half_shape = struct(group_subs // 2, width_sub + 8, code_count)
    centre_sums = pl.pallas_call(
        functools.partial(centre_sums_kernel, chunk),
        grid_spec=pltpu.PrefetchScalarGridSpec(
            num_scalar_prefetch=1,
            grid=(1,),
            in_specs=[
                pl.BlockSpec((lists, share), lambda i, at: (0, at[1])),
                pl.BlockSpec((devices, request_rows, capacity), lambda i, at: (0, 0, 0)),
            ],
            out_specs=pl.BlockSpec((group_subs, width_sub, code_count), lambda i, at: (0, 0, 0)),
            scratch_shapes=[pltpu.VMEM((share, lists), BF16)],
        ),
        out_shape=struct(group_subs, width_sub, code_count),
        compiler_params=params(48),
        cost_estimate=cost(2 * devices * capacity * lists * share, 2 << 20),
        name="centre_sums",
    )(place, centroids, requests)
    keep, send = pl.pallas_call(
        functools.partial(row_sums_kernel, replicas, subs),
        grid_spec=pltpu.PrefetchScalarGridSpec(
            num_scalar_prefetch=1,
            grid=(1,),
            in_specs=[
                pl.BlockSpec((group_subs, width_sub, code_count), lambda i, at: (0, 0, 0)),
                pl.BlockSpec((group_subs, width_sub, code_count), lambda i, at: (at[1], 0, 0)),
            ]
            + [pl.BlockSpec(b.shape, lambda i, at: (0, 0)) for b in got_blocks],
            out_specs=[pl.BlockSpec(half_shape.shape, lambda i, at: (0, 0, 0))] * 2,
        ),
        out_shape=[half_shape] * 2,
        compiler_params=params(48),
        cost_estimate=cost(1 << 30, 2 << 20),
        name="row_sums",
    )(place, centre_sums, book, *got_blocks)

    own = keep + swap(send, "list", 1)
    others = [swap(own, "list", s) for s in range(2, owners, 2)]
    own = functools.reduce(jnp.add, others, own)
    own = own[:, :width_sub] / own[:, width_sub : width_sub + 1]
    other = swap(own, "list", 1)
    first = lax.axis_index("list") % 2 == 0
    new_codebook = jnp.concatenate(
        [jnp.where(first, own, other), jnp.where(first, other, own)], axis=0
    )

    offsets = pl.pallas_call(
        offset_kernel,
        in_specs=[VMEM] * 3,
        out_specs=VMEM,
        out_shape=struct(row_count, width),
        compiler_params=params(48),
        cost_estimate=cost(2 << 30, 2 << 20),
        name="offsets",
    )(memory_rows, codes, book)
    row_error = pl.pallas_call(
        error_kernel,
        in_specs=[SMEM] + [VMEM] * 3,
        out_specs=VMEM,
        out_shape=struct(1, row_count),
        compiler_params=params(48),
        cost_estimate=cost(2 * owners * capacity * row_count * width, 3 << 20),
        name="errors",
    )(valid_rows, position, offsets, centres)
    return (jnp.transpose(new_codebook, (0, 2, 1)), row_error.reshape(row_count))


def solution(mesh):
    in_specs = (
        P(("list", "rep"), None),
        P(("list", "rep"), None),
        P(("list", "rep")),
        P(("list", "rep"), None),
        P(("list", "rep")),
        P("list", None),
        P(),
    )
    out_specs = (P("rep", None, None), P(("list", "rep")))
    return jax.shard_map(body, mesh=mesh, in_specs=in_specs, out_specs=out_specs, check_vma=False)
```

time: 102 us -> 72.8 us (0.71)
  waiting for transfers between devices: 28.2 us -> 11.8 us
  starting transfers between devices: 20.9 us -> 11.9 us
  blocking collectives: 7.51 us -> 15.7 us
  local copies, waits for them, and re-layouts: 13.2 us -> 6.39 us
  Pallas kernels: 29.8 us -> 23.6 us
    ppermute x15 -> x8, waiting for transfers between devices: 28.2 us -> 11.8 us  [swap(): return lax.ppermute(array, axis, [(i, i ^ step) for i in range(count)])]
    all_to_all x1, blocking collectives: 7.51 us -> 15.7 us  [body(): requests = lax.all_to_all(requests, ('list', 'rep'), 0, 0, tiled=True)]
    unnamed x32 -> x27, local copies, waits for them, and re-layouts: 13.2 us -> 6.38 us
    pallas_call x5, Pallas kernels: 27.6 us -> 21.3 us  [the longest x1 8.37 us: body(): pl.pallas_call(functools.partial(centre_sums_kernel, chunk), grid_spec=pl...]
    ppermute x15 -> x8, starting transfers between devices: 13.6 us -> 8.13 us  [swap(): return lax.ppermute(array, axis, [(i, i ^ step) for i in range(count)])]
    all_to_all x1, starting transfers between devices: 7.3 us -> 3.75 us  [body(): lax.all_to_all(gathered.reshape(owners, capacity, width), 'list', 0, 0, t...]
  transfers between devices with their start and end apart: 16 -> 9, of which waited for: 7 -> 4; matrix products, arithmetic and copies ran while one was open for 1% -> 1% of each run, Pallas kernels for 15% -> 16%
where the time goes in v2:
time: 72.8 us; the launch traced here: 72.3 us
  Pallas kernels  23.6 us (32%)
  blocking collectives  15.7 us (22%)
  starting transfers between devices  11.9 us (16%)
  waiting for transfers between devices  11.8 us (16%)
  local copies, waits for them, and re-layouts  6.39 us (9%)
  between operations  1.48 us (2%)
  other arithmetic  1.38 us (2%)
    all_to_all x1, blocking collectives, body(): requests = lax.all_to_all(requests, ('list', 'rep'), 0, 0, tiled=True)  15.7 us
    ppermute x8, waiting for transfers between devices, swap(): return lax.ppermute(array, axis, [(i, i ^ step) for i in range(count)])  11.8 us
    pallas_call x1, Pallas kernels, body(): pl.pallas_call(functools.partial(centre_sums_kernel, chunk), grid_spec=pl...  8.37 us
    pallas_call x1, Pallas kernels, body(): pl.pallas_call(functools.partial(gather_kernel, group_subs), grid_spec=pl...  8.15 us
    ppermute x8, starting transfers between devices, swap(): return lax.ppermute(array, axis, [(i, i ^ step) for i in range(count)])  8.13 us
    unnamed x27, local copies, waits for them, and re-layouts  6.38 us
    all_to_all x1, starting transfers between devices, body(): lax.all_to_all(gathered.reshape(owners, capacity, width), 'list', 0, 0, t...  3.75 us
    pallas_call x1, Pallas kernels, body(): pl.pallas_call(functools.partial(row_sums_kernel, replicas, subs), grid_s...  2.34 us
  transfers between devices with their start and end apart: 9, of which 4 were waited for; matrix products, arithmetic and copies ran while one was open for 1% of the time, Pallas kernels for 16%

profile of v2, /device:TPU:0, one launch (start us, length us, event | category | flops | bytes accessed | tf_op | source)
XLA Modules:
  0.0 72.3 jit_solution(5800269168232561022)
XLA Ops:
  1.3 0.6 pad_add_fusion.place
  1.8 2.3 %pack.1 = (bf16[272,256]{1,0:T(8,128)(2,1)}, bf16[272,256]{1,0:T(8,128)(2,1)}, bf16[272,256]{1,0:T(8,128)(2,1)}, bf16[272,256]{1,0:T(8,128)(2,1)}, bf16[32,16,128]{2,1,0:T(8,128)(2,1)}, /*index=5*/s32[1,256]{1,0:T(1,128)}) custom-call(s32[2]{0:T(128)} %pad_add_fusion.place, s32[1]{0:T(128)S(6)} %copy.12.valid, bf16[256,1024]{1,0:T(8,128)(2,1)} %rows.3, ...), custom_call_target="tpu_custom_call" | custom-call | flops 1048576 | bytes 1048576 | tf_op jit(solution)/shard_map/pack/pallas_call | solution.py:239
  4.1 15.7 %all_to_all.10.requests = bf16[32,16,128]{2,1,0:T(8,128)(2,1)S(1)} all-to-all(bf16[32,16,128]{2,1,0:T(8,128)(2,1)} %get-tuple-element.10), channel_id=1, replica_groups=mesh['list'=8,'rep'=4] {'list','rep'}, dimensions={0} | all-to-all | bytes 262144 | tf_op jit(solution)/shard_map/all_to_all | solution.py:262
  19.9 0.6 copy-done.4
  20.4 8.2 %gather.1 = bf16[1024,1024]{1,0:T(8,128)(2,1)S(1)} custom-call(s32[2]{0:T(128)S(1)} %copy-done.4, bf16[8,4,16,128]{3,2,1,0:T(8,128)(2,1)S(1)} %bitcast.17, bf16[2048,1024]{1,0:T(8,128)(2,1)} %centres.3), custom_call_target="tpu_custom_call" | custom-call | flops 4294967296 | bytes 6291456 | tf_op jit(solution)/shard_map/gather/pallas_call | solution.py:266
  28.6 1.3 %copy-done = bf16[1024,1024]{1,0:T(8,128)(2,1)} copy-done((bf16[1024,1024]{1,0:T(8,128)(2,1)}, bf16[1024,1024]{1,0:T(8,128)(2,1)S(1)}, u32[]{:S(2)}) %copy-start) | copy-done | bytes 2097176
  29.9 3.7 %all-to-all-start.1 = ((bf16[8,128,1024]{2,1,0:T(8,128)(2,1)}), bf16[8,128,1024]{2,1,0:T(8,128)(2,1)S(1)}, u32[]{:S(2)}, u32[]{:S(2)}) async-start(bf16[8,128,1024]{2,1,0:T(8,128)(2,1)} %bitcast.16), calls=%async_computation.1 | async-start | bytes 4194304 | tf_op jit(solution)/shard_map/all_to_all | solution.py:284
  33.8 1.7 %collective-permute-start.1 = (bf16[272,256]{1,0:T(8,128)(2,1)S(1)}, bf16[272,256]{1,0:T(8,128)(2,1)S(1)}, u32[]{:S(2)}, u32[]{:S(2)}) collective-permute-start(bf16[272,256]{1,0:T(8,128)(2,1)S(1)} %copy-done.11), channel_id=1, source_target_pairs={{0,2},{1,3},{2,0},{3,1},{4,6},{5,7},{6,4},{7,5},{8,10},{9,11},{10,... | collective-permute-start | bytes 417800 | tf_op jit(solution)/shard_map/ppermute | solution.py:210
  35.5 2.6 %collective-permute-start.2 = (bf16[272,256]{1,0:T(8,128)(2,1)S(1)}, bf16[272,256]{1,0:T(8,128)(2,1)S(1)}, u32[]{:S(2)}, u32[]{:S(2)}) collective-permute-start(bf16[272,256]{1,0:T(8,128)(2,1)S(1)} %copy-done.10), channel_id=1, source_target_pairs={{0,3},{1,2},{2,1},{3,0},{4,7},{5,6},{6,5},{7,4},{8,11},{9,10},{10,... | collective-permute-start | bytes 417800 | tf_op jit(solution)/shard_map/ppermute | solution.py:210
  38.2 2.2 %copy-done.6 = bf16[2048,1024]{1,0:T(8,128)(2,1)S(1)} copy-done((bf16[2048,1024]{1,0:T(8,128)(2,1)S(1)}, bf16[2048,1024]{1,0:T(8,128)(2,1)}, u32[]{:S(2)}) %copy-start.6) | copy-done | bytes 4194328
  40.3 8.4 %centre_sums.1 = f32[4,64,256]{2,1,0:T(8,128)S(1)} custom-call(s32[2]{0:T(128)S(1)} %copy-done.5, bf16[2048,1024]{1,0:T(8,128)(2,1)S(1)} %copy-done.6, bf16[32,16,128]{2,1,0:T(8,128)(2,1)S(1)} %all_to_all.10.requests), custom_call_target="tpu_custom_call" | custom-call | flops 4294967296 | bytes 2097152 | tf_op jit(solution)/shard_map/centre_sums/pallas_call | solution.py:290
  48.8 2.3 %row_sums.1 = (f32[2,72,256]{2,1,0:T(8,128)S(1)}, f32[2,72,256]{2,1,0:T(8,128)S(1)}) custom-call(s32[2]{0:T(128)S(1)} %copy-done.5, f32[4,64,256]{2,1,0:T(8,128)S(1)} %centre_sums.1, f32[16,64,256]{2,1,0:T(8,128)S(1)} %bitcast.20, bf16[272,256]{1,0:T(8,128)(2,1)S(1)} %copy-done.9, bf16[272,256]{1,0:T(8,128)(2,1)S(1)} %collective-permute-done.refs_1_, ...), custom_call_target="tpu_custom_call" | custom-call | flops 1073741824 | bytes 2097152 | tf_op jit(solution)/shard_map/row_sums/pallas_call | solution.py:307
  51.2 1.4 %collective-permute-done.3 = f32[2,72,256]{2,1,0:T(8,128)S(1)} collective-permute-done((f32[2,72,256]{2,1,0:T(8,128)S(1)}, f32[2,72,256]{2,1,0:T(8,128)S(1)}, u32[]{:S(2)}, u32[]{:S(2)}) %collective-permute-start.3) | collective-permute-done | bytes 147488 | tf_op jit(solution)/shard_map/ppermute | solution.py:210
  52.6 1.9 %collective-permute-start.4 = (f32[2,72,256]{2,1,0:T(8,128)S(1)}, f32[2,72,256]{2,1,0:T(8,128)S(1)}, u32[]{:S(2)}, u32[]{:S(2)}) collective-permute-start(f32[2,72,256]{2,1,0:T(8,128)S(1)} %add.17), channel_id=1, source_target_pairs={{0,8},{4,12},{8,0},{12,4},{16,24},{20,28},{24,16},{28,20},{1,9},{5... | collective-permute-start | bytes 442376 | tf_op jit(solution)/shard_map/ppermute | solution.py:210
  54.5 1.5 %collective-permute-start.5 = (f32[2,72,256]{2,1,0:T(8,128)S(1)}, f32[2,72,256]{2,1,0:T(8,128)S(1)}, u32[]{:S(2)}, u32[]{:S(2)}) collective-permute-start(f32[2,72,256]{2,1,0:T(8,128)S(1)} %add.17), channel_id=1, source_target_pairs={{0,16},{4,20},{8,24},{12,28},{16,0},{20,4},{24,8},{28,12},{1,17},{... | collective-permute-start | bytes 442376 | tf_op jit(solution)/shard_map/ppermute | solution.py:210
  56.0 0.1 collective-permute-start.6
  56.1 6.9 %collective-permute-done.4 = f32[2,72,256]{2,1,0:T(8,128)S(1)} collective-permute-done((f32[2,72,256]{2,1,0:T(8,128)S(1)}, f32[2,72,256]{2,1,0:T(8,128)S(1)}, u32[]{:S(2)}, u32[]{:S(2)}) %collective-permute-start.4) | collective-permute-done | bytes 147488 | tf_op jit(solution)/shard_map/ppermute | solution.py:210
  63.0 0.8 %collective-permute-done.5 = f32[2,72,256]{2,1,0:T(8,128)S(1)} collective-permute-done((f32[2,72,256]{2,1,0:T(8,128)S(1)}, f32[2,72,256]{2,1,0:T(8,128)S(1)}, u32[]{:S(2)}, u32[]{:S(2)}) %collective-permute-start.5) | collective-permute-done | bytes 147488 | tf_op jit(solution)/shard_map/ppermute | solution.py:210
  63.8 2.8 %collective-permute-done.6 = f32[2,72,256]{2,1,0:T(8,128)S(1)} collective-permute-done((f32[2,72,256]{2,1,0:T(8,128)S(1)}, f32[2,72,256]{2,1,0:T(8,128)S(1)}, u32[]{:S(2)}, u32[]{:S(2)}) %collective-permute-start.6) | collective-permute-done | bytes 147488 | tf_op jit(solution)/shard_map/ppermute | solution.py:210
  66.8 1.0 %copy-done.1 = bf16[256,1024]{1,0:T(8,128)(2,1)S(1)} copy-done((bf16[256,1024]{1,0:T(8,128)(2,1)S(1)}, bf16[256,1024]{1,0:T(8,128)(2,1)}, u32[]{:S(2)}) %copy-start.1) | copy-done | bytes 524312
  67.8 1.2 %copy-done.8 = f32[16,256,64]{1,2,0:T(8,128)S(1)} copy-done((f32[16,256,64]{1,2,0:T(8,128)S(1)}, f32[16,256,64]{1,2,0:T(8,128)}, u32[]{:S(2)}) %copy-start.8) | copy-done | bytes 1048600
  69.1 0.9 %offsets.1 = f32[256,1024]{1,0:T(8,128)S(1)} custom-call(bf16[256,1024]{1,0:T(8,128)(2,1)S(1)} %copy-done.1, s32[16,256]{1,0:T(8,128)S(1)} %bitcast.19, f32[16,64,256]{2,1,0:T(8,128)S(1)} %bitcast.21), custom_call_target="tpu_custom_call" | custom-call | flops 2147483648 | bytes 2097152 | tf_op jit(solution)/shard_map/offsets/pallas_call | solution.py:335
  70.0 0.7 maximum_bitcast_fusion
  70.8 1.5 %errors.1 = f32[1,256]{1,0:T(1,128)} custom-call(s32[1]{0:T(128)S(6)} %copy.12.valid, s32[1,256]{1,0:T(1,128)S(1)} %copy-done.3, f32[256,1024]{1,0:T(8,128)S(1)} %offsets.1, bf16[1024,1024]{1,0:T(8,128)(2,1)S(1)} %bitcast.15), custom_call_target="tpu_custom_call" | custom-call | flops 536870912 | bytes 3145728 | tf_op jit(solution)/shard_map/errors/pallas_call | solution.py:344
  (35 shorter events, 0.4 us)
Async XLA Ops:
  19.8 0.6 copy-start.4
  28.6 1.3 %copy-start = (bf16[1024,1024]{1,0:T(8,128)(2,1)}, bf16[1024,1024]{1,0:T(8,128)(2,1)S(1)}, u32[]{:S(2)}) copy-start(bf16[1024,1024]{1,0:T(8,128)(2,1)S(1)} %gather.1) | copy-start | bytes 6291460
  29.9 3.8 %copy-start.12 = (bf16[272,256]{1,0:T(8,128)(2,1)S(1)}, bf16[272,256]{1,0:T(8,128)(2,1)}, u32[]{:S(2)}) copy-start(bf16[272,256]{1,0:T(8,128)(2,1)} %get-tuple-element.12) | copy-start | bytes 417796
  29.9 3.9 %copy-start.11 = (bf16[272,256]{1,0:T(8,128)(2,1)S(1)}, bf16[272,256]{1,0:T(8,128)(2,1)}, u32[]{:S(2)}) copy-start(bf16[272,256]{1,0:T(8,128)(2,1)} %get-tuple-element.13) | copy-start | bytes 417796
  29.9 5.6 %copy-start.10 = (bf16[272,256]{1,0:T(8,128)(2,1)S(1)}, bf16[272,256]{1,0:T(8,128)(2,1)}, u32[]{:S(2)}) copy-start(bf16[272,256]{1,0:T(8,128)(2,1)} %get-tuple-element.14) | copy-start | bytes 417796
  29.9 8.2 %copy-start.5 = (s32[2]{0:T(128)S(1)}, s32[2]{0:T(128)}, u32[]{:S(2)}) copy-start(s32[2]{0:T(128)} %pad_add_fusion.place) | copy-start | bytes 28
  29.9 40.8 %all-to-all-start.1 = ((bf16[8,128,1024]{2,1,0:T(8,128)(2,1)}), bf16[8,128,1024]{2,1,0:T(8,128)(2,1)S(1)}, u32[]{:S(2)}, u32[]{:S(2)}) async-start(bf16[8,128,1024]{2,1,0:T(8,128)(2,1)} %bitcast.16), calls=%async_computation.1 | async-start | bytes 4194304 | tf_op jit(solution)/shard_map/all_to_all | solution.py:284
  33.7 15.0 %collective-permute-start = (bf16[272,256]{1,0:T(8,128)(2,1)S(1)}, bf16[272,256]{1,0:T(8,128)(2,1)S(1)}, u32[]{:S(2)}, u32[]{:S(2)}) collective-permute-start(bf16[272,256]{1,0:T(8,128)(2,1)S(1)} %copy-done.12), channel_id=1, source_target_pairs={{0,1},{1,0},{2,3},{3,2},{4,5},{5,4},{6,7},{7,6},{8,9},{9,8},{10,11... | collective-permute-start | bytes 417800 | tf_op jit(solution)/shard_map/ppermute | solution.py:210
  33.8 14.9 %collective-permute-start.1 = (bf16[272,256]{1,0:T(8,128)(2,1)S(1)}, bf16[272,256]{1,0:T(8,128)(2,1)S(1)}, u32[]{:S(2)}, u32[]{:S(2)}) collective-permute-start(bf16[272,256]{1,0:T(8,128)(2,1)S(1)} %copy-done.11), channel_id=1, source_target_pairs={{0,2},{1,3},{2,0},{3,1},{4,6},{5,7},{6,4},{7,5},{8,10},{9,11},{10,... | collective-permute-start | bytes 417800 | tf_op jit(solution)/shard_map/ppermute | solution.py:210
  35.5 13.2 %collective-permute-start.2 = (bf16[272,256]{1,0:T(8,128)(2,1)S(1)}, bf16[272,256]{1,0:T(8,128)(2,1)S(1)}, u32[]{:S(2)}, u32[]{:S(2)}) collective-permute-start(bf16[272,256]{1,0:T(8,128)(2,1)S(1)} %copy-done.10), channel_id=1, source_target_pairs={{0,3},{1,2},{2,1},{3,0},{4,7},{5,6},{6,5},{7,4},{8,11},{9,10},{10,... | collective-permute-start | bytes 417800 | tf_op jit(solution)/shard_map/ppermute | solution.py:210
  38.2 2.2 %copy-start.6 = (bf16[2048,1024]{1,0:T(8,128)(2,1)S(1)}, bf16[2048,1024]{1,0:T(8,128)(2,1)}, u32[]{:S(2)}) copy-start(bf16[2048,1024]{1,0:T(8,128)(2,1)} %centres.3) | copy-start | bytes 12582916
  40.3 8.4 %copy-start.7 = (f32[16,256,64]{1,2,0:T(8,128)S(1)}, f32[16,256,64]{1,2,0:T(8,128)}, u32[]{:S(2)}) copy-start(f32[16,256,64]{1,2,0:T(8,128)} %param.13) | copy-start | bytes 3145732
  40.3 8.4 %copy-start.9 = (bf16[272,256]{1,0:T(8,128)(2,1)S(1)}, bf16[272,256]{1,0:T(8,128)(2,1)}, u32[]{:S(2)}) copy-start(bf16[272,256]{1,0:T(8,128)(2,1)} %get-tuple-element.11.refs_0_) | copy-start | bytes 417796
  48.8 18.0 %copy-start.2 = (s32[256,16]{0,1:T(8,128)S(1)}, s32[256,16]{0,1:T(8,128)}, u32[]{:S(2)}) copy-start(s32[256,16]{0,1:T(8,128)} %param.10) | copy-start | bytes 49156
  51.1 1.4 %collective-permute-start.3 = (f32[2,72,256]{2,1,0:T(8,128)S(1)}, f32[2,72,256]{2,1,0:T(8,128)S(1)}, u32[]{:S(2)}, u32[]{:S(2)}) collective-permute-start(f32[2,72,256]{2,1,0:T(8,128)S(1)} %get-tuple-element.16), channel_id=1, source_target_pairs={{0,4},{4,0},{8,12},{12,8},{16,20},{20,16},{24,28},{28,24},{1,5},{5... | collective-permute-start | bytes 442376 | tf_op jit(solution)/shard_map/ppermute | solution.py:210
  52.6 10.4 %collective-permute-start.4 = (f32[2,72,256]{2,1,0:T(8,128)S(1)}, f32[2,72,256]{2,1,0:T(8,128)S(1)}, u32[]{:S(2)}, u32[]{:S(2)}) collective-permute-start(f32[2,72,256]{2,1,0:T(8,128)S(1)} %add.17), channel_id=1, source_target_pairs={{0,8},{4,12},{8,0},{12,4},{16,24},{20,28},{24,16},{28,20},{1,9},{5... | collective-permute-start | bytes 442376 | tf_op jit(solution)/shard_map/ppermute | solution.py:210
  54.5 9.3 %collective-permute-start.5 = (f32[2,72,256]{2,1,0:T(8,128)S(1)}, f32[2,72,256]{2,1,0:T(8,128)S(1)}, u32[]{:S(2)}, u32[]{:S(2)}) collective-permute-start(f32[2,72,256]{2,1,0:T(8,128)S(1)} %add.17), channel_id=1, source_target_pairs={{0,16},{4,20},{8,24},{12,28},{16,0},{20,4},{24,8},{28,12},{1,17},{... | collective-permute-start | bytes 442376 | tf_op jit(solution)/shard_map/ppermute | solution.py:210
  56.0 10.6 %collective-permute-start.6 = (f32[2,72,256]{2,1,0:T(8,128)S(1)}, f32[2,72,256]{2,1,0:T(8,128)S(1)}, u32[]{:S(2)}, u32[]{:S(2)}) collective-permute-start(f32[2,72,256]{2,1,0:T(8,128)S(1)} %add.17), channel_id=1, source_target_pairs={{0,24},{4,28},{8,16},{12,20},{16,8},{20,12},{24,0},{28,4},{1,25},{... | collective-permute-start | bytes 442376 | tf_op jit(solution)/shard_map/ppermute | solution.py:210
  66.7 3.3 %collective-permute-start.7 = (f32[2,64,256]{2,1,0:T(8,128)S(1)}, f32[2,64,256]{2,1,0:T(8,128)S(1)}, u32[]{:S(2)}, u32[]{:S(2)}) collective-permute-start(f32[2,64,256]{2,1,0:T(8,128)S(1)} %slice_divide_fusion), channel_id=1, source_target_pairs={{0,4},{4,0},{8,12},{12,8},{16,20},{20,16},{24,28},{28,24},{1,5},{5... | collective-permute-start | bytes 393224 | tf_op jit(solution)/shard_map/ppermute | solution.py:210
  66.8 1.0 %copy-start.1 = (bf16[256,1024]{1,0:T(8,128)(2,1)S(1)}, bf16[256,1024]{1,0:T(8,128)(2,1)}, u32[]{:S(2)}) copy-start(bf16[256,1024]{1,0:T(8,128)(2,1)} %rows.3) | copy-start | bytes 1572868
  67.8 1.2 %copy-start.8 = (f32[16,256,64]{1,2,0:T(8,128)S(1)}, f32[16,256,64]{1,2,0:T(8,128)}, u32[]{:S(2)}) copy-start(f32[16,256,64]{1,2,0:T(8,128)} %param.13) | copy-start | bytes 3145732
  69.1 1.7 %copy-start.3 = (s32[1,256]{1,0:T(1,128)S(1)}, s32[1,256]{1,0:T(1,128)}, u32[]{:S(2)}) copy-start(s32[1,256]{1,0:T(1,128)} %get-tuple-element.17.position) | copy-start | bytes 3076

commit v3 on v2

v3 whole, which is shorter than its diff:
```python
import functools

import jax
import jax.numpy as jnp
from jax import lax
from jax.experimental import pallas as pl
from jax.experimental.pallas import tpu as pltpu
from jax.sharding import PartitionSpec as P

prior_weight = 4.0
F32, BF16, I32 = jnp.float32, jnp.bfloat16, jnp.int32
VMEM = pl.BlockSpec(memory_space=pltpu.VMEM)
ANY = pl.BlockSpec(memory_space=pl.ANY)
SMEM = pl.BlockSpec(memory_space=pltpu.SMEM)
NT = (((1,), (1,)), ((), ()))
extra = 16


def mask_bf16(mask):
    return jnp.where(mask, 1.0, 0.0).astype(BF16)


def dot(a, b):
    return jnp.dot(a, b, preferred_element_type=F32)


def dot_nt(a, b):
    return lax.dot_general(a, b, NT, preferred_element_type=F32)


def pack_kernel(owners, capacity, valid, owner, slot, codes, requests, position_out):
    row_count = owner.shape[1]
    lane = lax.broadcasted_iota(I32, (1, row_count), 1)
    live = lane < valid[0]
    target = jnp.where(live, owner[...], -1)
    hit = jnp.where(lax.broadcasted_iota(I32, (owners, row_count), 0) == target, 1.0, 0.0)
    earlier = mask_bf16(
        lax.broadcasted_iota(I32, (row_count, row_count), 0)
        < lax.broadcasted_iota(I32, (row_count, row_count), 1)
    )
    before = dot(hit.astype(BF16), earlier)
    rank = jnp.sum(hit * before, axis=0, keepdims=True).astype(I32)
    position = jnp.where(live, target * capacity + rank, -1)
    position_out[...] = position

    high = (slot[...] // 256).astype(F32)
    low = (slot[...] % 256).astype(F32)
    which = lax.broadcasted_iota(I32, (extra, row_count), 0)
    tail = jnp.where(which == 0, high, jnp.where(which == 1, low, 0.0))
    info = jnp.concatenate([codes[...].astype(F32) - 256.0, tail], axis=0).astype(BF16)
    within = lax.broadcasted_iota(I32, (capacity, row_count), 0)
    for dest in range(owners):
        place_at = mask_bf16(within == position - dest * capacity)
        requests[dest] = dot_nt(info, place_at).astype(BF16)


def row_sums_kernel(valid, rows, codes, out):
    subs, padded, code_count = out.shape
    row_count, width = rows.shape
    width_sub = width // subs
    lane = lax.broadcasted_iota(I32, (1, row_count), 1)
    live_codes = jnp.where(lane < valid[0], codes[...], -1)
    columns = rows[...].T
    code_iota = lax.broadcasted_iota(I32, (code_count, row_count), 0)
    ones = jnp.ones((16, row_count), BF16)
    for m in range(subs):
        code_hit = mask_bf16(code_iota == live_codes[m : m + 1])
        out[m, 0:width_sub] = dot_nt(columns[m * width_sub : (m + 1) * width_sub], code_hit)
        out[m, width_sub:padded] = dot_nt(ones, code_hit)[0 : padded - width_sub]


def sums_kernel(replicas, requests, gathered, row_sums, keep, send):
    subs, padded, code_count = row_sums.shape
    owners, _, capacity = requests.shape
    slots, width = gathered.shape
    width_sub = width // subs
    group_subs = subs // replicas
    half = group_subs // 2
    mine = jnp.bitwise_and(lax.axis_index("list"), 1)
    rep = lax.axis_index("rep")
    asked = jnp.concatenate([requests[j] for j in range(owners)], axis=1)
    codes = asked.astype(F32).astype(I32) + 256
    code_iota = lax.broadcasted_iota(I32, (code_count, slots), 0)
    first = lax.broadcasted_iota(I32, (code_count, 2 * width_sub), 1) < width_sub
    for pair in range(subs // 2):
        span = slice(pair * 2 * width_sub, (pair + 1) * 2 * width_sub)
        found = [
            dot(mask_bf16(code_iota == codes[m : m + 1]), gathered[:, span])
            for m in (2 * pair, 2 * pair + 1)
        ]
        centre_sums = jnp.where(first, found[0], found[1]).T
        for j in range(2):
            m = 2 * pair + j
            sums = row_sums[m, 0:width_sub] - centre_sums[j * width_sub : (j + 1) * width_sub]
            counts = row_sums[m, width_sub:padded]
            group, at = m // group_subs, m % group_subs
            step = jnp.bitwise_xor(rep, group)

            def store(out, sums=sums, counts=counts, step=step, at=at):
                out[step, at % half, 0:width_sub] = sums
                out[step, at % half, width_sub:padded] = counts

            pl.when(mine == at // half)(functools.partial(store, keep))
            pl.when(mine != at // half)(functools.partial(store, send))


def gather_kernel(subs, requests, centres, pieces, near, hit, found, read, written):
    owners, _, capacity = requests.shape
    slots, lists = hit.shape
    loads = []
    for part in range(read.shape[0]):
        rows = pl.ds(part * (lists // read.shape[0]), lists // read.shape[0])
        loads.append(pltpu.make_async_copy(centres.at[rows], near.at[rows], read.at[part]))
        loads[-1].start()
    chunk = 4
    span = chunk * capacity
    for first in range(0, owners, chunk):
        asked = jnp.concatenate([requests[first + j] for j in range(chunk)], axis=1)
        turned = asked.astype(F32).T.astype(I32)
        high, low = (turned[:, subs + i : subs + i + 1] for i in range(2))
        low_hit = mask_bf16(lax.broadcasted_iota(I32, (span, 256), 1) == low)
        for h in range(lists // 256):
            hit[first * capacity : first * capacity + span, h * 256 : (h + 1) * 256] = (
                low_hit * mask_bf16(high == h)
            )
    for load in loads:
        load.wait()
    stores = []
    for index in range(owners // chunk):
        part = dot(hit[index * span : (index + 1) * span], near[...]).astype(BF16)
        found[index * chunk : (index + 1) * chunk] = part.reshape((chunk, *found.shape[1:]))
        block = pl.ds(index * chunk, chunk)
        stores.append(
            pltpu.make_async_copy(found.at[block], pieces.at[block], written.at[index])
        )
        stores[-1].start()
    for store in stores:
        store.wait()


def offset_kernel(rows, codes, book, out):
    subs, width_sub, code_count = book.shape
    row_count = rows.shape[0]
    turned = codes[...].astype(F32).T.astype(I32)
    code_iota = lax.broadcasted_iota(I32, (row_count, code_count), 1)
    empty = jnp.zeros((width_sub, code_count), BF16)
    for pair in range(subs // 2):
        hits, highs, lows = [], [], []
        for m in (2 * pair, 2 * pair + 1):
            hits.append(mask_bf16(code_iota == turned[:, m : m + 1]))
            high = book[m].astype(BF16)
            highs.append(high)
            lows.append((book[m] - high.astype(F32)).astype(BF16))
        table = jnp.concatenate(
            [
                jnp.concatenate([highs[0], empty], axis=1),
                jnp.concatenate([empty, highs[1]], axis=1),
                jnp.concatenate([lows[0], empty], axis=1),
                jnp.concatenate([empty, lows[1]], axis=1),
            ],
            axis=0,
        )
        recon = dot_nt(jnp.concatenate(hits, axis=1), table)
        lanes = 2 * width_sub
        span = slice(pair * lanes, (pair + 1) * lanes)
        out[:, span] = rows[:, span].astype(F32) - (recon[:, :lanes] + recon[:, lanes:])


def error_kernel(valid, position, offsets, centres, out):
    slots, width = centres.shape
    row_count = offsets.shape[0]
    column_at = jnp.broadcast_to(position[...].astype(F32), (8, row_count)).T.astype(I32)[:, 0:1]
    hit = mask_bf16(lax.broadcasted_iota(I32, (row_count, slots), 1) == column_at)
    partial = jnp.zeros((row_count, 128), F32)
    for start in range(0, width, 256):
        gap = offsets[:, start : start + 256] - dot(hit, centres[:, start : start + 256])
        square = gap * gap
        partial += square[:, :128] + square[:, 128:]
    error = jnp.sum(partial.T, axis=0, keepdims=True) * (1.0 / width)
    lane = lax.broadcasted_iota(I32, (1, row_count), 1)
    out[...] = jnp.where(lane < valid[0], error, 0.0)


def swap(array, axis, step):
    count = lax.axis_size(axis)
    return lax.ppermute(array, axis, [(i, i ^ step) for i in range(count)])


def struct(*shape, dtype=F32):
    return jax.ShapeDtypeStruct(shape, dtype)


def params(mib):
    return pltpu.CompilerParams(vmem_limit_bytes=mib << 20)


def cost(flops, size):
    return pl.CostEstimate(flops=int(flops), bytes_accessed=int(size), transcendentals=0)


def body(memory_rows, list_owner, list_slot, pq_codes, valid_rows, centroids, codebook):
    row_count, width = memory_rows.shape
    lists = centroids.shape[0]
    subs, code_count, width_sub = codebook.shape
    owners, replicas = lax.axis_size("list"), lax.axis_size("rep")
    capacity = max(128, 4 * row_count // owners)
    group_subs = subs // replicas
    half = group_subs // 2
    padded = width_sub + 8
    book = jnp.transpose(codebook, (0, 2, 1))
    codes = pq_codes.T

    requests, position = pl.pallas_call(
        functools.partial(pack_kernel, owners, capacity),
        in_specs=[SMEM] + [VMEM] * 3,
        out_specs=[VMEM] * 2,
        out_shape=[
            struct(owners, subs + extra, capacity, dtype=BF16),
            struct(1, row_count, dtype=I32),
        ],
        compiler_params=params(60),
        cost_estimate=cost(1000, 1000),
        name="pack",
    )(
        valid_rows,
        list_owner.reshape(1, row_count),
        list_slot.reshape(1, row_count),
        codes,
    )
    requests = lax.all_to_all(requests, "list", 0, 0, tiled=True)

    row_sums = pl.pallas_call(
        row_sums_kernel,
        in_specs=[SMEM] + [VMEM] * 2,
        out_specs=VMEM,
        out_shape=struct(subs, padded, code_count),
        compiler_params=params(40),
        cost_estimate=cost(1000, 1000),
        name="row_sums",
    )(valid_rows, memory_rows, codes)
    offsets = pl.pallas_call(
        offset_kernel,
        in_specs=[VMEM] * 3,
        out_specs=VMEM,
        out_shape=struct(row_count, width),
        compiler_params=params(48),
        cost_estimate=cost(1000, 1000),
        name="offsets",
    )(memory_rows, codes, book)
    requests, row_sums = lax.optimization_barrier((requests, row_sums))
    gathered = pl.pallas_call(
        functools.partial(gather_kernel, subs),
        in_specs=[VMEM, ANY],
        out_specs=ANY,
        out_shape=struct(owners, capacity, width, dtype=BF16),
        scratch_shapes=[
            pltpu.VMEM((lists, width), BF16),
            pltpu.VMEM((owners * capacity, lists), BF16),
            pltpu.VMEM((owners, capacity, width), BF16),
            pltpu.SemaphoreType.DMA((8,)),
            pltpu.SemaphoreType.DMA((owners // 4,)),
        ],
        compiler_params=params(60),
        cost_estimate=cost(4 << 30, 6 << 20),
        name="gather",
    )(requests, centroids)
    pieces = lax.all_to_all(gathered, "list", 0, 0, tiled=True)

    half_shape = struct(replicas, half, padded, code_count)
    keep, send = pl.pallas_call(
        functools.partial(sums_kernel, replicas),
        in_specs=[VMEM] * 3,
        out_specs=[VMEM] * 2,
        out_shape=[half_shape] * 2,
        compiler_params=params(40),
        cost_estimate=cost(1000, 1000),
        name="sums",
    )(requests, gathered.reshape(owners * capacity, width), row_sums)

    own = keep + swap(send, "list", 1)
    row = lax.broadcasted_iota(I32, own.shape, 2)
    high = jnp.floor(own * (1.0 / 256.0))
    own = jnp.where(
        row < width_sub, own, jnp.where(row == width_sub, high, own - 256.0 * high)
    )
    own = own[0] + sum(
        swap(own[s].astype(BF16), "rep", s).astype(F32) for s in range(1, replicas)
    )
    own, offsets = lax.optimization_barrier((own, offsets))
    others = [swap(own, "list", s) for s in range(2, owners, 2)]
    pieces, *others = lax.optimization_barrier((pieces, *others))
    own = functools.reduce(jnp.add, others, own)
    core = lax.axis_index("list") % 2
    start = lax.axis_index("rep") * group_subs + core * half
    prior = prior_weight * lax.dynamic_slice_in_dim(book, start, half, 0)
    counts = 256.0 * own[:, width_sub : width_sub + 1] + own[:, width_sub + 1 : width_sub + 2]
    own = (own[:, :width_sub] + prior) / (counts + prior_weight)
    other = swap(own, "list", 1)
    new_codebook = jnp.concatenate(
        [jnp.where(core == 0, own, other), jnp.where(core == 0, other, own)], axis=0
    )
    row_error = pl.pallas_call(
        error_kernel,
        in_specs=[SMEM] + [VMEM] * 3,
        out_specs=VMEM,
        out_shape=struct(1, row_count),
        compiler_params=params(48),
        cost_estimate=cost(1000, 1000),
        name="errors",
    )(valid_rows, position, offsets, pieces.reshape(owners * capacity, width))
    return (jnp.transpose(new_codebook, (0, 2, 1)), row_error.reshape(row_count))


def solution(mesh):
    in_specs = (
        P(("list", "rep"), None),
        P(("list", "rep"), None),
        P(("list", "rep")),
        P(("list", "rep"), None),
        P(("list", "rep")),
        P("list", None),
        P(),
    )
    out_specs = (P("rep", None, None), P(("list", "rep")))
    return jax.shard_map(body, mesh=mesh, in_specs=in_specs, out_specs=out_specs, check_vma=False)
```

time: 72.8 us -> 64.3 us (0.88)
  blocking collectives: 15.7 us -> 0 us
  waiting for transfers between devices: 11.8 us -> 19.3 us
  starting transfers between devices: 11.9 us -> 17.5 us
  Pallas kernels: 23.6 us -> 18.5 us
  local copies, waits for them, and re-layouts: 6.39 us -> 4.05 us
  other arithmetic: 1.38 us -> 2.97 us
    all_to_all x1 -> x0, blocking collectives: 15.7 us -> none  [body(): requests = lax.all_to_all(requests, ('list', 'rep'), 0, 0, tiled=True)]
    ppermute x8, waiting for transfers between devices: 11.8 us -> 17.3 us  [swap(): return lax.ppermute(array, axis, [(i, i ^ step) for i in range(count)])]
    pallas_call x4, Pallas kernels: 21.2 us -> 16 us  [the longest x1 8.53 us: body(): pl.pallas_call(functools.partial(gather_kernel, subs), in_specs=[VMEM, AN...]
    all_to_all x1 -> x2, starting transfers between devices: 3.75 us -> 8.92 us  [the longest x1 5.17 us: body(): requests = lax.all_to_all(requests, 'list', 0, 0, tiled=True)]
    unnamed x27 -> x19, local copies, waits for them, and re-layouts: 6.38 us -> 4.03 us
    all_to_all x1 -> x2, waiting for transfers between devices: 0.01 us -> 1.96 us  [the longest x1 1.96 us: body(): requests = lax.all_to_all(requests, 'list', 0, 0, tiled=True)]
    add x1, other arithmetic: 0.04 us -> 1.03 us  [body(): own = functools.reduce(jnp.add, others, own)]
    div x1, other arithmetic: 0.02 us -> 0.94 us  [body(): own = (own[:, :width_sub] + prior) / (counts + prior_weight)]
  transfers between devices with their start and end apart: 9 -> 10, of which waited for: 4 -> 6; matrix products, arithmetic and copies ran while one was open for 1% -> 0% of each run, Pallas kernels for 16% -> 13%
where the time goes in v3:
time: 64.3 us; the launch traced here: 63.7 us
  waiting for transfers between devices  19.3 us (30%)
  Pallas kernels  18.5 us (29%)
  starting transfers between devices  17.5 us (27%)
  local copies, waits for them, and re-layouts  4.05 us (6%)
  other arithmetic  2.97 us (5%)
  between operations  1.46 us (2%)
    ppermute x8, waiting for transfers between devices, swap(): return lax.ppermute(array, axis, [(i, i ^ step) for i in range(count)])  17.3 us
    ppermute x8, starting transfers between devices, swap(): return lax.ppermute(array, axis, [(i, i ^ step) for i in range(count)])  8.56 us
    pallas_call x1, Pallas kernels, body(): pl.pallas_call(functools.partial(gather_kernel, subs), in_specs=[VMEM, AN...  8.53 us
    all_to_all x1, starting transfers between devices, body(): requests = lax.all_to_all(requests, 'list', 0, 0, tiled=True)  5.17 us
    pallas_call x1, Pallas kernels, body(): pl.pallas_call(functools.partial(sums_kernel, replicas), in_specs=[VMEM]...  4.31 us
    unnamed x19, local copies, waits for them, and re-layouts  4.03 us
    all_to_all x1, starting transfers between devices, body(): pieces = lax.all_to_all(gathered, 'list', 0, 0, tiled=True)  3.75 us
    all_to_all x1, waiting for transfers between devices, body(): requests = lax.all_to_all(requests, 'list', 0, 0, tiled=True)  1.96 us
  transfers between devices with their start and end apart: 10, of which 6 were waited for; matrix products, arithmetic and copies ran while one was open for 0% of the time, Pallas kernels for 13%

profile of v3, /device:TPU:0, one launch (start us, length us, event | category | flops | bytes accessed | tf_op | source)
XLA Modules:
  0.0 63.7 jit_solution(2846722128885212903)
XLA Ops:
  1.3 1.9 %pack.1 = (bf16[8,32,128]{2,1,0:T(8,128)(2,1)}, s32[1,256]{1,0:T(1,128)}) custom-call(s32[1]{0:T(128)S(6)} %copy.12.valid, s32[1,256]{1,0:T(1,128)} %bitcast.32, s32[1,256]{1,0:T(1,128)} %bitcast.33, s32[16,256]{1,0:T(8,128)} %bitcast.27), custom_call_target="tpu_custom_call" | custom-call | flops 1000 | bytes 1000 | tf_op jit(solution)/shard_map/pack/pallas_call | solution.py:213
  3.1 5.2 %all-to-all-start = ((bf16[8,32,128]{2,1,0:T(8,128)(2,1)}), bf16[8,32,128]{2,1,0:T(8,128)(2,1)S(1)}, u32[]{:S(2)}, u32[]{:S(2)}) async-start(bf16[8,32,128]{2,1,0:T(8,128)(2,1)} %get-tuple-element.14), calls=%async_computation | async-start | bytes 131072 | tf_op jit(solution)/shard_map/all_to_all | solution.py:230
  8.3 1.0 %copy-done.1 = bf16[256,1024]{1,0:T(8,128)(2,1)S(1)} copy-done((bf16[256,1024]{1,0:T(8,128)(2,1)S(1)}, bf16[256,1024]{1,0:T(8,128)(2,1)}, u32[]{:S(2)}) %copy-start.1) | copy-done | bytes 524312
  9.3 0.7 %copy-done.6 = s32[256,16]{0,1:T(8,128)S(1)} copy-done((s32[256,16]{0,1:T(8,128)S(1)}, s32[256,16]{0,1:T(8,128)}, u32[]{:S(2)}) %copy-start.6) | copy-done | bytes 16408
  10.1 1.3 %row_sums.1 = f32[16,72,256]{2,1,0:T(8,128)S(1)} custom-call(s32[1]{0:T(128)S(6)} %copy.12.valid, bf16[256,1024]{1,0:T(8,128)(2,1)S(1)} %copy-done.1, s32[16,256]{1,0:T(8,128)S(1)} %bitcast.28), custom_call_target="tpu_custom_call" | custom-call | flops 1000 | bytes 1000 | tf_op jit(solution)/shard_map/row_sums/pallas_call | solution.py:232
  11.4 2.0 %all-to-all-done.requests = bf16[8,32,128]{2,1,0:T(8,128)(2,1)S(1)} async-done(((bf16[8,32,128]{2,1,0:T(8,128)(2,1)}), bf16[8,32,128]{2,1,0:T(8,128)(2,1)S(1)}, u32[]{:S(2)}, u32[]{:S(2)}) %all-to-all-start) | async-done | bytes 65568 | tf_op jit(solution)/shard_map/all_to_all | solution.py:230
  14.0 8.5 %gather.1 = bf16[8,128,1024]{2,1,0:T(8,128)(2,1)} custom-call(bf16[8,32,128]{2,1,0:T(8,128)(2,1)} %copy-done.4, bf16[2048,1024]{1,0:T(8,128)(2,1)} %centres.1), custom_call_target="tpu_custom_call" | custom-call | flops 4294967296 | bytes 6291456 | tf_op jit(solution)/shard_map/gather/pallas_call | solution.py:251
  22.5 3.7 %all-to-all-start.1 = ((bf16[8,128,1024]{2,1,0:T(8,128)(2,1)}), bf16[8,128,1024]{2,1,0:T(8,128)(2,1)S(1)}, u32[]{:S(2)}, u32[]{:S(2)}) async-start(bf16[8,128,1024]{2,1,0:T(8,128)(2,1)} %gather.1), calls=%async_computation.1 | async-start | bytes 4194304 | tf_op jit(solution)/shard_map/all_to_all | solution.py:267
  26.3 1.6 %copy-done = bf16[8,128,1024]{2,1,0:T(8,128)(2,1)S(1)} copy-done((bf16[8,128,1024]{2,1,0:T(8,128)(2,1)S(1)}, bf16[8,128,1024]{2,1,0:T(8,128)(2,1)}, u32[]{:S(2)}) %copy-start) | copy-done | bytes 2097176
  27.9 4.3 %sums.1 = (f32[4,2,72,256]{3,2,1,0:T(8,128)S(1)}, f32[4,2,72,256]{3,2,1,0:T(8,128)S(1)}) custom-call(bf16[8,32,128]{2,1,0:T(8,128)(2,1)S(1)} %copy-done.5, bf16[1024,1024]{1,0:T(8,128)(2,1)S(1)} %bitcast.25, f32[16,72,256]{2,1,0:T(8,128)S(1)} %row_sums.1), custom_call_target="tpu_custom_call" | custom-call | flops 1000 | bytes 1000 | tf_op jit(solution)/shard_map/sums/pallas_call | solution.py:270
  32.7 1.6 %collective-permute-done = f32[4,2,72,256]{3,2,1,0:T(8,128)S(1)} collective-permute-done((f32[4,2,72,256]{3,2,1,0:T(8,128)S(1)}, f32[4,2,72,256]{3,2,1,0:T(8,128)S(1)}, u32[]{:S(2)}, u32[]{:S(2)}) %collective-permute-start) | collective-permute-done | bytes 589856 | tf_op jit(solution)/shard_map/ppermute | solution.py:186
  34.6 1.7 %collective-permute-start.1 = (bf16[2,72,256]{2,1,0:T(8,128)(2,1)S(1)}, bf16[2,72,256]{2,1,0:T(8,128)(2,1)S(1)}, u32[]{:S(2)}, u32[]{:S(2)}) collective-permute-start(bf16[2,72,256]{2,1,0:T(8,128)(2,1)S(1)} %get-tuple-element.28), channel_id=1, source_target_pairs={{0,1},{1,0},{2,3},{3,2},{4,5},{5,4},{6,7},{7,6},{8,9},{9,8},{10,11... | collective-permute-start | bytes 221192 | tf_op jit(solution)/shard_map/ppermute | solution.py:186
  36.2 2.6 %collective-permute-start.2 = (bf16[2,72,256]{2,1,0:T(8,128)(2,1)S(1)}, bf16[2,72,256]{2,1,0:T(8,128)(2,1)S(1)}, u32[]{:S(2)}, u32[]{:S(2)}) collective-permute-start(bf16[2,72,256]{2,1,0:T(8,128)(2,1)S(1)} %get-tuple-element.30), channel_id=1, source_target_pairs={{0,2},{1,3},{2,0},{3,1},{4,6},{5,7},{6,4},{7,5},{8,10},{9,11},{10,... | collective-permute-start | bytes 221192 | tf_op jit(solution)/shard_map/ppermute | solution.py:186
  39.1 0.9 %offsets.1 = f32[256,1024]{1,0:T(8,128)S(1)} custom-call(bf16[256,1024]{1,0:T(8,128)(2,1)S(1)} %copy-done.2, s32[16,256]{1,0:T(8,128)S(1)} %bitcast.29, f32[16,64,256]{2,1,0:T(8,128)S(1)} %bitcast.26), custom_call_target="tpu_custom_call" | custom-call | flops 1000 | bytes 1000 | tf_op jit(solution)/shard_map/offsets/pallas_call | solution.py:241
  40.0 5.2 %collective-permute-done.2 = bf16[2,72,256]{2,1,0:T(8,128)(2,1)S(1)} collective-permute-done((bf16[2,72,256]{2,1,0:T(8,128)(2,1)S(1)}, bf16[2,72,256]{2,1,0:T(8,128)(2,1)S(1)}, u32[]{:S(2)}, u32[]{:S(2)}) %collective-permute-start.2) | collective-permute-done | bytes 73760 | tf_op jit(solution)/shard_map/ppermute | solution.py:186
  45.3 1.8 %collective-permute-start.4 = (f32[2,72,256]{2,1,0:T(8,128)S(1)}, f32[2,72,256]{2,1,0:T(8,128)S(1)}, u32[]{:S(2)}, u32[]{:S(2)}) collective-permute-start(f32[2,72,256]{2,1,0:T(8,128)S(1)} %fusion), channel_id=1, source_target_pairs={{0,8},{4,12},{8,0},{12,4},{16,24},{20,28},{24,16},{28,20},{1,9},{5... | collective-permute-start | bytes 442376 | tf_op jit(solution)/shard_map/ppermute | solution.py:186
  47.1 1.5 %collective-permute-start.5 = (f32[2,72,256]{2,1,0:T(8,128)S(1)}, f32[2,72,256]{2,1,0:T(8,128)}, u32[]{:S(2)}, u32[]{:S(2)}) collective-permute-start(f32[2,72,256]{2,1,0:T(8,128)S(1)} %fusion), channel_id=1, source_target_pairs={{0,16},{4,20},{8,24},{12,28},{16,0},{20,4},{24,8},{28,12},{1,17},{... | collective-permute-start | bytes 442376 | tf_op jit(solution)/shard_map/ppermute | solution.py:186
  48.8 6.8 %collective-permute-done.4 = f32[2,72,256]{2,1,0:T(8,128)S(1)} collective-permute-done((f32[2,72,256]{2,1,0:T(8,128)S(1)}, f32[2,72,256]{2,1,0:T(8,128)S(1)}, u32[]{:S(2)}, u32[]{:S(2)}) %collective-permute-start.4) | collective-permute-done | bytes 147488 | tf_op jit(solution)/shard_map/ppermute | solution.py:186
  55.6 0.9 %collective-permute-done.5 = f32[2,72,256]{2,1,0:T(8,128)} collective-permute-done((f32[2,72,256]{2,1,0:T(8,128)S(1)}, f32[2,72,256]{2,1,0:T(8,128)}, u32[]{:S(2)}, u32[]{:S(2)}) %collective-permute-start.5) | collective-permute-done | bytes 147488 | tf_op jit(solution)/shard_map/ppermute | solution.py:186
  56.5 2.8 %collective-permute-done.6 = f32[2,72,256]{2,1,0:T(8,128)} collective-permute-done((f32[2,72,256]{2,1,0:T(8,128)S(1)}, f32[2,72,256]{2,1,0:T(8,128)}, u32[]{:S(2)}, u32[]{:S(2)}) %collective-permute-start.6) | collective-permute-done | bytes 147488 | tf_op jit(solution)/shard_map/ppermute | solution.py:186
  59.3 1.0 %add_add_fusion = f32[2,72,256]{2,1,0:T(8,128)S(1)} fusion(f32[2,72,256]{2,1,0:T(8,128)} %collective-permute-done.6, f32[2,72,256]{2,1,0:T(8,128)} %collective-permute-done.5, f32[2,72,256]{2,1,0:T(8,128)S(1)} %fusion, f32[2,72,256]{2,1,0:T(8,128)S(1)} %collective-permute-done.4), kind=kLoop, calls=%fused_computation.4 | loop fusion | flops 110592 | bytes 737280 | tf_op jit(solution)/shard_map/add | solution.py:292
  60.4 0.9 %fusion.1 = f32[2,64,256]{2,1,0:T(8,128)S(1)} fusion(f32[2,72,256]{2,1,0:T(8,128)S(1)} %add_add_fusion, f32[16,256,64]{1,2,0:T(8,128)} %param.13, s32[]{:T(128)S(6)} %select_n.33, f32[2,256]{1,0:T(2,128)S(1)} %bitcast.30), kind=kLoop, calls=%fused_computation.6 | loop fusion | flops 98304 | bytes 395268 | tf_op jit(solution)/shard_map/div | solution.py:297
  61.4 1.5 %errors.1 = f32[1,256]{1,0:T(1,128)} custom-call(s32[1]{0:T(128)S(6)} %copy.12.valid, s32[1,256]{1,0:T(1,128)S(1)} %copy-done.8, f32[256,1024]{1,0:T(8,128)S(1)} %offsets.1, bf16[1024,1024]{1,0:T(8,128)(2,1)S(1)} %bitcast.24), custom_call_target="tpu_custom_call" | custom-call | flops 1000 | bytes 1000 | tf_op jit(solution)/shard_map/errors/pallas_call | solution.py:302
  63.0 0.7 %maximum_bitcast_fusion = f32[4,256,64]{1,2,0:T(8,128)} fusion(f32[2,64,256]{2,1,0:T(8,128)S(1)} %get-tuple-element.32, f32[2,64,256]{2,1,0:T(8,128)S(1)} %get-tuple-element.31), kind=kLoop, calls=%fused_computation.1 | loop fusion | flops 65536 | bytes 524288 | tf_op jit(solution)/shard_map/transpose | solution.py:311
  (30 shorter events, 2.0 us)
Async XLA Ops:
  3.1 10.2 %all-to-all-start = ((bf16[8,32,128]{2,1,0:T(8,128)(2,1)}), bf16[8,32,128]{2,1,0:T(8,128)(2,1)S(1)}, u32[]{:S(2)}, u32[]{:S(2)}) async-start(bf16[8,32,128]{2,1,0:T(8,128)(2,1)} %get-tuple-element.14), calls=%async_computation | async-start | bytes 131072 | tf_op jit(solution)/shard_map/all_to_all | solution.py:230
  8.3 1.0 %copy-start.1 = (bf16[256,1024]{1,0:T(8,128)(2,1)S(1)}, bf16[256,1024]{1,0:T(8,128)(2,1)}, u32[]{:S(2)}) copy-start(bf16[256,1024]{1,0:T(8,128)(2,1)} %rows.3) | copy-start | bytes 1572868
  9.3 0.7 %copy-start.6 = (s32[256,16]{0,1:T(8,128)S(1)}, s32[256,16]{0,1:T(8,128)}, u32[]{:S(2)}) copy-start(s32[256,16]{0,1:T(8,128)} %param.10) | copy-start | bytes 49156
  13.3 0.6 copy-start.4
  22.5 3.8 %copy-start.5 = (bf16[8,32,128]{2,1,0:T(8,128)(2,1)S(1)}, bf16[8,32,128]{2,1,0:T(8,128)(2,1)}, u32[]{:S(2)}) copy-start(bf16[8,32,128]{2,1,0:T(8,128)(2,1)} %copy-done.4) | copy-start | bytes 196612
  22.5 36.8 %all-to-all-start.1 = ((bf16[8,128,1024]{2,1,0:T(8,128)(2,1)}), bf16[8,128,1024]{2,1,0:T(8,128)(2,1)S(1)}, u32[]{:S(2)}, u32[]{:S(2)}) async-start(bf16[8,128,1024]{2,1,0:T(8,128)(2,1)} %gather.1), calls=%async_computation.1 | async-start | bytes 4194304 | tf_op jit(solution)/shard_map/all_to_all | solution.py:267
  26.3 1.6 %copy-start = (bf16[8,128,1024]{2,1,0:T(8,128)(2,1)S(1)}, bf16[8,128,1024]{2,1,0:T(8,128)(2,1)}, u32[]{:S(2)}) copy-start(bf16[8,128,1024]{2,1,0:T(8,128)(2,1)} %gather.1) | copy-start | bytes 6291460
  32.2 6.9 %copy-start.2 = (bf16[256,1024]{1,0:T(8,128)(2,1)S(1)}, bf16[256,1024]{1,0:T(8,128)(2,1)}, u32[]{:S(2)}) copy-start(bf16[256,1024]{1,0:T(8,128)(2,1)} %rows.3) | copy-start | bytes 1572868
  32.2 6.8 %copy-start.3 = (f32[16,256,64]{1,2,0:T(8,128)S(1)}, f32[16,256,64]{1,2,0:T(8,128)}, u32[]{:S(2)}) copy-start(f32[16,256,64]{1,2,0:T(8,128)} %param.13) | copy-start | bytes 3145732
  32.2 6.8 %copy-start.7 = (s32[256,16]{0,1:T(8,128)S(1)}, s32[256,16]{0,1:T(8,128)}, u32[]{:S(2)}) copy-start(s32[256,16]{0,1:T(8,128)} %param.10) | copy-start | bytes 49156
  32.2 2.1 %collective-permute-start = (f32[4,2,72,256]{3,2,1,0:T(8,128)S(1)}, f32[4,2,72,256]{3,2,1,0:T(8,128)S(1)}, u32[]{:S(2)}, u32[]{:S(2)}) collective-permute-start(f32[4,2,72,256]{3,2,1,0:T(8,128)S(1)} %get-tuple-element.18), channel_id=1, source_target_pairs={{0,4},{4,0},{8,12},{12,8},{16,20},{20,16},{24,28},{28,24},{1,5},{5... | collective-permute-start | bytes 1769480 | tf_op jit(solution)/shard_map/ppermute | solution.py:186
  34.6 5.4 %collective-permute-start.1 = (bf16[2,72,256]{2,1,0:T(8,128)(2,1)S(1)}, bf16[2,72,256]{2,1,0:T(8,128)(2,1)S(1)}, u32[]{:S(2)}, u32[]{:S(2)}) collective-permute-start(bf16[2,72,256]{2,1,0:T(8,128)(2,1)S(1)} %get-tuple-element.28), channel_id=1, source_target_pairs={{0,1},{1,0},{2,3},{3,2},{4,5},{5,4},{6,7},{7,6},{8,9},{9,8},{10,11... | collective-permute-start | bytes 221192 | tf_op jit(solution)/shard_map/ppermute | solution.py:186
  36.2 9.0 %collective-permute-start.2 = (bf16[2,72,256]{2,1,0:T(8,128)(2,1)S(1)}, bf16[2,72,256]{2,1,0:T(8,128)(2,1)S(1)}, u32[]{:S(2)}, u32[]{:S(2)}) collective-permute-start(bf16[2,72,256]{2,1,0:T(8,128)(2,1)S(1)} %get-tuple-element.30), channel_id=1, source_target_pairs={{0,2},{1,3},{2,0},{3,1},{4,6},{5,7},{6,4},{7,5},{8,10},{9,11},{10,... | collective-permute-start | bytes 221192 | tf_op jit(solution)/shard_map/ppermute | solution.py:186
  38.8 6.4 %collective-permute-start.3 = (bf16[2,72,256]{2,1,0:T(8,128)(2,1)S(1)}, bf16[2,72,256]{2,1,0:T(8,128)(2,1)S(1)}, u32[]{:S(2)}, u32[]{:S(2)}) collective-permute-start(bf16[2,72,256]{2,1,0:T(8,128)(2,1)S(1)} %get-tuple-element.29), channel_id=1, source_target_pairs={{0,3},{1,2},{2,1},{3,0},{4,7},{5,6},{6,5},{7,4},{8,11},{9,10},{10,... | collective-permute-start | bytes 221192 | tf_op jit(solution)/shard_map/ppermute | solution.py:186
  39.1 22.3 %copy-start.8 = (s32[1,256]{1,0:T(1,128)S(1)}, s32[1,256]{1,0:T(1,128)}, u32[]{:S(2)}) copy-start(s32[1,256]{1,0:T(1,128)} %get-tuple-element.23.position) | copy-start | bytes 3076
  45.3 10.3 %collective-permute-start.4 = (f32[2,72,256]{2,1,0:T(8,128)S(1)}, f32[2,72,256]{2,1,0:T(8,128)S(1)}, u32[]{:S(2)}, u32[]{:S(2)}) collective-permute-start(f32[2,72,256]{2,1,0:T(8,128)S(1)} %fusion), channel_id=1, source_target_pairs={{0,8},{4,12},{8,0},{12,4},{16,24},{20,28},{24,16},{28,20},{1,9},{5... | collective-permute-start | bytes 442376 | tf_op jit(solution)/shard_map/ppermute | solution.py:186
  47.1 9.4 %collective-permute-start.5 = (f32[2,72,256]{2,1,0:T(8,128)S(1)}, f32[2,72,256]{2,1,0:T(8,128)}, u32[]{:S(2)}, u32[]{:S(2)}) collective-permute-start(f32[2,72,256]{2,1,0:T(8,128)S(1)} %fusion), channel_id=1, source_target_pairs={{0,16},{4,20},{8,24},{12,28},{16,0},{20,4},{24,8},{28,12},{1,17},{... | collective-permute-start | bytes 442376 | tf_op jit(solution)/shard_map/ppermute | solution.py:186
  48.6 10.7 %collective-permute-start.6 = (f32[2,72,256]{2,1,0:T(8,128)S(1)}, f32[2,72,256]{2,1,0:T(8,128)}, u32[]{:S(2)}, u32[]{:S(2)}) collective-permute-start(f32[2,72,256]{2,1,0:T(8,128)S(1)} %fusion), channel_id=1, source_target_pairs={{0,24},{4,28},{8,16},{12,20},{16,8},{20,12},{24,0},{28,4},{1,25},{... | collective-permute-start | bytes 442376 | tf_op jit(solution)/shard_map/ppermute | solution.py:186
  61.3 1.6 %collective-permute-start.7 = (f32[2,64,256]{2,1,0:T(8,128)S(1)}, f32[2,64,256]{2,1,0:T(8,128)S(1)}, u32[]{:S(2)}, u32[]{:S(2)}) collective-permute-start(f32[2,64,256]{2,1,0:T(8,128)S(1)} %fusion.1), channel_id=1, source_target_pairs={{0,4},{4,0},{8,12},{12,8},{16,20},{20,16},{24,28},{28,24},{1,5},{5... | collective-permute-start | bytes 393224 | tf_op jit(solution)/shard_map/ppermute | solution.py:186

commit v4 on v3

--- a/solution.py
+++ b/solution.py
@@ -10,7 +10,7 @@
 prior_weight = 4.0
 F32, BF16, I32 = jnp.float32, jnp.bfloat16, jnp.int32
 VMEM = pl.BlockSpec(memory_space=pltpu.VMEM)
-ANY = pl.BlockSpec(memory_space=pl.ANY)
+HBM = pl.BlockSpec(memory_space=pltpu.HBM)
 SMEM = pl.BlockSpec(memory_space=pltpu.SMEM)
 NT = (((1,), (1,)), ((), ()))
 extra = 16
@@ -104,32 +104,33 @@
             pl.when(mine != at // half)(functools.partial(store, send))
 
 
-def gather_kernel(subs, requests, centres, pieces, near, hit, found, read, written):
+def gather_kernel(subs, requests, centres, pieces, near, found, loaded, written):
     owners, _, capacity = requests.shape
-    slots, lists = hit.shape
-    loads = []
-    for part in range(read.shape[0]):
-        rows = pl.ds(part * (lists // read.shape[0]), lists // read.shape[0])
-        loads.append(pltpu.make_async_copy(centres.at[rows], near.at[rows], read.at[part]))
+    lists = centres.shape[0]
+    parts, chunks = loaded.shape[0], written.shape[0]
+    chunk = owners // chunks
+    span = chunk * capacity
+    loads, stores = [], []
+    for part in range(parts):
+        rows = pl.ds(part * (lists // parts), lists // parts)
+        loads.append(pltpu.make_async_copy(centres.at[rows], near.at[rows], loaded.at[part]))
         loads[-1].start()
-    chunk = 4
-    span = chunk * capacity
-    for first in range(0, owners, chunk):
-        asked = jnp.concatenate([requests[first + j] for j in range(chunk)], axis=1)
+    for index in range(chunks):
+        asked = jnp.concatenate([requests[index * chunk + j] for j in range(chunk)], axis=1)
         turned = asked.astype(F32).T.astype(I32)
         high, low = (turned[:, subs + i : subs + i + 1] for i in range(2))
         low_hit = mask_bf16(lax.broadcasted_iota(I32, (span, 256), 1) == low)
-        for h in range(lists // 256):
-            hit[first * capacity : first * capacity + span, h * 256 : (h + 1) * 256] = (
-                low_hit * mask_bf16(high == h)
+        total = jnp.zeros((span, centres.shape[1]), F32)
+        for part in range(parts):
+            first, last = part * (lists // parts), (part + 1) * (lists // parts)
+            hit = jnp.concatenate(
+                [low_hit * mask_bf16(high == h) for h in range(first // 256, last // 256)], axis=1
             )
-    for load in loads:
-        load.wait()
-    stores = []
-    for index in range(owners // chunk):
-        part = dot(hit[index * span : (index + 1) * span], near[...]).astype(BF16)
-        found[index * chunk : (index + 1) * chunk] = part.reshape((chunk, *found.shape[1:]))
+            if index == 0:
+                loads[part].wait()
+            total += dot(hit, near[first:last])
         block = pl.ds(index * chunk, chunk)
+        found[block] = total.astype(BF16).reshape((chunk, *found.shape[1:]))
         stores.append(
             pltpu.make_async_copy(found.at[block], pieces.at[block], written.at[index])
         )
@@ -181,6 +182,22 @@
     out[...] = jnp.where(lane < valid[0], error, 0.0)
 
 
+def encode_kernel(width_sub, *refs):
+    parts, out = refs[:-1], refs[-1]
+    half, padded, code_count = out.shape
+    which = lax.broadcasted_iota(I32, (padded - width_sub, code_count), 0)
+    for m in range(half):
+        total = parts[0][m]
+        for part in parts[1:]:
+            total += part[m].astype(F32)
+        sums, counts = total[:width_sub], total[width_sub:]
+        top = jnp.max(jnp.abs(sums), axis=0, keepdims=True)
+        exponent = jnp.clip(jnp.ceil(jnp.log2(top)) - 1.0, -125.0, 127.0)
+        scaled = jnp.clip(jnp.round(sums / jnp.exp2(exponent) * 16384.0), -32767.0, 32767.0)
+        tail = jnp.where(which < 2, counts, jnp.where(which == 2, exponent, 0.0))
+        out[m] = jnp.concatenate([scaled, tail], axis=0).astype(I32).astype(jnp.int16)
+
+
 def swap(array, axis, step):
     count = lax.axis_size(axis)
     return lax.ppermute(array, axis, [(i, i ^ step) for i in range(count)])
@@ -234,8 +251,8 @@
         in_specs=[SMEM] + [VMEM] * 2,
         out_specs=VMEM,
         out_shape=struct(subs, padded, code_count),
-        compiler_params=params(40),
-        cost_estimate=cost(1000, 1000),
+        compiler_params=params(24),
+        cost_estimate=cost(8 << 30, 16 << 20),
         name="row_sums",
     )(valid_rows, memory_rows, codes)
     offsets = pl.pallas_call(
@@ -250,17 +267,16 @@
     requests, row_sums = lax.optimization_barrier((requests, row_sums))
     gathered = pl.pallas_call(
         functools.partial(gather_kernel, subs),
-        in_specs=[VMEM, ANY],
-        out_specs=ANY,
+        in_specs=[VMEM, HBM],
+        out_specs=HBM,
         out_shape=struct(owners, capacity, width, dtype=BF16),
         scratch_shapes=[
             pltpu.VMEM((lists, width), BF16),
-            pltpu.VMEM((owners * capacity, lists), BF16),
             pltpu.VMEM((owners, capacity, width), BF16),
-            pltpu.SemaphoreType.DMA((8,)),
-            pltpu.SemaphoreType.DMA((owners // 4,)),
+            pltpu.SemaphoreType.DMA((4,)),
+            pltpu.SemaphoreType.DMA((2,)),
         ],
-        compiler_params=params(60),
+        compiler_params=params(57),
         cost_estimate=cost(4 << 30, 6 << 20),
         name="gather",
     )(requests, centroids)
@@ -272,7 +288,7 @@
         in_specs=[VMEM] * 3,
         out_specs=[VMEM] * 2,
         out_shape=[half_shape] * 2,
-        compiler_params=params(40),
+        compiler_params=params(20),
         cost_estimate=cost(1000, 1000),
         name="sums",
     )(requests, gathered.reshape(owners * capacity, width), row_sums)
@@ -283,22 +299,18 @@
     own = jnp.where(
         row < width_sub, own, jnp.where(row == width_sub, high, own - 256.0 * high)
     )
-    own = own[0] + sum(
-        swap(own[s].astype(BF16), "rep", s).astype(F32) for s in range(1, replicas)
-    )
+    parts = [own[0]] + [swap(own[s].astype(BF16), "rep", s) for s in range(1, replicas)]
+    own = pl.pallas_call(
+        functools.partial(encode_kernel, width_sub),
+        in_specs=[VMEM] * replicas,
+        out_specs=VMEM,
+        out_shape=struct(half, padded, code_count, dtype=jnp.int16),
+        compiler_params=params(20),
+        cost_estimate=cost(1000, 1000),
+        name="encode",
+    )(*parts)
     own, offsets = lax.optimization_barrier((own, offsets))
     others = [swap(own, "list", s) for s in range(2, owners, 2)]
-    pieces, *others = lax.optimization_barrier((pieces, *others))
-    own = functools.reduce(jnp.add, others, own)
-    core = lax.axis_index("list") % 2
-    start = lax.axis_index("rep") * group_subs + core * half
-    prior = prior_weight * lax.dynamic_slice_in_dim(book, start, half, 0)
-    counts = 256.0 * own[:, width_sub : width_sub + 1] + own[:, width_sub + 1 : width_sub + 2]
-    own = (own[:, :width_sub] + prior) / (counts + prior_weight)
-    other = swap(own, "list", 1)
-    new_codebook = jnp.concatenate(
-        [jnp.where(core == 0, own, other), jnp.where(core == 0, other, own)], axis=0
-    )
     row_error = pl.pallas_call(
         error_kernel,
         in_specs=[SMEM] + [VMEM] * 3,
@@ -308,6 +320,32 @@
         cost_estimate=cost(1000, 1000),
         name="errors",
     )(valid_rows, position, offsets, pieces.reshape(owners * capacity, width))
+    row_error, *others = lax.optimization_barrier((row_error, *others))
+    core = lax.axis_index("list") % 2
+    start = lax.axis_index("rep") * group_subs + core * half
+    prior = prior_weight * lax.dynamic_slice_in_dim(book, start, half, 0)
+    parts = [part.astype(F32) for part in (own, *others)]
+    parts = [
+        jnp.where(
+            lax.broadcasted_iota(I32, part.shape, 1) < width_sub,
+            part * (jnp.exp2(part[:, width_sub + 2 : width_sub + 3]) / 16384.0),
+            part,
+        )
+        for part in parts
+    ]
+    sums, high, low = (
+        functools.reduce(jnp.add, [part[:, first:last] for part in parts])
+        for first, last in (
+            (0, width_sub),
+            (width_sub, width_sub + 1),
+            (width_sub + 1, width_sub + 2),
+        )
+    )
+    own = (sums + prior) / (256.0 * high + low + prior_weight)
+    other = swap(own, "list", 1)
+    new_codebook = jnp.concatenate(
+        [jnp.where(core == 0, own, other), jnp.where(core == 0, other, own)], axis=0
+    )
     return (jnp.transpose(new_codebook, (0, 2, 1)), row_error.reshape(row_count))
 
 

time: 64.3 us -> 59.9 us (0.932)
  waiting for transfers between devices: 19.3 us -> 13.4 us
    ppermute x8, waiting for transfers between devices: 17.3 us -> 9.56 us  [swap(): return lax.ppermute(array, axis, [(i, i ^ step) for i in range(count)])]
    all_to_all x1, waiting for transfers between devices: 0.01 us -> 1.93 us  [body(): pieces = lax.all_to_all(gathered, 'list', 0, 0, tiled=True)]
    another operation x1, other arithmetic: 0.22 us -> 1.45 us
    add x3 -> x1, other arithmetic: 1.07 us -> 0.02 us  [body(): own = (sums + prior) / (256.0 * high + low + prior_weight)]
    pallas_call x1, Pallas kernels: 4.31 us -> 5.33 us  [body(): pl.pallas_call(functools.partial(sums_kernel, replicas), in_specs=[VMEM]...]
    pallas_call x1 -> x2, Pallas kernels: 8.53 us -> 8.1 us  [the longest x1 8.02 us: body(): pl.pallas_call(functools.partial(gather_kernel, subs), in_specs=[VMEM, HB...]
    unnamed x19 -> x25, local copies, waits for them, and re-layouts: 4.03 us -> 4.44 us
  transfers between devices with their start and end apart: 10 -> 10, of which waited for: 6 -> 7; matrix products, arithmetic and copies ran while one was open for 0% -> 3% of each run, Pallas kernels for 13% -> 15%
where the time goes in v4:
time: 59.9 us; the launch traced here: 59.4 us
  Pallas kernels  19 us (32%)
  starting transfers between devices  17.4 us (29%)
  waiting for transfers between devices  13.4 us (22%)
  local copies, waits for them, and re-layouts  4.46 us (7%)
  other arithmetic  3.46 us (6%)
  between operations  1.53 us (3%)
    ppermute x8, waiting for transfers between devices, swap(): return lax.ppermute(array, axis, [(i, i ^ step) for i in range(count)])  9.56 us
    ppermute x8, starting transfers between devices, swap(): return lax.ppermute(array, axis, [(i, i ^ step) for i in range(count)])  8.5 us
    pallas_call x1, Pallas kernels, body(): pl.pallas_call(functools.partial(gather_kernel, subs), in_specs=[VMEM, HB...  8.02 us
    pallas_call x1, Pallas kernels, body(): pl.pallas_call(functools.partial(sums_kernel, replicas), in_specs=[VMEM]...  5.33 us
    all_to_all x1, starting transfers between devices, body(): requests = lax.all_to_all(requests, 'list', 0, 0, tiled=True)  5.17 us
    unnamed x25, local copies, waits for them, and re-layouts  4.44 us
    all_to_all x1, starting transfers between devices, body(): pieces = lax.all_to_all(gathered, 'list', 0, 0, tiled=True)  3.75 us
    all_to_all x1, waiting for transfers between devices, body(): requests = lax.all_to_all(requests, 'list', 0, 0, tiled=True)  1.96 us
  transfers between devices with their start and end apart: 10, of which 7 were waited for; matrix products, arithmetic and copies ran while one was open for 3% of the time, Pallas kernels for 15%

profile of v4, /device:TPU:0, one launch (start us, length us, event | category | flops | bytes accessed | tf_op | source)
XLA Modules:
  0.0 59.4 jit_solution(15669067743085386671)
XLA Ops:
  1.3 1.9 %pack.1 = (bf16[8,32,128]{2,1,0:T(8,128)(2,1)}, s32[1,256]{1,0:T(1,128)}) custom-call(s32[1]{0:T(128)S(6)} %copy.24.valid, s32[1,256]{1,0:T(1,128)} %bitcast.46, s32[1,256]{1,0:T(1,128)} %bitcast.47, s32[16,256]{1,0:T(8,128)} %bitcast.37), custom_call_target="tpu_custom_call" | custom-call | flops 1000 | bytes 1000 | tf_op jit(solution)/shard_map/pack/pallas_call | solution.py:230
  3.1 5.2 %all-to-all-start = ((bf16[8,32,128]{2,1,0:T(8,128)(2,1)}), bf16[8,32,128]{2,1,0:T(8,128)(2,1)S(1)}, u32[]{:S(2)}, u32[]{:S(2)}) async-start(bf16[8,32,128]{2,1,0:T(8,128)(2,1)} %get-tuple-element.14), calls=%async_computation | async-start | bytes 131072 | tf_op jit(solution)/shard_map/all_to_all | solution.py:247
  8.3 1.0 %copy-done.3 = bf16[256,1024]{1,0:T(8,128)(2,1)S(1)} copy-done((bf16[256,1024]{1,0:T(8,128)(2,1)S(1)}, bf16[256,1024]{1,0:T(8,128)(2,1)}, u32[]{:S(2)}) %copy-start.3) | copy-done | bytes 524312
  9.3 0.7 %copy-done.7 = s32[256,16]{0,1:T(8,128)S(1)} copy-done((s32[256,16]{0,1:T(8,128)S(1)}, s32[256,16]{0,1:T(8,128)}, u32[]{:S(2)}) %copy-start.7) | copy-done | bytes 16408
  10.1 1.3 %row_sums.1 = f32[16,72,256]{2,1,0:T(8,128)S(1)} custom-call(s32[1]{0:T(128)S(6)} %copy.24.valid, bf16[256,1024]{1,0:T(8,128)(2,1)S(1)} %copy-done.3, s32[16,256]{1,0:T(8,128)S(1)} %bitcast.38), custom_call_target="tpu_custom_call" | custom-call | flops 8589934592 | bytes 16777216 | tf_op jit(solution)/shard_map/row_sums/pallas_call | solution.py:249
  11.4 2.0 %all-to-all-done.requests = bf16[8,32,128]{2,1,0:T(8,128)(2,1)S(1)} async-done(((bf16[8,32,128]{2,1,0:T(8,128)(2,1)}), bf16[8,32,128]{2,1,0:T(8,128)(2,1)S(1)}, u32[]{:S(2)}, u32[]{:S(2)}) %all-to-all-start) | async-done | bytes 65568 | tf_op jit(solution)/shard_map/all_to_all | solution.py:247
  13.3 0.6 %copy-done.5 = bf16[8,32,128]{2,1,0:T(8,128)(2,1)} copy-done((bf16[8,32,128]{2,1,0:T(8,128)(2,1)}, bf16[8,32,128]{2,1,0:T(8,128)(2,1)S(1)}, u32[]{:S(2)}) %copy-start.5) | copy-done | bytes 65560
  14.0 8.0 %gather.1 = bf16[8,128,1024]{2,1,0:T(8,128)(2,1)} custom-call(bf16[8,32,128]{2,1,0:T(8,128)(2,1)} %copy-done.5, bf16[2048,1024]{1,0:T(8,128)(2,1)} %centres.1), custom_call_target="tpu_custom_call" | custom-call | flops 4294967296 | bytes 6291456 | tf_op jit(solution)/shard_map/gather/pallas_call | solution.py:268
  22.0 3.7 %all-to-all-start.1 = ((bf16[8,128,1024]{2,1,0:T(8,128)(2,1)}), bf16[8,128,1024]{2,1,0:T(8,128)(2,1)S(1)}, u32[]{:S(2)}, u32[]{:S(2)}) async-start(bf16[8,128,1024]{2,1,0:T(8,128)(2,1)} %gather.1), calls=%async_computation.1 | async-start | bytes 4194304 | tf_op jit(solution)/shard_map/all_to_all | solution.py:283
  25.8 1.6 %copy-done = bf16[8,128,1024]{2,1,0:T(8,128)(2,1)S(1)} copy-done((bf16[8,128,1024]{2,1,0:T(8,128)(2,1)S(1)}, bf16[8,128,1024]{2,1,0:T(8,128)(2,1)}, u32[]{:S(2)}) %copy-start) | copy-done | bytes 2097176
  27.4 5.3 %sums.1 = (f32[4,2,72,256]{3,2,1,0:T(8,128)S(1)}, f32[4,2,72,256]{3,2,1,0:T(8,128)}) custom-call(bf16[8,32,128]{2,1,0:T(8,128)(2,1)S(1)} %copy-done.6, bf16[1024,1024]{1,0:T(8,128)(2,1)S(1)} %bitcast.35, f32[16,72,256]{2,1,0:T(8,128)S(1)} %row_sums.1), custom_call_target="tpu_custom_call" | custom-call | flops 1000 | bytes 1000 | tf_op jit(solution)/shard_map/sums/pallas_call | solution.py:286
  33.5 0.9 %offsets.1 = f32[256,1024]{1,0:T(8,128)S(1)} custom-call(bf16[256,1024]{1,0:T(8,128)(2,1)S(1)} %copy-done.4, s32[16,256]{1,0:T(8,128)S(1)} %bitcast.39, f32[16,64,256]{2,1,0:T(8,128)S(1)} %bitcast.36), custom_call_target="tpu_custom_call" | custom-call | flops 1000 | bytes 1000 | tf_op jit(solution)/shard_map/offsets/pallas_call | solution.py:258
  35.1 1.4 %fusion.13 = (bf16[4,2,72,256]{3,2,1,0:T(8,128)(2,1)S(1)}, f32[4,2,72,256]{3,2,1,0:T(8,128)S(1)}) fusion(pred[72]{0:T(512)(128)(4,1)S(1)} %get-tuple-element.37, f32[4,2,72,256]{3,2,1,0:T(8,128)} %copy-done.2, f32[4,2,72,256]{3,2,1,0:T(8,128)} %collective-permute-done, pred[72]{0:T(512)(128)(4,1)S(1)} %get-tuple-element.38), kind=kLoop, calls=%fused_computation.45 | loop fusion | flops 1179648 | bytes 2064528 | tf_op jit(solution)/shard_map/convert.2
  36.6 1.6 %collective-permute-start.1 = (bf16[2,72,256]{2,1,0:T(8,128)(2,1)S(1)}, bf16[2,72,256]{2,1,0:T(8,128)(2,1)S(1)}, u32[]{:S(2)}, u32[]{:S(2)}) collective-permute-start(bf16[2,72,256]{2,1,0:T(8,128)(2,1)S(1)} %get-tuple-element.30), channel_id=1, source_target_pairs={{0,1},{1,0},{2,3},{3,2},{4,5},{5,4},{6,7},{7,6},{8,9},{9,8},{10,11... | collective-permute-start | bytes 221192 | tf_op jit(solution)/shard_map/ppermute | solution.py:203
  38.2 2.6 %collective-permute-start.2 = (bf16[2,72,256]{2,1,0:T(8,128)(2,1)S(1)}, bf16[2,72,256]{2,1,0:T(8,128)(2,1)S(1)}, u32[]{:S(2)}, u32[]{:S(2)}) collective-permute-start(bf16[2,72,256]{2,1,0:T(8,128)(2,1)S(1)} %get-tuple-element.29), channel_id=1, source_target_pairs={{0,2},{1,3},{2,0},{3,1},{4,6},{5,7},{6,4},{7,5},{8,10},{9,11},{10,... | collective-permute-start | bytes 221192 | tf_op jit(solution)/shard_map/ppermute | solution.py:203
  41.2 6.0 %collective-permute-done.2.refs_2_ = bf16[2,72,256]{2,1,0:T(8,128)(2,1)S(1)} collective-permute-done((bf16[2,72,256]{2,1,0:T(8,128)(2,1)S(1)}, bf16[2,72,256]{2,1,0:T(8,128)(2,1)S(1)}, u32[]{:S(2)}, u32[]{:S(2)}) %collective-permute-start.2) | collective-permute-done | bytes 73760 | tf_op jit(solution)/shard_map/ppermute | solution.py:203
  47.3 1.8 %collective-permute-start.4 = (s16[2,72,256]{2,1,0:T(8,128)(2,1)S(1)}, s16[2,72,256]{2,1,0:T(8,128)(2,1)S(1)}, u32[]{:S(2)}, u32[]{:S(2)}) collective-permute-start(s16[2,72,256]{2,1,0:T(8,128)(2,1)S(1)} %encode.1), channel_id=1, source_target_pairs={{0,8},{4,12},{8,0},{12,4},{16,24},{20,28},{24,16},{28,20},{1,9},{5... | collective-permute-start | bytes 221192 | tf_op jit(solution)/shard_map/ppermute | solution.py:203
  49.1 1.5 %collective-permute-start.5 = (s16[2,72,256]{2,1,0:T(8,128)(2,1)S(1)}, s16[2,72,256]{2,1,0:T(8,128)(2,1)S(1)}, u32[]{:S(2)}, u32[]{:S(2)}) collective-permute-start(s16[2,72,256]{2,1,0:T(8,128)(2,1)S(1)} %encode.1), channel_id=1, source_target_pairs={{0,16},{4,20},{8,24},{12,28},{16,0},{20,4},{24,8},{28,12},{1,17},{... | collective-permute-start | bytes 221192 | tf_op jit(solution)/shard_map/ppermute | solution.py:203
  50.9 1.9 %all-to-all-done.1 = bf16[8,128,1024]{2,1,0:T(8,128)(2,1)S(1)} async-done(((bf16[8,128,1024]{2,1,0:T(8,128)(2,1)}), bf16[8,128,1024]{2,1,0:T(8,128)(2,1)S(1)}, u32[]{:S(2)}, u32[]{:S(2)}) %all-to-all-start.1) | async-done | bytes 2097184 | tf_op jit(solution)/shard_map/all_to_all | solution.py:283
  52.8 1.5 %errors.1 = f32[1,256]{1,0:T(1,128)} custom-call(s32[1]{0:T(128)S(6)} %copy.24.valid, s32[1,256]{1,0:T(1,128)S(1)} %copy-done.9, f32[256,1024]{1,0:T(8,128)S(1)} %offsets.1, bf16[1024,1024]{1,0:T(8,128)(2,1)S(1)} %bitcast.34), custom_call_target="tpu_custom_call" | custom-call | flops 1000 | bytes 1000 | tf_op jit(solution)/shard_map/errors/pallas_call | solution.py:314
  54.4 1.5 %collective-permute-done.6 = s16[2,72,256]{2,1,0:T(8,128)(2,1)S(1)} collective-permute-done((s16[2,72,256]{2,1,0:T(8,128)(2,1)S(1)}, s16[2,72,256]{2,1,0:T(8,128)(2,1)S(1)}, u32[]{:S(2)}, u32[]{:S(2)}) %collective-permute-start.6) | collective-permute-done | bytes 73760 | tf_op jit(solution)/shard_map/ppermute | solution.py:203
  56.2 1.0 %fusion.1 = f32[2,64,256]{2,1,0:T(8,128)S(1)} fusion(f32[2,72,256]{2,1,0:T(8,128)S(1)} %get-tuple-element.36, f32[2,72,256]{2,1,0:T(8,128)S(1)} %get-tuple-element.35, f32[2,72,256]{2,1,0:T(8,128)S(1)} %get-tuple-element.34, f32[2,72,256]{2,1,0:T(8,128)S(1)} %get-tuple-element.33, f32[16,256,64]{1,2,0:T(8,128)} %param.13, s32[]{:T(128)S(6)} %select_n.50, ...), kind=kLoop, calls=%fused_computation.9 | loop fusion | flops 196608 | bytes 788484 | tf_op jit(solution)/shard_map/div | solution.py:344
  57.3 1.3 %collective-permute-done.7 = f32[2,64,256]{2,1,0:T(8,128)S(1)} collective-permute-done((f32[2,64,256]{2,1,0:T(8,128)S(1)}, f32[2,64,256]{2,1,0:T(8,128)S(1)}, u32[]{:S(2)}, u32[]{:S(2)}) %collective-permute-start.7) | collective-permute-done | bytes 131104 | tf_op jit(solution)/shard_map/ppermute | solution.py:203
  58.6 0.7 %maximum_bitcast_fusion = f32[4,256,64]{1,2,0:T(8,128)} fusion(f32[2,64,256]{2,1,0:T(8,128)S(1)} %get-tuple-element.32, f32[2,64,256]{2,1,0:T(8,128)S(1)} %get-tuple-element.31), kind=kLoop, calls=%fused_computation.1 | loop fusion | flops 65536 | bytes 524288 | tf_op jit(solution)/shard_map/transpose | solution.py:349
  (45 shorter events, 2.6 us)
Async XLA Ops:
  3.1 10.2 %all-to-all-start = ((bf16[8,32,128]{2,1,0:T(8,128)(2,1)}), bf16[8,32,128]{2,1,0:T(8,128)(2,1)S(1)}, u32[]{:S(2)}, u32[]{:S(2)}) async-start(bf16[8,32,128]{2,1,0:T(8,128)(2,1)} %get-tuple-element.14), calls=%async_computation | async-start | bytes 131072 | tf_op jit(solution)/shard_map/all_to_all | solution.py:247
  8.3 1.0 %copy-start.3 = (bf16[256,1024]{1,0:T(8,128)(2,1)S(1)}, bf16[256,1024]{1,0:T(8,128)(2,1)}, u32[]{:S(2)}) copy-start(bf16[256,1024]{1,0:T(8,128)(2,1)} %rows.3) | copy-start | bytes 1572868
  9.3 0.7 %copy-start.7 = (s32[256,16]{0,1:T(8,128)S(1)}, s32[256,16]{0,1:T(8,128)}, u32[]{:S(2)}) copy-start(s32[256,16]{0,1:T(8,128)} %param.10) | copy-start | bytes 49156
  13.3 0.6 %copy-start.5 = (bf16[8,32,128]{2,1,0:T(8,128)(2,1)}, bf16[8,32,128]{2,1,0:T(8,128)(2,1)S(1)}, u32[]{:S(2)}) copy-start(bf16[8,32,128]{2,1,0:T(8,128)(2,1)S(1)} %all-to-all-done.requests) | copy-start | bytes 196612
  22.0 3.8 %copy-start.6 = (bf16[8,32,128]{2,1,0:T(8,128)(2,1)S(1)}, bf16[8,32,128]{2,1,0:T(8,128)(2,1)}, u32[]{:S(2)}) copy-start(bf16[8,32,128]{2,1,0:T(8,128)(2,1)} %copy-done.5) | copy-start | bytes 196612
  22.0 30.8 %all-to-all-start.1 = ((bf16[8,128,1024]{2,1,0:T(8,128)(2,1)}), bf16[8,128,1024]{2,1,0:T(8,128)(2,1)S(1)}, u32[]{:S(2)}, u32[]{:S(2)}) async-start(bf16[8,128,1024]{2,1,0:T(8,128)(2,1)} %gather.1), calls=%async_computation.1 | async-start | bytes 4194304 | tf_op jit(solution)/shard_map/all_to_all | solution.py:283
  25.8 1.6 %copy-start = (bf16[8,128,1024]{2,1,0:T(8,128)(2,1)S(1)}, bf16[8,128,1024]{2,1,0:T(8,128)(2,1)}, u32[]{:S(2)}) copy-start(bf16[8,128,1024]{2,1,0:T(8,128)(2,1)} %gather.1) | copy-start | bytes 6291460
  27.4 6.1 %copy-start.1 = (f32[16,256,64]{1,2,0:T(8,128)S(1)}, f32[16,256,64]{1,2,0:T(8,128)}, u32[]{:S(2)}) copy-start(f32[16,256,64]{1,2,0:T(8,128)} %param.13) | copy-start | bytes 3145732
  27.4 6.1 %copy-start.4 = (bf16[256,1024]{1,0:T(8,128)(2,1)S(1)}, bf16[256,1024]{1,0:T(8,128)(2,1)}, u32[]{:S(2)}) copy-start(bf16[256,1024]{1,0:T(8,128)(2,1)} %rows.3) | copy-start | bytes 1572868
  27.4 6.1 %copy-start.8 = (s32[256,16]{0,1:T(8,128)S(1)}, s32[256,16]{0,1:T(8,128)}, u32[]{:S(2)}) copy-start(s32[256,16]{0,1:T(8,128)} %param.10) | copy-start | bytes 49156
  32.7 0.8 %copy-start.2 = (f32[4,2,72,256]{3,2,1,0:T(8,128)}, f32[4,2,72,256]{3,2,1,0:T(8,128)S(1)}, u32[]{:S(2)}) copy-start(f32[4,2,72,256]{3,2,1,0:T(8,128)S(1)} %get-tuple-element.17) | copy-start | bytes 1769476
  32.7 2.4 %collective-permute-start = (f32[4,2,72,256]{3,2,1,0:T(8,128)}, f32[4,2,72,256]{3,2,1,0:T(8,128)}, u32[]{:S(2)}, u32[]{:S(2)}) collective-permute-start(f32[4,2,72,256]{3,2,1,0:T(8,128)} %get-tuple-element.18), channel_id=1, source_target_pairs={{0,4},{4,0},{8,12},{12,8},{16,20},{20,16},{24,28},{28,24},{1,5},{5... | collective-permute-start | bytes 1769480 | tf_op jit(solution)/shard_map/ppermute | solution.py:203
  34.5 18.4 %copy-start.9 = (s32[1,256]{1,0:T(1,128)S(1)}, s32[1,256]{1,0:T(1,128)}, u32[]{:S(2)}) copy-start(s32[1,256]{1,0:T(1,128)} %get-tuple-element.20.position) | copy-start | bytes 3076
  36.6 4.6 %collective-permute-start.1 = (bf16[2,72,256]{2,1,0:T(8,128)(2,1)S(1)}, bf16[2,72,256]{2,1,0:T(8,128)(2,1)S(1)}, u32[]{:S(2)}, u32[]{:S(2)}) collective-permute-start(bf16[2,72,256]{2,1,0:T(8,128)(2,1)S(1)} %get-tuple-element.30), channel_id=1, source_target_pairs={{0,1},{1,0},{2,3},{3,2},{4,5},{5,4},{6,7},{7,6},{8,9},{9,8},{10,11... | collective-permute-start | bytes 221192 | tf_op jit(solution)/shard_map/ppermute | solution.py:203
  38.2 9.0 %collective-permute-start.2 = (bf16[2,72,256]{2,1,0:T(8,128)(2,1)S(1)}, bf16[2,72,256]{2,1,0:T(8,128)(2,1)S(1)}, u32[]{:S(2)}, u32[]{:S(2)}) collective-permute-start(bf16[2,72,256]{2,1,0:T(8,128)(2,1)S(1)} %get-tuple-element.29), channel_id=1, source_target_pairs={{0,2},{1,3},{2,0},{3,1},{4,6},{5,7},{6,4},{7,5},{8,10},{9,11},{10,... | collective-permute-start | bytes 221192 | tf_op jit(solution)/shard_map/ppermute | solution.py:203
  40.8 6.4 %collective-permute-start.3 = (bf16[2,72,256]{2,1,0:T(8,128)(2,1)S(1)}, bf16[2,72,256]{2,1,0:T(8,128)(2,1)S(1)}, u32[]{:S(2)}, u32[]{:S(2)}) collective-permute-start(bf16[2,72,256]{2,1,0:T(8,128)(2,1)S(1)} %get-tuple-element.28), channel_id=1, source_target_pairs={{0,3},{1,2},{2,1},{3,0},{4,7},{5,6},{6,5},{7,4},{8,11},{9,10},{10,... | collective-permute-start | bytes 221192 | tf_op jit(solution)/shard_map/ppermute | solution.py:203
  47.3 7.1 %collective-permute-start.4 = (s16[2,72,256]{2,1,0:T(8,128)(2,1)S(1)}, s16[2,72,256]{2,1,0:T(8,128)(2,1)S(1)}, u32[]{:S(2)}, u32[]{:S(2)}) collective-permute-start(s16[2,72,256]{2,1,0:T(8,128)(2,1)S(1)} %encode.1), channel_id=1, source_target_pairs={{0,8},{4,12},{8,0},{12,4},{16,24},{20,28},{24,16},{28,20},{1,9},{5... | collective-permute-start | bytes 221192 | tf_op jit(solution)/shard_map/ppermute | solution.py:203
  49.1 5.3 %collective-permute-start.5 = (s16[2,72,256]{2,1,0:T(8,128)(2,1)S(1)}, s16[2,72,256]{2,1,0:T(8,128)(2,1)S(1)}, u32[]{:S(2)}, u32[]{:S(2)}) collective-permute-start(s16[2,72,256]{2,1,0:T(8,128)(2,1)S(1)} %encode.1), channel_id=1, source_target_pairs={{0,16},{4,20},{8,24},{12,28},{16,0},{20,4},{24,8},{28,12},{1,17},{... | collective-permute-start | bytes 221192 | tf_op jit(solution)/shard_map/ppermute | solution.py:203
  50.6 5.3 %collective-permute-start.6 = (s16[2,72,256]{2,1,0:T(8,128)(2,1)S(1)}, s16[2,72,256]{2,1,0:T(8,128)(2,1)S(1)}, u32[]{:S(2)}, u32[]{:S(2)}) collective-permute-start(s16[2,72,256]{2,1,0:T(8,128)(2,1)S(1)} %encode.1), channel_id=1, source_target_pairs={{0,24},{4,28},{8,16},{12,20},{16,8},{20,12},{24,0},{28,4},{1,25},{... | collective-permute-start | bytes 221192 | tf_op jit(solution)/shard_map/ppermute | solution.py:203
  57.2 1.4 %collective-permute-start.7 = (f32[2,64,256]{2,1,0:T(8,128)S(1)}, f32[2,64,256]{2,1,0:T(8,128)S(1)}, u32[]{:S(2)}, u32[]{:S(2)}) collective-permute-start(f32[2,64,256]{2,1,0:T(8,128)S(1)} %fusion.1), channel_id=1, source_target_pairs={{0,4},{4,0},{8,12},{12,8},{16,20},{20,16},{24,28},{28,24},{1,5},{5... | collective-permute-start | bytes 393224 | tf_op jit(solution)/shard_map/ppermute | solution.py:203

commit v5 on v4

--- a/solution.py
+++ b/solution.py
@@ -54,7 +54,9 @@
         requests[dest] = dot_nt(info, place_at).astype(BF16)
 
 
-def row_sums_kernel(valid, rows, codes, out):
+def row_sums_kernel(valid, rows, codes, centres, out, held, loaded):
+    load = pltpu.make_async_copy(centres.at[pl.ds(0, held.shape[0])], held, loaded)
+    load.start()
     subs, padded, code_count = out.shape
     row_count, width = rows.shape
     width_sub = width // subs
@@ -67,6 +69,7 @@
         code_hit = mask_bf16(code_iota == live_codes[m : m + 1])
         out[m, 0:width_sub] = dot_nt(columns[m * width_sub : (m + 1) * width_sub], code_hit)
         out[m, width_sub:padded] = dot_nt(ones, code_hit)[0 : padded - width_sub]
+    load.wait()
 
 
 def sums_kernel(replicas, requests, gathered, row_sums, keep, send):
@@ -104,28 +107,33 @@
             pl.when(mine != at // half)(functools.partial(store, send))
 
 
-def gather_kernel(subs, requests, centres, pieces, near, found, loaded, written):
+def gather_kernel(subs, requests, held, centres, pieces, near, found, loaded, written):
     owners, _, capacity = requests.shape
     lists = centres.shape[0]
+    ready = held.shape[0]
     parts, chunks = loaded.shape[0], written.shape[0]
     chunk = owners // chunks
     span = chunk * capacity
+    step = (lists - ready) // parts
     loads, stores = [], []
     for part in range(parts):
-        rows = pl.ds(part * (lists // parts), lists // parts)
-        loads.append(pltpu.make_async_copy(centres.at[rows], near.at[rows], loaded.at[part]))
-        loads[-1].start()
+        load = pltpu.make_async_copy(
+            centres.at[pl.ds(ready + part * step, step)],
+            near.at[pl.ds(part * step, step)],
+            loaded.at[part],
+        )
+        load.start()
+        loads.append(load)
     for index in range(chunks):
         asked = jnp.concatenate([requests[index * chunk + j] for j in range(chunk)], axis=1)
         turned = asked.astype(F32).T.astype(I32)
         high, low = (turned[:, subs + i : subs + i + 1] for i in range(2))
         low_hit = mask_bf16(lax.broadcasted_iota(I32, (span, 256), 1) == low)
-        total = jnp.zeros((span, centres.shape[1]), F32)
+        hits = [low_hit * mask_bf16(high == h) for h in range(lists // 256)]
+        total = dot(jnp.concatenate(hits[: ready // 256], axis=1), held[...])
         for part in range(parts):
-            first, last = part * (lists // parts), (part + 1) * (lists // parts)
-            hit = jnp.concatenate(
-                [low_hit * mask_bf16(high == h) for h in range(first // 256, last // 256)], axis=1
-            )
+            first, last = part * step, (part + 1) * step
+            hit = jnp.concatenate(hits[(ready + first) // 256 : (ready + last) // 256], axis=1)
             if index == 0:
                 loads[part].wait()
             total += dot(hit, near[first:last])
@@ -182,15 +190,24 @@
     out[...] = jnp.where(lane < valid[0], error, 0.0)
 
 
-def encode_kernel(width_sub, *refs):
-    parts, out = refs[:-1], refs[-1]
+def encode_kernel(width_sub, book, *refs):
+    parts = refs[:-3]
+    out, near, loaded = refs[-3:]
     half, padded, code_count = out.shape
+    me, rep = lax.axis_index("list"), lax.axis_index("rep")
+    start = (2 * rep + jnp.bitwise_and(me, 1)) * half
+    load = pltpu.make_async_copy(book.at[pl.ds(start, half)], near, loaded)
+    load.start()
+    prior = jnp.where(me < 2, prior_weight, 0.0)
     which = lax.broadcasted_iota(I32, (padded - width_sub, code_count), 0)
     for m in range(half):
         total = parts[0][m]
         for part in parts[1:]:
             total += part[m].astype(F32)
-        sums, counts = total[:width_sub], total[width_sub:]
+        if m == 0:
+            load.wait()
+        sums = total[:width_sub] + prior * near[m]
+        counts = total[width_sub:] + jnp.where(which == 1, prior, 0.0)
         top = jnp.max(jnp.abs(sums), axis=0, keepdims=True)
         exponent = jnp.clip(jnp.ceil(jnp.log2(top)) - 1.0, -125.0, 127.0)
         scaled = jnp.clip(jnp.round(sums / jnp.exp2(exponent) * 16384.0), -32767.0, 32767.0)
@@ -246,15 +263,20 @@
     )
     requests = lax.all_to_all(requests, "list", 0, 0, tiled=True)
 
-    row_sums = pl.pallas_call(
+    far = pltpu.with_memory_space_constraint(centroids, pltpu.HBM)
+    row_sums, held = pl.pallas_call(
         row_sums_kernel,
-        in_specs=[SMEM] + [VMEM] * 2,
-        out_specs=VMEM,
-        out_shape=struct(subs, padded, code_count),
+        in_specs=[SMEM] + [VMEM] * 2 + [HBM],
+        out_specs=[VMEM] * 2,
+        out_shape=[
+            struct(subs, padded, code_count),
+            struct(lists // 2, width, dtype=BF16),
+        ],
+        scratch_shapes=[pltpu.SemaphoreType.DMA],
         compiler_params=params(24),
-        cost_estimate=cost(8 << 30, 16 << 20),
+        cost_estimate=cost(2 << 30, 4 << 20),
         name="row_sums",
-    )(valid_rows, memory_rows, codes)
+    )(valid_rows, memory_rows, codes, far)
     offsets = pl.pallas_call(
         offset_kernel,
         in_specs=[VMEM] * 3,
@@ -264,22 +286,21 @@
         cost_estimate=cost(1000, 1000),
         name="offsets",
     )(memory_rows, codes, book)
-    requests, row_sums = lax.optimization_barrier((requests, row_sums))
     gathered = pl.pallas_call(
         functools.partial(gather_kernel, subs),
-        in_specs=[VMEM, HBM],
+        in_specs=[VMEM, VMEM, HBM],
         out_specs=HBM,
-        out_shape=struct(owners, capacity, width, dtype=BF16),
+        out_shape=pltpu.HBM((owners, capacity, width), BF16),
         scratch_shapes=[
-            pltpu.VMEM((lists, width), BF16),
+            pltpu.VMEM((lists - lists // 2, width), BF16),
             pltpu.VMEM((owners, capacity, width), BF16),
             pltpu.SemaphoreType.DMA((4,)),
             pltpu.SemaphoreType.DMA((2,)),
         ],
-        compiler_params=params(57),
+        compiler_params=params(20 + 5 * (owners * capacity * width >> 19)),
         cost_estimate=cost(4 << 30, 6 << 20),
         name="gather",
-    )(requests, centroids)
+    )(requests, held, far)
     pieces = lax.all_to_all(gathered, "list", 0, 0, tiled=True)
 
     half_shape = struct(replicas, half, padded, code_count)
@@ -302,13 +323,17 @@
     parts = [own[0]] + [swap(own[s].astype(BF16), "rep", s) for s in range(1, replicas)]
     own = pl.pallas_call(
         functools.partial(encode_kernel, width_sub),
-        in_specs=[VMEM] * replicas,
+        in_specs=[HBM] + [VMEM] * replicas,
         out_specs=VMEM,
         out_shape=struct(half, padded, code_count, dtype=jnp.int16),
+        scratch_shapes=[
+            pltpu.VMEM((half, width_sub, code_count), F32),
+            pltpu.SemaphoreType.DMA,
+        ],
         compiler_params=params(20),
         cost_estimate=cost(1000, 1000),
         name="encode",
-    )(*parts)
+    )(book, *parts)
     own, offsets = lax.optimization_barrier((own, offsets))
     others = [swap(own, "list", s) for s in range(2, owners, 2)]
     row_error = pl.pallas_call(
@@ -322,8 +347,6 @@
     )(valid_rows, position, offsets, pieces.reshape(owners * capacity, width))
     row_error, *others = lax.optimization_barrier((row_error, *others))
     core = lax.axis_index("list") % 2
-    start = lax.axis_index("rep") * group_subs + core * half
-    prior = prior_weight * lax.dynamic_slice_in_dim(book, start, half, 0)
     parts = [part.astype(F32) for part in (own, *others)]
     parts = [
         jnp.where(
@@ -341,7 +364,7 @@
             (width_sub + 1, width_sub + 2),
         )
     )
-    own = (sums + prior) / (256.0 * high + low + prior_weight)
+    own = sums / (256.0 * high + low)
     other = swap(own, "list", 1)
     new_codebook = jnp.concatenate(
         [jnp.where(core == 0, own, other), jnp.where(core == 0, other, own)], axis=0

time: 59.9 us -> 56.6 us (0.945)
  other arithmetic: 3.46 us -> 1.31 us
  Pallas kernels: 19 us -> 17.4 us
  waiting for transfers between devices: 13.4 us -> 15 us
  local copies, waits for them, and re-layouts: 4.46 us -> 3.43 us
    all_to_all x1, waiting for transfers between devices: 1.93 us -> 4.09 us  [body(): pieces = lax.all_to_all(gathered, 'list', 0, 0, tiled=True)]
    another operation x1, other arithmetic: 1.45 us -> 0.22 us
    unnamed x25 -> x19, local copies, waits for them, and re-layouts: 4.44 us -> 3.4 us
    div x1, other arithmetic: 0.96 us -> 0.04 us  [body(): own = sums / (256.0 * high + low)]
    pallas_call x1, Pallas kernels: 5.33 us -> 4.49 us  [body(): pl.pallas_call(functools.partial(sums_kernel, replicas), in_specs=[VMEM]...]
    pallas_call x3, Pallas kernels: 9.39 us -> 8.61 us  [the longest x1 6.76 us: body(): pl.pallas_call(functools.partial(gather_kernel, subs), in_specs=[VMEM, VM...]
  transfers between devices with their start and end apart: 10 -> 10, of which waited for: 7 -> 7; matrix products, arithmetic and copies ran while one was open for 3% -> 1% of each run, Pallas kernels for 15% -> 16%
where the time goes in v5:
time: 56.6 us; the launch traced here: 56.1 us
  Pallas kernels  17.4 us (31%)
  starting transfers between devices  17.4 us (31%)
  waiting for transfers between devices  15 us (27%)
  local copies, waits for them, and re-layouts  3.43 us (6%)
  between operations  1.52 us (3%)
  other arithmetic  1.31 us (2%)
    ppermute x8, waiting for transfers between devices, swap(): return lax.ppermute(array, axis, [(i, i ^ step) for i in range(count)])  9.3 us
    ppermute x8, starting transfers between devices, swap(): return lax.ppermute(array, axis, [(i, i ^ step) for i in range(count)])  8.57 us
    pallas_call x1, Pallas kernels, body(): pl.pallas_call(functools.partial(gather_kernel, subs), in_specs=[VMEM, VM...  6.76 us
    all_to_all x1, starting transfers between devices, body(): requests = lax.all_to_all(requests, 'list', 0, 0, tiled=True)  5.17 us
    pallas_call x1, Pallas kernels, body(): pl.pallas_call(functools.partial(sums_kernel, replicas), in_specs=[VMEM]...  4.49 us
    all_to_all x1, waiting for transfers between devices, body(): pieces = lax.all_to_all(gathered, 'list', 0, 0, tiled=True)  4.09 us
    all_to_all x1, starting transfers between devices, body(): pieces = lax.all_to_all(gathered, 'list', 0, 0, tiled=True)  3.61 us
    unnamed x19, local copies, waits for them, and re-layouts  3.4 us
  transfers between devices with their start and end apart: 10, of which 7 were waited for; matrix products, arithmetic and copies ran while one was open for 1% of the time, Pallas kernels for 16%

profile of v5, /device:TPU:0, one launch (start us, length us, event | category | flops | bytes accessed | tf_op | source)
XLA Modules:
  0.0 56.1 jit_solution(11240547302763599393)
XLA Ops:
  1.3 1.9 %pack.1 = (bf16[8,32,128]{2,1,0:T(8,128)(2,1)}, s32[1,256]{1,0:T(1,128)}) custom-call(s32[1]{0:T(128)S(6)} %copy.24.valid, s32[1,256]{1,0:T(1,128)} %bitcast.45, s32[1,256]{1,0:T(1,128)} %bitcast.46, s32[16,256]{1,0:T(8,128)} %bitcast.36), custom_call_target="tpu_custom_call" | custom-call | flops 1000 | bytes 1000 | tf_op jit(solution)/shard_map/pack/pallas_call | solution.py:247
  3.1 5.2 %all-to-all-start = ((bf16[8,32,128]{2,1,0:T(8,128)(2,1)}), bf16[8,32,128]{2,1,0:T(8,128)(2,1)S(1)}, u32[]{:S(2)}, u32[]{:S(2)}) async-start(bf16[8,32,128]{2,1,0:T(8,128)(2,1)} %get-tuple-element.14), calls=%async_computation | async-start | bytes 131072 | tf_op jit(solution)/shard_map/all_to_all | solution.py:264
  8.3 1.0 %copy-done.2 = bf16[256,1024]{1,0:T(8,128)(2,1)S(1)} copy-done((bf16[256,1024]{1,0:T(8,128)(2,1)S(1)}, bf16[256,1024]{1,0:T(8,128)(2,1)}, u32[]{:S(2)}) %copy-start.2) | copy-done | bytes 524312
  9.3 0.7 %copy-done.4 = s32[256,16]{0,1:T(8,128)S(1)} copy-done((s32[256,16]{0,1:T(8,128)S(1)}, s32[256,16]{0,1:T(8,128)}, u32[]{:S(2)}) %copy-start.4) | copy-done | bytes 16408
  10.1 1.6 %row_sums.1 = (f32[16,72,256]{2,1,0:T(8,128)S(1)}, bf16[1024,1024]{1,0:T(8,128)(2,1)S(1)}) custom-call(s32[1]{0:T(128)S(6)} %copy.24.valid, bf16[256,1024]{1,0:T(8,128)(2,1)S(1)} %copy-done.2, s32[16,256]{1,0:T(8,128)S(1)} %bitcast.37, bf16[2048,1024]{1,0:T(8,128)(2,1)} %centres.3), custom_call_target="tpu_custom_call" | custom-call | flops 2147483648 | bytes 4194304 | tf_op jit(solution)/shard_map/row_sums/pallas_call | solution.py:267
  11.7 1.7 %all-to-all-done.requests = bf16[8,32,128]{2,1,0:T(8,128)(2,1)S(1)} async-done(((bf16[8,32,128]{2,1,0:T(8,128)(2,1)}), bf16[8,32,128]{2,1,0:T(8,128)(2,1)S(1)}, u32[]{:S(2)}, u32[]{:S(2)}) %all-to-all-start) | async-done | bytes 65568 | tf_op jit(solution)/shard_map/all_to_all | solution.py:264
  13.3 6.8 %gather.1 = bf16[8,128,1024]{2,1,0:T(8,128)(2,1)} custom-call(bf16[8,32,128]{2,1,0:T(8,128)(2,1)S(1)} %all-to-all-done.requests, bf16[1024,1024]{1,0:T(8,128)(2,1)S(1)} %get-tuple-element.15.held, bf16[2048,1024]{1,0:T(8,128)(2,1)} %centres.3), custom_call_target="tpu_custom_call" | custom-call | flops 4294967296 | bytes 6291456 | tf_op jit(solution)/shard_map/gather/pallas_call | solution.py:289
  20.1 3.6 %all-to-all-start.1 = ((bf16[8,128,1024]{2,1,0:T(8,128)(2,1)}), bf16[8,128,1024]{2,1,0:T(8,128)(2,1)S(1)}, u32[]{:S(2)}, u32[]{:S(2)}) async-start(bf16[8,128,1024]{2,1,0:T(8,128)(2,1)} %gather.1), calls=%async_computation.1 | async-start | bytes 4194304 | tf_op jit(solution)/shard_map/all_to_all | solution.py:304
  23.7 1.6 %copy-done = bf16[8,128,1024]{2,1,0:T(8,128)(2,1)S(1)} copy-done((bf16[8,128,1024]{2,1,0:T(8,128)(2,1)S(1)}, bf16[8,128,1024]{2,1,0:T(8,128)(2,1)}, u32[]{:S(2)}) %copy-start) | copy-done | bytes 2097176
  25.4 4.5 %sums.1 = (f32[4,2,72,256]{3,2,1,0:T(8,128)S(1)}, f32[4,2,72,256]{3,2,1,0:T(8,128)S(1)}) custom-call(bf16[8,32,128]{2,1,0:T(8,128)(2,1)S(1)} %all-to-all-done.requests, bf16[1024,1024]{1,0:T(8,128)(2,1)S(1)} %bitcast.33, f32[16,72,256]{2,1,0:T(8,128)S(1)} %get-tuple-element.16.row_sums), custom_call_target="tpu_custom_call" | custom-call | flops 1000 | bytes 1000 | tf_op jit(solution)/shard_map/sums/pallas_call | solution.py:307
  29.8 0.5 collective-permute-start
  30.3 0.9 %offsets.1 = f32[256,1024]{1,0:T(8,128)S(1)} custom-call(bf16[256,1024]{1,0:T(8,128)(2,1)S(1)} %copy-done.3, s32[16,256]{1,0:T(8,128)S(1)} %bitcast.38, f32[16,64,256]{2,1,0:T(8,128)S(1)} %bitcast.34), custom_call_target="tpu_custom_call" | custom-call | flops 1000 | bytes 1000 | tf_op jit(solution)/shard_map/offsets/pallas_call | solution.py:280
  31.3 0.7 %collective-permute-done = f32[4,2,72,256]{3,2,1,0:T(8,128)S(1)} collective-permute-done((f32[4,2,72,256]{3,2,1,0:T(8,128)S(1)}, f32[4,2,72,256]{3,2,1,0:T(8,128)S(1)}, u32[]{:S(2)}, u32[]{:S(2)}) %collective-permute-start) | collective-permute-done | bytes 589856 | tf_op jit(solution)/shard_map/ppermute | solution.py:220
  32.2 1.7 %collective-permute-start.1 = (bf16[2,72,256]{2,1,0:T(8,128)(2,1)S(1)}, bf16[2,72,256]{2,1,0:T(8,128)(2,1)S(1)}, u32[]{:S(2)}, u32[]{:S(2)}) collective-permute-start(bf16[2,72,256]{2,1,0:T(8,128)(2,1)S(1)} %get-tuple-element.30), channel_id=1, source_target_pairs={{0,1},{1,0},{2,3},{3,2},{4,5},{5,4},{6,7},{7,6},{8,9},{9,8},{10,11... | collective-permute-start | bytes 221192 | tf_op jit(solution)/shard_map/ppermute | solution.py:220
  33.9 2.6 %collective-permute-start.2 = (bf16[2,72,256]{2,1,0:T(8,128)(2,1)S(1)}, bf16[2,72,256]{2,1,0:T(8,128)(2,1)S(1)}, u32[]{:S(2)}, u32[]{:S(2)}) collective-permute-start(bf16[2,72,256]{2,1,0:T(8,128)(2,1)S(1)} %get-tuple-element.29), channel_id=1, source_target_pairs={{0,2},{1,3},{2,0},{3,1},{4,6},{5,7},{6,4},{7,5},{8,10},{9,11},{10,... | collective-permute-start | bytes 221192 | tf_op jit(solution)/shard_map/ppermute | solution.py:220
  36.8 6.0 %collective-permute-done.2.refs_2_ = bf16[2,72,256]{2,1,0:T(8,128)(2,1)S(1)} collective-permute-done((bf16[2,72,256]{2,1,0:T(8,128)(2,1)S(1)}, bf16[2,72,256]{2,1,0:T(8,128)(2,1)S(1)}, u32[]{:S(2)}, u32[]{:S(2)}) %collective-permute-start.2) | collective-permute-done | bytes 73760 | tf_op jit(solution)/shard_map/ppermute | solution.py:220
  42.9 0.3 encode.1
  43.1 1.8 %collective-permute-start.4 = (s16[2,72,256]{2,1,0:T(8,128)(2,1)S(1)}, s16[2,72,256]{2,1,0:T(8,128)(2,1)S(1)}, u32[]{:S(2)}, u32[]{:S(2)}) collective-permute-start(s16[2,72,256]{2,1,0:T(8,128)(2,1)S(1)} %encode.1), channel_id=1, source_target_pairs={{0,8},{4,12},{8,0},{12,4},{16,24},{20,28},{24,16},{28,20},{1,9},{5... | collective-permute-start | bytes 221192 | tf_op jit(solution)/shard_map/ppermute | solution.py:220
  44.9 1.5 %collective-permute-start.5 = (s16[2,72,256]{2,1,0:T(8,128)(2,1)S(1)}, s16[2,72,256]{2,1,0:T(8,128)(2,1)S(1)}, u32[]{:S(2)}, u32[]{:S(2)}) collective-permute-start(s16[2,72,256]{2,1,0:T(8,128)(2,1)S(1)} %encode.1), channel_id=1, source_target_pairs={{0,16},{4,20},{8,24},{12,28},{16,0},{20,4},{24,8},{28,12},{1,17},{... | collective-permute-start | bytes 221192 | tf_op jit(solution)/shard_map/ppermute | solution.py:220
  46.7 4.1 %all-to-all-done.1 = bf16[8,128,1024]{2,1,0:T(8,128)(2,1)S(1)} async-done(((bf16[8,128,1024]{2,1,0:T(8,128)(2,1)}), bf16[8,128,1024]{2,1,0:T(8,128)(2,1)S(1)}, u32[]{:S(2)}, u32[]{:S(2)}) %all-to-all-start.1) | async-done | bytes 2097184 | tf_op jit(solution)/shard_map/all_to_all | solution.py:304
  50.8 1.5 %errors.1 = f32[1,256]{1,0:T(1,128)} custom-call(s32[1]{0:T(128)S(6)} %copy.24.valid, s32[1,256]{1,0:T(1,128)S(1)} %copy-done.6, f32[256,1024]{1,0:T(8,128)S(1)} %offsets.1, bf16[1024,1024]{1,0:T(8,128)(2,1)S(1)} %bitcast.32), custom_call_target="tpu_custom_call" | custom-call | flops 1000 | bytes 1000 | tf_op jit(solution)/shard_map/errors/pallas_call | solution.py:339
  52.4 1.1 %collective-permute-done.6 = s16[2,72,256]{2,1,0:T(8,128)(2,1)S(1)} collective-permute-done((s16[2,72,256]{2,1,0:T(8,128)(2,1)S(1)}, s16[2,72,256]{2,1,0:T(8,128)(2,1)S(1)}, u32[]{:S(2)}, u32[]{:S(2)}) %collective-permute-start.6) | collective-permute-done | bytes 73760 | tf_op jit(solution)/shard_map/ppermute | solution.py:220
  54.0 1.3 %collective-permute-done.7 = f32[2,64,256]{2,1,0:T(8,128)S(1)} collective-permute-done((f32[2,64,256]{2,1,0:T(8,128)S(1)}, f32[2,64,256]{2,1,0:T(8,128)S(1)}, u32[]{:S(2)}, u32[]{:S(2)}) %collective-permute-start.7) | collective-permute-done | bytes 131104 | tf_op jit(solution)/shard_map/ppermute | solution.py:220
  55.4 0.7 %maximum_bitcast_fusion = f32[4,256,64]{1,2,0:T(8,128)} fusion(f32[2,64,256]{2,1,0:T(8,128)S(1)} %get-tuple-element.32, f32[2,64,256]{2,1,0:T(8,128)S(1)} %get-tuple-element.31), kind=kLoop, calls=%fused_computation.1 | loop fusion | flops 65536 | bytes 524288 | tf_op jit(solution)/shard_map/transpose | solution.py:372
  (39 shorter events, 1.3 us)
Async XLA Ops:
  3.1 10.2 %all-to-all-start = ((bf16[8,32,128]{2,1,0:T(8,128)(2,1)}), bf16[8,32,128]{2,1,0:T(8,128)(2,1)S(1)}, u32[]{:S(2)}, u32[]{:S(2)}) async-start(bf16[8,32,128]{2,1,0:T(8,128)(2,1)} %get-tuple-element.14), calls=%async_computation | async-start | bytes 131072 | tf_op jit(solution)/shard_map/all_to_all | solution.py:264
  8.3 1.0 %copy-start.2 = (bf16[256,1024]{1,0:T(8,128)(2,1)S(1)}, bf16[256,1024]{1,0:T(8,128)(2,1)}, u32[]{:S(2)}) copy-start(bf16[256,1024]{1,0:T(8,128)(2,1)} %rows.3) | copy-start | bytes 1572868
  9.3 0.7 %copy-start.4 = (s32[256,16]{0,1:T(8,128)S(1)}, s32[256,16]{0,1:T(8,128)}, u32[]{:S(2)}) copy-start(s32[256,16]{0,1:T(8,128)} %param.10) | copy-start | bytes 49156
  20.1 10.2 %copy-start.5 = (s32[256,16]{0,1:T(8,128)S(1)}, s32[256,16]{0,1:T(8,128)}, u32[]{:S(2)}) copy-start(s32[256,16]{0,1:T(8,128)} %param.10) | copy-start | bytes 49156
  20.1 30.7 %all-to-all-start.1 = ((bf16[8,128,1024]{2,1,0:T(8,128)(2,1)}), bf16[8,128,1024]{2,1,0:T(8,128)(2,1)S(1)}, u32[]{:S(2)}, u32[]{:S(2)}) async-start(bf16[8,128,1024]{2,1,0:T(8,128)(2,1)} %gather.1), calls=%async_computation.1 | async-start | bytes 4194304 | tf_op jit(solution)/shard_map/all_to_all | solution.py:304
  23.7 1.6 %copy-start = (bf16[8,128,1024]{2,1,0:T(8,128)(2,1)S(1)}, bf16[8,128,1024]{2,1,0:T(8,128)(2,1)}, u32[]{:S(2)}) copy-start(bf16[8,128,1024]{2,1,0:T(8,128)(2,1)} %gather.1) | copy-start | bytes 6291460
  25.3 5.0 %copy-start.1 = (f32[16,256,64]{1,2,0:T(8,128)S(1)}, f32[16,256,64]{1,2,0:T(8,128)}, u32[]{:S(2)}) copy-start(f32[16,256,64]{1,2,0:T(8,128)} %param.13) | copy-start | bytes 3145732
  25.3 5.0 %copy-start.3 = (bf16[256,1024]{1,0:T(8,128)(2,1)S(1)}, bf16[256,1024]{1,0:T(8,128)(2,1)}, u32[]{:S(2)}) copy-start(bf16[256,1024]{1,0:T(8,128)(2,1)} %rows.3) | copy-start | bytes 1572868
  29.8 2.1 %collective-permute-start = (f32[4,2,72,256]{3,2,1,0:T(8,128)S(1)}, f32[4,2,72,256]{3,2,1,0:T(8,128)S(1)}, u32[]{:S(2)}, u32[]{:S(2)}) collective-permute-start(f32[4,2,72,256]{3,2,1,0:T(8,128)S(1)} %get-tuple-element.18), channel_id=1, source_target_pairs={{0,4},{4,0},{8,12},{12,8},{16,20},{20,16},{24,28},{28,24},{1,5},{5... | collective-permute-start | bytes 1769480 | tf_op jit(solution)/shard_map/ppermute | solution.py:220
  32.0 18.9 %copy-start.6 = (s32[1,256]{1,0:T(1,128)S(1)}, s32[1,256]{1,0:T(1,128)}, u32[]{:S(2)}) copy-start(s32[1,256]{1,0:T(1,128)} %get-tuple-element.20.position) | copy-start | bytes 3076
  32.2 4.6 %collective-permute-start.1 = (bf16[2,72,256]{2,1,0:T(8,128)(2,1)S(1)}, bf16[2,72,256]{2,1,0:T(8,128)(2,1)S(1)}, u32[]{:S(2)}, u32[]{:S(2)}) collective-permute-start(bf16[2,72,256]{2,1,0:T(8,128)(2,1)S(1)} %get-tuple-element.30), channel_id=1, source_target_pairs={{0,1},{1,0},{2,3},{3,2},{4,5},{5,4},{6,7},{7,6},{8,9},{9,8},{10,11... | collective-permute-start | bytes 221192 | tf_op jit(solution)/shard_map/ppermute | solution.py:220
  33.9 9.0 %collective-permute-start.2 = (bf16[2,72,256]{2,1,0:T(8,128)(2,1)S(1)}, bf16[2,72,256]{2,1,0:T(8,128)(2,1)S(1)}, u32[]{:S(2)}, u32[]{:S(2)}) collective-permute-start(bf16[2,72,256]{2,1,0:T(8,128)(2,1)S(1)} %get-tuple-element.29), channel_id=1, source_target_pairs={{0,2},{1,3},{2,0},{3,1},{4,6},{5,7},{6,4},{7,5},{8,10},{9,11},{10,... | collective-permute-start | bytes 221192 | tf_op jit(solution)/shard_map/ppermute | solution.py:220
  36.5 6.4 %collective-permute-start.3 = (bf16[2,72,256]{2,1,0:T(8,128)(2,1)S(1)}, bf16[2,72,256]{2,1,0:T(8,128)(2,1)S(1)}, u32[]{:S(2)}, u32[]{:S(2)}) collective-permute-start(bf16[2,72,256]{2,1,0:T(8,128)(2,1)S(1)} %get-tuple-element.28), channel_id=1, source_target_pairs={{0,3},{1,2},{2,1},{3,0},{4,7},{5,6},{6,5},{7,4},{8,11},{9,10},{10,... | collective-permute-start | bytes 221192 | tf_op jit(solution)/shard_map/ppermute | solution.py:220
  43.1 9.3 %collective-permute-start.4 = (s16[2,72,256]{2,1,0:T(8,128)(2,1)S(1)}, s16[2,72,256]{2,1,0:T(8,128)(2,1)S(1)}, u32[]{:S(2)}, u32[]{:S(2)}) collective-permute-start(s16[2,72,256]{2,1,0:T(8,128)(2,1)S(1)} %encode.1), channel_id=1, source_target_pairs={{0,8},{4,12},{8,0},{12,4},{16,24},{20,28},{24,16},{28,20},{1,9},{5... | collective-permute-start | bytes 221192 | tf_op jit(solution)/shard_map/ppermute | solution.py:220
  44.9 7.4 %collective-permute-start.5 = (s16[2,72,256]{2,1,0:T(8,128)(2,1)S(1)}, s16[2,72,256]{2,1,0:T(8,128)(2,1)S(1)}, u32[]{:S(2)}, u32[]{:S(2)}) collective-permute-start(s16[2,72,256]{2,1,0:T(8,128)(2,1)S(1)} %encode.1), channel_id=1, source_target_pairs={{0,16},{4,20},{8,24},{12,28},{16,0},{20,4},{24,8},{28,12},{1,17},{... | collective-permute-start | bytes 221192 | tf_op jit(solution)/shard_map/ppermute | solution.py:220
  46.4 7.1 %collective-permute-start.6 = (s16[2,72,256]{2,1,0:T(8,128)(2,1)S(1)}, s16[2,72,256]{2,1,0:T(8,128)(2,1)S(1)}, u32[]{:S(2)}, u32[]{:S(2)}) collective-permute-start(s16[2,72,256]{2,1,0:T(8,128)(2,1)S(1)} %encode.1), channel_id=1, source_target_pairs={{0,24},{4,28},{8,16},{12,20},{16,8},{20,12},{24,0},{28,4},{1,25},{... | collective-permute-start | bytes 221192 | tf_op jit(solution)/shard_map/ppermute | solution.py:220
  53.9 1.4 %collective-permute-start.7 = (f32[2,64,256]{2,1,0:T(8,128)S(1)}, f32[2,64,256]{2,1,0:T(8,128)S(1)}, u32[]{:S(2)}, u32[]{:S(2)}) collective-permute-start(f32[2,64,256]{2,1,0:T(8,128)S(1)} %fusion), channel_id=1, source_target_pairs={{0,4},{4,0},{8,12},{12,8},{16,20},{20,16},{24,28},{28,24},{1,5},{5... | collective-permute-start | bytes 393224 | tf_op jit(solution)/shard_map/ppermute | solution.py:220

commit v6 on v5

--- a/solution.py
+++ b/solution.py
@@ -190,7 +190,31 @@
     out[...] = jnp.where(lane < valid[0], error, 0.0)
 
 
-def encode_kernel(width_sub, book, *refs):
+def scaled_codes(sums, counts, which):
+    top = jnp.max(jnp.abs(sums), axis=0, keepdims=True)
+    exponent = jnp.clip(jnp.ceil(jnp.log2(top)) - 1.0, -125.0, 127.0)
+    scaled = jnp.clip(jnp.round(sums / jnp.exp2(exponent) * 16384.0), -32767.0, 32767.0)
+    tail = jnp.where(which < 2, counts, jnp.where(which == 2, exponent, 0.0))
+    return jnp.concatenate([scaled, tail], axis=0).astype(I32).astype(jnp.int16)
+
+
+def add_kernel(width_sub, keep, got, own, *codes):
+    replicas, half, padded, code_count = keep.shape
+    which = lax.broadcasted_iota(I32, (padded - width_sub, code_count), 0)
+    for step in range(replicas):
+        for m in range(half):
+            sums = keep[step, m, 0:width_sub] + got[step, m, 0:width_sub]
+            counts = keep[step, m, width_sub:padded] + got[step, m, width_sub:padded]
+            high = jnp.floor(counts * (1.0 / 256.0))
+            counts = jnp.where(which == 0, high, counts - 256.0 * high)
+            if step == 0:
+                own[m, 0:width_sub] = sums
+                own[m, width_sub:padded] = counts
+            else:
+                codes[step - 1][m] = scaled_codes(sums, counts, which)
+
+
+def encode_kernel(width_sub, book, own, *refs):
     parts = refs[:-3]
     out, near, loaded = refs[-3:]
     half, padded, code_count = out.shape
@@ -200,19 +224,16 @@
     load.start()
     prior = jnp.where(me < 2, prior_weight, 0.0)
     which = lax.broadcasted_iota(I32, (padded - width_sub, code_count), 0)
+    load.wait()
     for m in range(half):
-        total = parts[0][m]
-        for part in parts[1:]:
-            total += part[m].astype(F32)
-        if m == 0:
-            load.wait()
-        sums = total[:width_sub] + prior * near[m]
-        counts = total[width_sub:] + jnp.where(which == 1, prior, 0.0)
-        top = jnp.max(jnp.abs(sums), axis=0, keepdims=True)
-        exponent = jnp.clip(jnp.ceil(jnp.log2(top)) - 1.0, -125.0, 127.0)
-        scaled = jnp.clip(jnp.round(sums / jnp.exp2(exponent) * 16384.0), -32767.0, 32767.0)
-        tail = jnp.where(which < 2, counts, jnp.where(which == 2, exponent, 0.0))
-        out[m] = jnp.concatenate([scaled, tail], axis=0).astype(I32).astype(jnp.int16)
+        sums = own[m, 0:width_sub] + prior * near[m]
+        counts = own[m, width_sub:padded] + jnp.where(which == 1, prior, 0.0)
+        for part in parts:
+            coded = part[m].astype(I32).astype(F32)
+            tail = coded[width_sub:padded]
+            sums += coded[0:width_sub] * (jnp.exp2(tail[2:3]) * (1.0 / 16384.0))
+            counts += tail
+        out[m] = scaled_codes(sums, counts, which)
 
 
 def swap(array, axis, step):
@@ -263,7 +284,10 @@
     )
     requests = lax.all_to_all(requests, "list", 0, 0, tiled=True)
 
-    far = pltpu.with_memory_space_constraint(centroids, pltpu.HBM)
+    far, far_rows, far_codes = (
+        pltpu.with_memory_space_constraint(array, pltpu.HBM)
+        for array in (centroids, memory_rows, codes)
+    )
     row_sums, held = pl.pallas_call(
         row_sums_kernel,
         in_specs=[SMEM] + [VMEM] * 2 + [HBM],
@@ -276,7 +300,7 @@
         compiler_params=params(24),
         cost_estimate=cost(2 << 30, 4 << 20),
         name="row_sums",
-    )(valid_rows, memory_rows, codes, far)
+    )(valid_rows, far_rows, far_codes, far)
     offsets = pl.pallas_call(
         offset_kernel,
         in_specs=[VMEM] * 3,
@@ -314,13 +338,18 @@
         name="sums",
     )(requests, gathered.reshape(owners * capacity, width), row_sums)
 
-    own = keep + swap(send, "list", 1)
-    row = lax.broadcasted_iota(I32, own.shape, 2)
-    high = jnp.floor(own * (1.0 / 256.0))
-    own = jnp.where(
-        row < width_sub, own, jnp.where(row == width_sub, high, own - 256.0 * high)
-    )
-    parts = [own[0]] + [swap(own[s].astype(BF16), "rep", s) for s in range(1, replicas)]
+    part_shape = (half, padded, code_count)
+    own, *codes_out = pl.pallas_call(
+        functools.partial(add_kernel, width_sub),
+        in_specs=[VMEM] * 2,
+        out_specs=[VMEM] * replicas,
+        out_shape=[struct(*part_shape)]
+        + [struct(*part_shape, dtype=jnp.int16)] * (replicas - 1),
+        compiler_params=params(20),
+        cost_estimate=cost(1000, 1000),
+        name="add",
+    )(keep, swap(send, "list", 1))
+    parts = [own] + [swap(codes_out[s - 1], "rep", s) for s in range(1, replicas)]
     own = pl.pallas_call(
         functools.partial(encode_kernel, width_sub),
         in_specs=[HBM] + [VMEM] * replicas,

time: 56.6 us -> 56.6 us (level)
  local copies, waits for them, and re-layouts: 3.43 us -> 1.65 us
  Pallas kernels: 17.4 us -> 18.7 us
  waiting for transfers between devices: 15 us -> 15.8 us
    unnamed x19 -> x13, local copies, waits for them, and re-layouts: 3.4 us -> 1.65 us
    pallas_call x1, Pallas kernels: 1.6 us -> 2.64 us  [body(): pl.pallas_call(row_sums_kernel, in_specs=[SMEM] + [VMEM] * 2 + [HBM], out...]
    all_to_all x1, waiting for transfers between devices: 1.65 us -> 2.37 us  [body(): requests = lax.all_to_all(requests, 'list', 0, 0, tiled=True)]
  transfers between devices with their start and end apart: 10 -> 10, of which waited for: 7 -> 7; matrix products, arithmetic and copies ran while one was open for 1% -> 0% of each run, Pallas kernels for 16% -> 18%
where the time goes in v6:
time: 56.6 us; the launch traced here: 56.1 us
  Pallas kernels  18.7 us (33%)
  starting transfers between devices  17.3 us (31%)
  waiting for transfers between devices  15.8 us (28%)
  local copies, waits for them, and re-layouts  1.65 us (3%)
  between operations  1.49 us (3%)
  other arithmetic  1.1 us (2%)
    ppermute x8, waiting for transfers between devices, swap(): return lax.ppermute(array, axis, [(i, i ^ step) for i in range(count)])  9.3 us
    ppermute x8, starting transfers between devices, swap(): return lax.ppermute(array, axis, [(i, i ^ step) for i in range(count)])  8.57 us
    pallas_call x1, Pallas kernels, body(): pl.pallas_call(functools.partial(gather_kernel, subs), in_specs=[VMEM, VM...  6.77 us
    all_to_all x1, starting transfers between devices, body(): requests = lax.all_to_all(requests, 'list', 0, 0, tiled=True)  5.17 us
    pallas_call x1, Pallas kernels, body(): pl.pallas_call(functools.partial(sums_kernel, replicas), in_specs=[VMEM]...  4.49 us
    all_to_all x1, waiting for transfers between devices, body(): pieces = lax.all_to_all(gathered, 'list', 0, 0, tiled=True)  4.16 us
    all_to_all x1, starting transfers between devices, body(): pieces = lax.all_to_all(gathered, 'list', 0, 0, tiled=True)  3.61 us
    pallas_call x1, Pallas kernels, body(): pl.pallas_call(row_sums_kernel, in_specs=[SMEM] + [VMEM] * 2 + [HBM], out...  2.64 us
  transfers between devices with their start and end apart: 10, of which 7 were waited for; matrix products, arithmetic and copies ran while one was open for 0% of the time, Pallas kernels for 18%

profile of v6, /device:TPU:0, one launch (start us, length us, event | category | flops | bytes accessed | tf_op | source)
XLA Modules:
  0.0 56.1 jit_solution(11166058703122838045)
XLA Ops:
  1.3 1.9 %pack.1 = (bf16[8,32,128]{2,1,0:T(8,128)(2,1)}, s32[1,256]{1,0:T(1,128)}) custom-call(s32[1]{0:T(128)S(6)} %copy.20.valid, s32[1,256]{1,0:T(1,128)} %bitcast.29, s32[1,256]{1,0:T(1,128)} %bitcast.30, s32[16,256]{1,0:T(8,128)} %bitcast.24), custom_call_target="tpu_custom_call" | custom-call | flops 1000 | bytes 1000 | tf_op jit(solution)/shard_map/pack/pallas_call | solution.py:268
  3.1 5.2 %all-to-all-start = ((bf16[8,32,128]{2,1,0:T(8,128)(2,1)}), bf16[8,32,128]{2,1,0:T(8,128)(2,1)S(1)}, u32[]{:S(2)}, u32[]{:S(2)}) async-start(bf16[8,32,128]{2,1,0:T(8,128)(2,1)} %get-tuple-element.18), calls=%async_computation | async-start | bytes 131072 | tf_op jit(solution)/shard_map/all_to_all | solution.py:285
  8.3 2.6 %row_sums.1 = (f32[16,72,256]{2,1,0:T(8,128)S(1)}, bf16[1024,1024]{1,0:T(8,128)(2,1)S(1)}) custom-call(s32[1]{0:T(128)S(6)} %copy.20.valid, bf16[256,1024]{1,0:T(8,128)(2,1)} %rows.3, s32[16,256]{1,0:T(8,128)} %bitcast.25, bf16[2048,1024]{1,0:T(8,128)(2,1)} %centres.3), custom_call_target="tpu_custom_call" | custom-call | flops 2147483648 | bytes 4194304 | tf_op jit(solution)/shard_map/row_sums/pallas_call | solution.py:291
  11.0 2.4 %all-to-all-done.requests = bf16[8,32,128]{2,1,0:T(8,128)(2,1)S(1)} async-done(((bf16[8,32,128]{2,1,0:T(8,128)(2,1)}), bf16[8,32,128]{2,1,0:T(8,128)(2,1)S(1)}, u32[]{:S(2)}, u32[]{:S(2)}) %all-to-all-start) | async-done | bytes 65568 | tf_op jit(solution)/shard_map/all_to_all | solution.py:285
  13.3 6.8 %gather.1 = bf16[8,128,1024]{2,1,0:T(8,128)(2,1)} custom-call(bf16[8,32,128]{2,1,0:T(8,128)(2,1)S(1)} %all-to-all-done.requests, bf16[1024,1024]{1,0:T(8,128)(2,1)S(1)} %get-tuple-element.19.held, bf16[2048,1024]{1,0:T(8,128)(2,1)} %centres.3), custom_call_target="tpu_custom_call" | custom-call | flops 4294967296 | bytes 6291456 | tf_op jit(solution)/shard_map/gather/pallas_call | solution.py:313
  20.1 3.6 %all-to-all-start.1 = ((bf16[8,128,1024]{2,1,0:T(8,128)(2,1)}), bf16[8,128,1024]{2,1,0:T(8,128)(2,1)S(1)}, u32[]{:S(2)}, u32[]{:S(2)}) async-start(bf16[8,128,1024]{2,1,0:T(8,128)(2,1)} %gather.1), calls=%async_computation.1 | async-start | bytes 4194304 | tf_op jit(solution)/shard_map/all_to_all | solution.py:328
  23.7 1.6 %copy-done = bf16[8,128,1024]{2,1,0:T(8,128)(2,1)S(1)} copy-done((bf16[8,128,1024]{2,1,0:T(8,128)(2,1)S(1)}, bf16[8,128,1024]{2,1,0:T(8,128)(2,1)}, u32[]{:S(2)}) %copy-start) | copy-done | bytes 2097176
  25.4 4.5 %sums.1 = (f32[4,2,72,256]{3,2,1,0:T(8,128)S(1)}, f32[4,2,72,256]{3,2,1,0:T(8,128)S(1)}) custom-call(bf16[8,32,128]{2,1,0:T(8,128)(2,1)S(1)} %all-to-all-done.requests, bf16[1024,1024]{1,0:T(8,128)(2,1)S(1)} %bitcast.21, f32[16,72,256]{2,1,0:T(8,128)S(1)} %get-tuple-element.20.row_sums), custom_call_target="tpu_custom_call" | custom-call | flops 1000 | bytes 1000 | tf_op jit(solution)/shard_map/sums/pallas_call | solution.py:331
  29.9 0.5 collective-permute-start
  30.3 0.9 %offsets.1 = f32[256,1024]{1,0:T(8,128)S(1)} custom-call(bf16[256,1024]{1,0:T(8,128)(2,1)S(1)} %copy-done.2, s32[16,256]{1,0:T(8,128)S(1)} %bitcast.26, f32[16,64,256]{2,1,0:T(8,128)S(1)} %bitcast.22), custom_call_target="tpu_custom_call" | custom-call | flops 1000 | bytes 1000 | tf_op jit(solution)/shard_map/offsets/pallas_call | solution.py:304
  31.3 0.7 %collective-permute-done.got = f32[4,2,72,256]{3,2,1,0:T(8,128)S(1)} collective-permute-done((f32[4,2,72,256]{3,2,1,0:T(8,128)S(1)}, f32[4,2,72,256]{3,2,1,0:T(8,128)S(1)}, u32[]{:S(2)}, u32[]{:S(2)}) %collective-permute-start) | collective-permute-done | bytes 589856 | tf_op jit(solution)/shard_map/ppermute | solution.py:241
  32.1 1.7 %collective-permute-start.1 = (s16[2,72,256]{2,1,0:T(8,128)(2,1)S(1)}, s16[2,72,256]{2,1,0:T(8,128)(2,1)S(1)}, u32[]{:S(2)}, u32[]{:S(2)}) collective-permute-start(s16[2,72,256]{2,1,0:T(8,128)(2,1)S(1)} %get-tuple-element.24), channel_id=1, source_target_pairs={{0,1},{1,0},{2,3},{3,2},{4,5},{5,4},{6,7},{7,6},{8,9},{9,8},{10,11... | collective-permute-start | bytes 221192 | tf_op jit(solution)/shard_map/ppermute | solution.py:241
  33.8 2.6 %collective-permute-start.2 = (s16[2,72,256]{2,1,0:T(8,128)(2,1)S(1)}, s16[2,72,256]{2,1,0:T(8,128)(2,1)S(1)}, u32[]{:S(2)}, u32[]{:S(2)}) collective-permute-start(s16[2,72,256]{2,1,0:T(8,128)(2,1)S(1)} %get-tuple-element.25), channel_id=1, source_target_pairs={{0,2},{1,3},{2,0},{3,1},{4,6},{5,7},{6,4},{7,5},{8,10},{9,11},{10,... | collective-permute-start | bytes 221192 | tf_op jit(solution)/shard_map/ppermute | solution.py:241
  36.4 0.2 collective-permute-start.3
  36.7 6.0 %collective-permute-done.2.refs_1_ = s16[2,72,256]{2,1,0:T(8,128)(2,1)S(1)} collective-permute-done((s16[2,72,256]{2,1,0:T(8,128)(2,1)S(1)}, s16[2,72,256]{2,1,0:T(8,128)(2,1)S(1)}, u32[]{:S(2)}, u32[]{:S(2)}) %collective-permute-start.2) | collective-permute-done | bytes 73760 | tf_op jit(solution)/shard_map/ppermute | solution.py:241
  42.8 0.3 encode.1
  43.1 1.8 %collective-permute-start.4 = (s16[2,72,256]{2,1,0:T(8,128)(2,1)S(1)}, s16[2,72,256]{2,1,0:T(8,128)(2,1)S(1)}, u32[]{:S(2)}, u32[]{:S(2)}) collective-permute-start(s16[2,72,256]{2,1,0:T(8,128)(2,1)S(1)} %encode.1), channel_id=1, source_target_pairs={{0,8},{4,12},{8,0},{12,4},{16,24},{20,28},{24,16},{28,20},{1,9},{5... | collective-permute-start | bytes 221192 | tf_op jit(solution)/shard_map/ppermute | solution.py:241
  44.9 1.5 %collective-permute-start.5 = (s16[2,72,256]{2,1,0:T(8,128)(2,1)S(1)}, s16[2,72,256]{2,1,0:T(8,128)(2,1)S(1)}, u32[]{:S(2)}, u32[]{:S(2)}) collective-permute-start(s16[2,72,256]{2,1,0:T(8,128)(2,1)S(1)} %encode.1), channel_id=1, source_target_pairs={{0,16},{4,20},{8,24},{12,28},{16,0},{20,4},{24,8},{28,12},{1,17},{... | collective-permute-start | bytes 221192 | tf_op jit(solution)/shard_map/ppermute | solution.py:241
  46.4 0.2 collective-permute-start.6
  46.7 4.2 %all-to-all-done.1 = bf16[8,128,1024]{2,1,0:T(8,128)(2,1)S(1)} async-done(((bf16[8,128,1024]{2,1,0:T(8,128)(2,1)}), bf16[8,128,1024]{2,1,0:T(8,128)(2,1)S(1)}, u32[]{:S(2)}, u32[]{:S(2)}) %all-to-all-start.1) | async-done | bytes 2097184 | tf_op jit(solution)/shard_map/all_to_all | solution.py:328
  50.8 1.6 %errors.1 = f32[1,256]{1,0:T(1,128)} custom-call(s32[1]{0:T(128)S(6)} %copy.20.valid, s32[1,256]{1,0:T(1,128)S(1)} %copy-done.4, f32[256,1024]{1,0:T(8,128)S(1)} %offsets.1, bf16[1024,1024]{1,0:T(8,128)(2,1)S(1)} %bitcast.20), custom_call_target="tpu_custom_call" | custom-call | flops 1000 | bytes 1000 | tf_op jit(solution)/shard_map/errors/pallas_call | solution.py:368
  52.4 1.1 %collective-permute-done.6 = s16[2,72,256]{2,1,0:T(8,128)(2,1)S(1)} collective-permute-done((s16[2,72,256]{2,1,0:T(8,128)(2,1)S(1)}, s16[2,72,256]{2,1,0:T(8,128)(2,1)S(1)}, u32[]{:S(2)}, u32[]{:S(2)}) %collective-permute-start.6) | collective-permute-done | bytes 73760 | tf_op jit(solution)/shard_map/ppermute | solution.py:241
  54.0 1.3 %collective-permute-done.7 = f32[2,64,256]{2,1,0:T(8,128)S(1)} collective-permute-done((f32[2,64,256]{2,1,0:T(8,128)S(1)}, f32[2,64,256]{2,1,0:T(8,128)S(1)}, u32[]{:S(2)}, u32[]{:S(2)}) %collective-permute-start.7) | collective-permute-done | bytes 131104 | tf_op jit(solution)/shard_map/ppermute | solution.py:241
  55.4 0.7 %maximum_bitcast_fusion = f32[4,256,64]{1,2,0:T(8,128)} fusion(f32[2,64,256]{2,1,0:T(8,128)S(1)} %get-tuple-element.35, f32[2,64,256]{2,1,0:T(8,128)S(1)} %get-tuple-element.34), kind=kLoop, calls=%fused_computation | loop fusion | flops 65536 | bytes 524288 | tf_op jit(solution)/shard_map/transpose | solution.py:401
  (31 shorter events, 0.8 us)
Async XLA Ops:
  3.1 10.2 %all-to-all-start = ((bf16[8,32,128]{2,1,0:T(8,128)(2,1)}), bf16[8,32,128]{2,1,0:T(8,128)(2,1)S(1)}, u32[]{:S(2)}, u32[]{:S(2)}) async-start(bf16[8,32,128]{2,1,0:T(8,128)(2,1)} %get-tuple-element.18), calls=%async_computation | async-start | bytes 131072 | tf_op jit(solution)/shard_map/all_to_all | solution.py:285
  20.1 10.2 %copy-start.3 = (s32[256,16]{0,1:T(8,128)S(1)}, s32[256,16]{0,1:T(8,128)}, u32[]{:S(2)}) copy-start(s32[256,16]{0,1:T(8,128)} %param.10) | copy-start | bytes 49156
  20.1 30.7 %all-to-all-start.1 = ((bf16[8,128,1024]{2,1,0:T(8,128)(2,1)}), bf16[8,128,1024]{2,1,0:T(8,128)(2,1)S(1)}, u32[]{:S(2)}, u32[]{:S(2)}) async-start(bf16[8,128,1024]{2,1,0:T(8,128)(2,1)} %gather.1), calls=%async_computation.1 | async-start | bytes 4194304 | tf_op jit(solution)/shard_map/all_to_all | solution.py:328
  23.7 1.6 %copy-start = (bf16[8,128,1024]{2,1,0:T(8,128)(2,1)S(1)}, bf16[8,128,1024]{2,1,0:T(8,128)(2,1)}, u32[]{:S(2)}) copy-start(bf16[8,128,1024]{2,1,0:T(8,128)(2,1)} %gather.1) | copy-start | bytes 6291460
  25.4 5.0 %copy-start.1 = (f32[16,256,64]{1,2,0:T(8,128)S(1)}, f32[16,256,64]{1,2,0:T(8,128)}, u32[]{:S(2)}) copy-start(f32[16,256,64]{1,2,0:T(8,128)} %param.13) | copy-start | bytes 3145732
  25.4 5.0 %copy-start.2 = (bf16[256,1024]{1,0:T(8,128)(2,1)S(1)}, bf16[256,1024]{1,0:T(8,128)(2,1)}, u32[]{:S(2)}) copy-start(bf16[256,1024]{1,0:T(8,128)(2,1)} %rows.3) | copy-start | bytes 1572868
  29.9 2.1 %collective-permute-start = (f32[4,2,72,256]{3,2,1,0:T(8,128)S(1)}, f32[4,2,72,256]{3,2,1,0:T(8,128)S(1)}, u32[]{:S(2)}, u32[]{:S(2)}) collective-permute-start(f32[4,2,72,256]{3,2,1,0:T(8,128)S(1)} %get-tuple-element.22), channel_id=1, source_target_pairs={{0,4},{4,0},{8,12},{12,8},{16,20},{20,16},{24,28},{28,24},{1,5},{5... | collective-permute-start | bytes 1769480 | tf_op jit(solution)/shard_map/ppermute | solution.py:241
  31.3 19.6 %copy-start.4 = (s32[1,256]{1,0:T(1,128)S(1)}, s32[1,256]{1,0:T(1,128)}, u32[]{:S(2)}) copy-start(s32[1,256]{1,0:T(1,128)} %get-tuple-element.28.position) | copy-start | bytes 3076
  32.1 4.6 %collective-permute-start.1 = (s16[2,72,256]{2,1,0:T(8,128)(2,1)S(1)}, s16[2,72,256]{2,1,0:T(8,128)(2,1)S(1)}, u32[]{:S(2)}, u32[]{:S(2)}) collective-permute-start(s16[2,72,256]{2,1,0:T(8,128)(2,1)S(1)} %get-tuple-element.24), channel_id=1, source_target_pairs={{0,1},{1,0},{2,3},{3,2},{4,5},{5,4},{6,7},{7,6},{8,9},{9,8},{10,11... | collective-permute-start | bytes 221192 | tf_op jit(solution)/shard_map/ppermute | solution.py:241
  33.8 9.0 %collective-permute-start.2 = (s16[2,72,256]{2,1,0:T(8,128)(2,1)S(1)}, s16[2,72,256]{2,1,0:T(8,128)(2,1)S(1)}, u32[]{:S(2)}, u32[]{:S(2)}) collective-permute-start(s16[2,72,256]{2,1,0:T(8,128)(2,1)S(1)} %get-tuple-element.25), channel_id=1, source_target_pairs={{0,2},{1,3},{2,0},{3,1},{4,6},{5,7},{6,4},{7,5},{8,10},{9,11},{10,... | collective-permute-start | bytes 221192 | tf_op jit(solution)/shard_map/ppermute | solution.py:241
  36.4 6.4 %collective-permute-start.3 = (s16[2,72,256]{2,1,0:T(8,128)(2,1)S(1)}, s16[2,72,256]{2,1,0:T(8,128)(2,1)S(1)}, u32[]{:S(2)}, u32[]{:S(2)}) collective-permute-start(s16[2,72,256]{2,1,0:T(8,128)(2,1)S(1)} %get-tuple-element.26), channel_id=1, source_target_pairs={{0,3},{1,2},{2,1},{3,0},{4,7},{5,6},{6,5},{7,4},{8,11},{9,10},{10,... | collective-permute-start | bytes 221192 | tf_op jit(solution)/shard_map/ppermute | solution.py:241
  43.1 9.3 %collective-permute-start.4 = (s16[2,72,256]{2,1,0:T(8,128)(2,1)S(1)}, s16[2,72,256]{2,1,0:T(8,128)(2,1)S(1)}, u32[]{:S(2)}, u32[]{:S(2)}) collective-permute-start(s16[2,72,256]{2,1,0:T(8,128)(2,1)S(1)} %encode.1), channel_id=1, source_target_pairs={{0,8},{4,12},{8,0},{12,4},{16,24},{20,28},{24,16},{28,20},{1,9},{5... | collective-permute-start | bytes 221192 | tf_op jit(solution)/shard_map/ppermute | solution.py:241
  44.9 7.5 %collective-permute-start.5 = (s16[2,72,256]{2,1,0:T(8,128)(2,1)S(1)}, s16[2,72,256]{2,1,0:T(8,128)(2,1)S(1)}, u32[]{:S(2)}, u32[]{:S(2)}) collective-permute-start(s16[2,72,256]{2,1,0:T(8,128)(2,1)S(1)} %encode.1), channel_id=1, source_target_pairs={{0,16},{4,20},{8,24},{12,28},{16,0},{20,4},{24,8},{28,12},{1,17},{... | collective-permute-start | bytes 221192 | tf_op jit(solution)/shard_map/ppermute | solution.py:241
  46.4 7.1 %collective-permute-start.6 = (s16[2,72,256]{2,1,0:T(8,128)(2,1)S(1)}, s16[2,72,256]{2,1,0:T(8,128)(2,1)S(1)}, u32[]{:S(2)}, u32[]{:S(2)}) collective-permute-start(s16[2,72,256]{2,1,0:T(8,128)(2,1)S(1)} %encode.1), channel_id=1, source_target_pairs={{0,24},{4,28},{8,16},{12,20},{16,8},{20,12},{24,0},{28,4},{1,25},{... | collective-permute-start | bytes 221192 | tf_op jit(solution)/shard_map/ppermute | solution.py:241
  53.9 1.4 %collective-permute-start.7 = (f32[2,64,256]{2,1,0:T(8,128)S(1)}, f32[2,64,256]{2,1,0:T(8,128)S(1)}, u32[]{:S(2)}, u32[]{:S(2)}) collective-permute-start(f32[2,64,256]{2,1,0:T(8,128)S(1)} %fusion), channel_id=1, source_target_pairs={{0,4},{4,0},{8,12},{12,8},{16,20},{20,16},{24,28},{28,24},{1,5},{5... | collective-permute-start | bytes 393224 | tf_op jit(solution)/shard_map/ppermute | solution.py:241

commit v7 on v6

--- a/solution.py
+++ b/solution.py
@@ -318,8 +318,8 @@
         scratch_shapes=[
             pltpu.VMEM((lists - lists // 2, width), BF16),
             pltpu.VMEM((owners, capacity, width), BF16),
+            pltpu.SemaphoreType.DMA((2,)),
             pltpu.SemaphoreType.DMA((4,)),
-            pltpu.SemaphoreType.DMA((2,)),
         ],
         compiler_params=params(20 + 5 * (owners * capacity * width >> 19)),
         cost_estimate=cost(4 << 30, 6 << 20),

time: 56.6 us -> 56.5 us (level)
  no operation moved by 1% of the time
where the time goes in v7:
time: 56.5 us; the launch traced here: 56 us
  Pallas kernels  18.6 us (33%)
  starting transfers between devices  17.3 us (31%)
  waiting for transfers between devices  15.8 us (28%)
  local copies, waits for them, and re-layouts  1.65 us (3%)
  between operations  1.49 us (3%)
  other arithmetic  1.1 us (2%)
    ppermute x8, waiting for transfers between devices, swap(): return lax.ppermute(array, axis, [(i, i ^ step) for i in range(count)])  9.29 us
    ppermute x8, starting transfers between devices, swap(): return lax.ppermute(array, axis, [(i, i ^ step) for i in range(count)])  8.55 us
    pallas_call x1, Pallas kernels, body(): pl.pallas_call(functools.partial(gather_kernel, subs), in_specs=[VMEM, VM...  6.71 us
    all_to_all x1, starting transfers between devices, body(): requests = lax.all_to_all(requests, 'list', 0, 0, tiled=True)  5.17 us
    pallas_call x1, Pallas kernels, body(): pl.pallas_call(functools.partial(sums_kernel, replicas), in_specs=[VMEM]...  4.5 us
    all_to_all x1, waiting for transfers between devices, body(): pieces = lax.all_to_all(gathered, 'list', 0, 0, tiled=True)  4.18 us
    all_to_all x1, starting transfers between devices, body(): pieces = lax.all_to_all(gathered, 'list', 0, 0, tiled=True)  3.61 us
    pallas_call x1, Pallas kernels, body(): pl.pallas_call(row_sums_kernel, in_specs=[SMEM] + [VMEM] * 2 + [HBM], out...  2.64 us
  transfers between devices with their start and end apart: 10, of which 7 were waited for; matrix products, arithmetic and copies ran while one was open for 0% of the time, Pallas kernels for 18%

profile of v7, /device:TPU:0, one launch (start us, length us, event | category | flops | bytes accessed | tf_op | source)
XLA Modules:
  0.0 56.0 jit_solution(11972212514592078662)
XLA Ops:
  1.3 1.9 %pack.1 = (bf16[8,32,128]{2,1,0:T(8,128)(2,1)}, s32[1,256]{1,0:T(1,128)}) custom-call(s32[1]{0:T(128)S(6)} %copy.20.valid, s32[1,256]{1,0:T(1,128)} %bitcast.29, s32[1,256]{1,0:T(1,128)} %bitcast.30, s32[16,256]{1,0:T(8,128)} %bitcast.24), custom_call_target="tpu_custom_call" | custom-call | flops 1000 | bytes 1000 | tf_op jit(solution)/shard_map/pack/pallas_call | solution.py:268
  3.1 5.2 %all-to-all-start = ((bf16[8,32,128]{2,1,0:T(8,128)(2,1)}), bf16[8,32,128]{2,1,0:T(8,128)(2,1)S(1)}, u32[]{:S(2)}, u32[]{:S(2)}) async-start(bf16[8,32,128]{2,1,0:T(8,128)(2,1)} %get-tuple-element.18), calls=%async_computation | async-start | bytes 131072 | tf_op jit(solution)/shard_map/all_to_all | solution.py:285
  8.3 2.6 %row_sums.1 = (f32[16,72,256]{2,1,0:T(8,128)S(1)}, bf16[1024,1024]{1,0:T(8,128)(2,1)S(1)}) custom-call(s32[1]{0:T(128)S(6)} %copy.20.valid, bf16[256,1024]{1,0:T(8,128)(2,1)} %rows.3, s32[16,256]{1,0:T(8,128)} %bitcast.25, bf16[2048,1024]{1,0:T(8,128)(2,1)} %centres.3), custom_call_target="tpu_custom_call" | custom-call | flops 2147483648 | bytes 4194304 | tf_op jit(solution)/shard_map/row_sums/pallas_call | solution.py:291
  11.0 2.4 %all-to-all-done.requests = bf16[8,32,128]{2,1,0:T(8,128)(2,1)S(1)} async-done(((bf16[8,32,128]{2,1,0:T(8,128)(2,1)}), bf16[8,32,128]{2,1,0:T(8,128)(2,1)S(1)}, u32[]{:S(2)}, u32[]{:S(2)}) %all-to-all-start) | async-done | bytes 65568 | tf_op jit(solution)/shard_map/all_to_all | solution.py:285
  13.3 6.7 %gather.1 = bf16[8,128,1024]{2,1,0:T(8,128)(2,1)} custom-call(bf16[8,32,128]{2,1,0:T(8,128)(2,1)S(1)} %all-to-all-done.requests, bf16[1024,1024]{1,0:T(8,128)(2,1)S(1)} %get-tuple-element.19.held, bf16[2048,1024]{1,0:T(8,128)(2,1)} %centres.3), custom_call_target="tpu_custom_call" | custom-call | flops 4294967296 | bytes 6291456 | tf_op jit(solution)/shard_map/gather/pallas_call | solution.py:313
  20.1 3.6 %all-to-all-start.1 = ((bf16[8,128,1024]{2,1,0:T(8,128)(2,1)}), bf16[8,128,1024]{2,1,0:T(8,128)(2,1)S(1)}, u32[]{:S(2)}, u32[]{:S(2)}) async-start(bf16[8,128,1024]{2,1,0:T(8,128)(2,1)} %gather.1), calls=%async_computation.1 | async-start | bytes 4194304 | tf_op jit(solution)/shard_map/all_to_all | solution.py:328
  23.7 1.6 %copy-done = bf16[8,128,1024]{2,1,0:T(8,128)(2,1)S(1)} copy-done((bf16[8,128,1024]{2,1,0:T(8,128)(2,1)S(1)}, bf16[8,128,1024]{2,1,0:T(8,128)(2,1)}, u32[]{:S(2)}) %copy-start) | copy-done | bytes 2097176
  25.3 4.5 %sums.1 = (f32[4,2,72,256]{3,2,1,0:T(8,128)S(1)}, f32[4,2,72,256]{3,2,1,0:T(8,128)S(1)}) custom-call(bf16[8,32,128]{2,1,0:T(8,128)(2,1)S(1)} %all-to-all-done.requests, bf16[1024,1024]{1,0:T(8,128)(2,1)S(1)} %bitcast.21, f32[16,72,256]{2,1,0:T(8,128)S(1)} %get-tuple-element.20.row_sums), custom_call_target="tpu_custom_call" | custom-call | flops 1000 | bytes 1000 | tf_op jit(solution)/shard_map/sums/pallas_call | solution.py:331
  29.8 0.5 collective-permute-start
  30.3 0.9 %offsets.1 = f32[256,1024]{1,0:T(8,128)S(1)} custom-call(bf16[256,1024]{1,0:T(8,128)(2,1)S(1)} %copy-done.2, s32[16,256]{1,0:T(8,128)S(1)} %bitcast.26, f32[16,64,256]{2,1,0:T(8,128)S(1)} %bitcast.22), custom_call_target="tpu_custom_call" | custom-call | flops 1000 | bytes 1000 | tf_op jit(solution)/shard_map/offsets/pallas_call | solution.py:304
  31.2 0.7 %collective-permute-done.got = f32[4,2,72,256]{3,2,1,0:T(8,128)S(1)} collective-permute-done((f32[4,2,72,256]{3,2,1,0:T(8,128)S(1)}, f32[4,2,72,256]{3,2,1,0:T(8,128)S(1)}, u32[]{:S(2)}, u32[]{:S(2)}) %collective-permute-start) | collective-permute-done | bytes 589856 | tf_op jit(solution)/shard_map/ppermute | solution.py:241
  32.1 1.6 %collective-permute-start.1 = (s16[2,72,256]{2,1,0:T(8,128)(2,1)S(1)}, s16[2,72,256]{2,1,0:T(8,128)(2,1)S(1)}, u32[]{:S(2)}, u32[]{:S(2)}) collective-permute-start(s16[2,72,256]{2,1,0:T(8,128)(2,1)S(1)} %get-tuple-element.24), channel_id=1, source_target_pairs={{0,1},{1,0},{2,3},{3,2},{4,5},{5,4},{6,7},{7,6},{8,9},{9,8},{10,11... | collective-permute-start | bytes 221192 | tf_op jit(solution)/shard_map/ppermute | solution.py:241
  33.7 2.6 %collective-permute-start.2 = (s16[2,72,256]{2,1,0:T(8,128)(2,1)S(1)}, s16[2,72,256]{2,1,0:T(8,128)(2,1)S(1)}, u32[]{:S(2)}, u32[]{:S(2)}) collective-permute-start(s16[2,72,256]{2,1,0:T(8,128)(2,1)S(1)} %get-tuple-element.25), channel_id=1, source_target_pairs={{0,2},{1,3},{2,0},{3,1},{4,6},{5,7},{6,4},{7,5},{8,10},{9,11},{10,... | collective-permute-start | bytes 221192 | tf_op jit(solution)/shard_map/ppermute | solution.py:241
  36.3 0.2 collective-permute-start.3
  36.7 6.0 %collective-permute-done.2.refs_1_ = s16[2,72,256]{2,1,0:T(8,128)(2,1)S(1)} collective-permute-done((s16[2,72,256]{2,1,0:T(8,128)(2,1)S(1)}, s16[2,72,256]{2,1,0:T(8,128)(2,1)S(1)}, u32[]{:S(2)}, u32[]{:S(2)}) %collective-permute-start.2) | collective-permute-done | bytes 73760 | tf_op jit(solution)/shard_map/ppermute | solution.py:241
  42.7 0.3 encode.1
  43.0 1.8 %collective-permute-start.4 = (s16[2,72,256]{2,1,0:T(8,128)(2,1)S(1)}, s16[2,72,256]{2,1,0:T(8,128)(2,1)S(1)}, u32[]{:S(2)}, u32[]{:S(2)}) collective-permute-start(s16[2,72,256]{2,1,0:T(8,128)(2,1)S(1)} %encode.1), channel_id=1, source_target_pairs={{0,8},{4,12},{8,0},{12,4},{16,24},{20,28},{24,16},{28,20},{1,9},{5... | collective-permute-start | bytes 221192 | tf_op jit(solution)/shard_map/ppermute | solution.py:241
  44.8 1.5 %collective-permute-start.5 = (s16[2,72,256]{2,1,0:T(8,128)(2,1)S(1)}, s16[2,72,256]{2,1,0:T(8,128)(2,1)S(1)}, u32[]{:S(2)}, u32[]{:S(2)}) collective-permute-start(s16[2,72,256]{2,1,0:T(8,128)(2,1)S(1)} %encode.1), channel_id=1, source_target_pairs={{0,16},{4,20},{8,24},{12,28},{16,0},{20,4},{24,8},{28,12},{1,17},{... | collective-permute-start | bytes 221192 | tf_op jit(solution)/shard_map/ppermute | solution.py:241
  46.3 0.2 collective-permute-start.6
  46.6 4.2 %all-to-all-done.1 = bf16[8,128,1024]{2,1,0:T(8,128)(2,1)S(1)} async-done(((bf16[8,128,1024]{2,1,0:T(8,128)(2,1)}), bf16[8,128,1024]{2,1,0:T(8,128)(2,1)S(1)}, u32[]{:S(2)}, u32[]{:S(2)}) %all-to-all-start.1) | async-done | bytes 2097184 | tf_op jit(solution)/shard_map/all_to_all | solution.py:328
  50.8 1.6 %errors.1 = f32[1,256]{1,0:T(1,128)} custom-call(s32[1]{0:T(128)S(6)} %copy.20.valid, s32[1,256]{1,0:T(1,128)S(1)} %copy-done.4, f32[256,1024]{1,0:T(8,128)S(1)} %offsets.1, bf16[1024,1024]{1,0:T(8,128)(2,1)S(1)} %bitcast.20), custom_call_target="tpu_custom_call" | custom-call | flops 1000 | bytes 1000 | tf_op jit(solution)/shard_map/errors/pallas_call | solution.py:368
  52.3 1.1 %collective-permute-done.6 = s16[2,72,256]{2,1,0:T(8,128)(2,1)S(1)} collective-permute-done((s16[2,72,256]{2,1,0:T(8,128)(2,1)S(1)}, s16[2,72,256]{2,1,0:T(8,128)(2,1)S(1)}, u32[]{:S(2)}, u32[]{:S(2)}) %collective-permute-start.6) | collective-permute-done | bytes 73760 | tf_op jit(solution)/shard_map/ppermute | solution.py:241
  54.0 1.3 %collective-permute-done.7 = f32[2,64,256]{2,1,0:T(8,128)S(1)} collective-permute-done((f32[2,64,256]{2,1,0:T(8,128)S(1)}, f32[2,64,256]{2,1,0:T(8,128)S(1)}, u32[]{:S(2)}, u32[]{:S(2)}) %collective-permute-start.7) | collective-permute-done | bytes 131104 | tf_op jit(solution)/shard_map/ppermute | solution.py:241
  55.3 0.7 %maximum_bitcast_fusion = f32[4,256,64]{1,2,0:T(8,128)} fusion(f32[2,64,256]{2,1,0:T(8,128)S(1)} %get-tuple-element.35, f32[2,64,256]{2,1,0:T(8,128)S(1)} %get-tuple-element.34), kind=kLoop, calls=%fused_computation | loop fusion | flops 65536 | bytes 524288 | tf_op jit(solution)/shard_map/transpose | solution.py:401
  (31 shorter events, 0.8 us)
Async XLA Ops:
  3.1 10.2 %all-to-all-start = ((bf16[8,32,128]{2,1,0:T(8,128)(2,1)}), bf16[8,32,128]{2,1,0:T(8,128)(2,1)S(1)}, u32[]{:S(2)}, u32[]{:S(2)}) async-start(bf16[8,32,128]{2,1,0:T(8,128)(2,1)} %get-tuple-element.18), calls=%async_computation | async-start | bytes 131072 | tf_op jit(solution)/shard_map/all_to_all | solution.py:285
  20.0 10.2 %copy-start.3 = (s32[256,16]{0,1:T(8,128)S(1)}, s32[256,16]{0,1:T(8,128)}, u32[]{:S(2)}) copy-start(s32[256,16]{0,1:T(8,128)} %param.10) | copy-start | bytes 49156
  20.1 30.7 %all-to-all-start.1 = ((bf16[8,128,1024]{2,1,0:T(8,128)(2,1)}), bf16[8,128,1024]{2,1,0:T(8,128)(2,1)S(1)}, u32[]{:S(2)}, u32[]{:S(2)}) async-start(bf16[8,128,1024]{2,1,0:T(8,128)(2,1)} %gather.1), calls=%async_computation.1 | async-start | bytes 4194304 | tf_op jit(solution)/shard_map/all_to_all | solution.py:328
  23.7 1.6 %copy-start = (bf16[8,128,1024]{2,1,0:T(8,128)(2,1)S(1)}, bf16[8,128,1024]{2,1,0:T(8,128)(2,1)}, u32[]{:S(2)}) copy-start(bf16[8,128,1024]{2,1,0:T(8,128)(2,1)} %gather.1) | copy-start | bytes 6291460
  25.3 5.0 %copy-start.1 = (f32[16,256,64]{1,2,0:T(8,128)S(1)}, f32[16,256,64]{1,2,0:T(8,128)}, u32[]{:S(2)}) copy-start(f32[16,256,64]{1,2,0:T(8,128)} %param.13) | copy-start | bytes 3145732
  25.3 5.0 %copy-start.2 = (bf16[256,1024]{1,0:T(8,128)(2,1)S(1)}, bf16[256,1024]{1,0:T(8,128)(2,1)}, u32[]{:S(2)}) copy-start(bf16[256,1024]{1,0:T(8,128)(2,1)} %rows.3) | copy-start | bytes 1572868
  29.8 2.1 %collective-permute-start = (f32[4,2,72,256]{3,2,1,0:T(8,128)S(1)}, f32[4,2,72,256]{3,2,1,0:T(8,128)S(1)}, u32[]{:S(2)}, u32[]{:S(2)}) collective-permute-start(f32[4,2,72,256]{3,2,1,0:T(8,128)S(1)} %get-tuple-element.22), channel_id=1, source_target_pairs={{0,4},{4,0},{8,12},{12,8},{16,20},{20,16},{24,28},{28,24},{1,5},{5... | collective-permute-start | bytes 1769480 | tf_op jit(solution)/shard_map/ppermute | solution.py:241
  31.2 19.6 %copy-start.4 = (s32[1,256]{1,0:T(1,128)S(1)}, s32[1,256]{1,0:T(1,128)}, u32[]{:S(2)}) copy-start(s32[1,256]{1,0:T(1,128)} %get-tuple-element.28.position) | copy-start | bytes 3076
  32.1 4.6 %collective-permute-start.1 = (s16[2,72,256]{2,1,0:T(8,128)(2,1)S(1)}, s16[2,72,256]{2,1,0:T(8,128)(2,1)S(1)}, u32[]{:S(2)}, u32[]{:S(2)}) collective-permute-start(s16[2,72,256]{2,1,0:T(8,128)(2,1)S(1)} %get-tuple-element.24), channel_id=1, source_target_pairs={{0,1},{1,0},{2,3},{3,2},{4,5},{5,4},{6,7},{7,6},{8,9},{9,8},{10,11... | collective-permute-start | bytes 221192 | tf_op jit(solution)/shard_map/ppermute | solution.py:241
  33.7 9.0 %collective-permute-start.2 = (s16[2,72,256]{2,1,0:T(8,128)(2,1)S(1)}, s16[2,72,256]{2,1,0:T(8,128)(2,1)S(1)}, u32[]{:S(2)}, u32[]{:S(2)}) collective-permute-start(s16[2,72,256]{2,1,0:T(8,128)(2,1)S(1)} %get-tuple-element.25), channel_id=1, source_target_pairs={{0,2},{1,3},{2,0},{3,1},{4,6},{5,7},{6,4},{7,5},{8,10},{9,11},{10,... | collective-permute-start | bytes 221192 | tf_op jit(solution)/shard_map/ppermute | solution.py:241
  36.3 6.4 %collective-permute-start.3 = (s16[2,72,256]{2,1,0:T(8,128)(2,1)S(1)}, s16[2,72,256]{2,1,0:T(8,128)(2,1)S(1)}, u32[]{:S(2)}, u32[]{:S(2)}) collective-permute-start(s16[2,72,256]{2,1,0:T(8,128)(2,1)S(1)} %get-tuple-element.26), channel_id=1, source_target_pairs={{0,3},{1,2},{2,1},{3,0},{4,7},{5,6},{6,5},{7,4},{8,11},{9,10},{10,... | collective-permute-start | bytes 221192 | tf_op jit(solution)/shard_map/ppermute | solution.py:241
  43.0 9.3 %collective-permute-start.4 = (s16[2,72,256]{2,1,0:T(8,128)(2,1)S(1)}, s16[2,72,256]{2,1,0:T(8,128)(2,1)S(1)}, u32[]{:S(2)}, u32[]{:S(2)}) collective-permute-start(s16[2,72,256]{2,1,0:T(8,128)(2,1)S(1)} %encode.1), channel_id=1, source_target_pairs={{0,8},{4,12},{8,0},{12,4},{16,24},{20,28},{24,16},{28,20},{1,9},{5... | collective-permute-start | bytes 221192 | tf_op jit(solution)/shard_map/ppermute | solution.py:241
  44.8 7.5 %collective-permute-start.5 = (s16[2,72,256]{2,1,0:T(8,128)(2,1)S(1)}, s16[2,72,256]{2,1,0:T(8,128)(2,1)S(1)}, u32[]{:S(2)}, u32[]{:S(2)}) collective-permute-start(s16[2,72,256]{2,1,0:T(8,128)(2,1)S(1)} %encode.1), channel_id=1, source_target_pairs={{0,16},{4,20},{8,24},{12,28},{16,0},{20,4},{24,8},{28,12},{1,17},{... | collective-permute-start | bytes 221192 | tf_op jit(solution)/shard_map/ppermute | solution.py:241
  46.3 7.1 %collective-permute-start.6 = (s16[2,72,256]{2,1,0:T(8,128)(2,1)S(1)}, s16[2,72,256]{2,1,0:T(8,128)(2,1)S(1)}, u32[]{:S(2)}, u32[]{:S(2)}) collective-permute-start(s16[2,72,256]{2,1,0:T(8,128)(2,1)S(1)} %encode.1), channel_id=1, source_target_pairs={{0,24},{4,28},{8,16},{12,20},{16,8},{20,12},{24,0},{28,4},{1,25},{... | collective-permute-start | bytes 221192 | tf_op jit(solution)/shard_map/ppermute | solution.py:241
  53.9 1.4 %collective-permute-start.7 = (f32[2,64,256]{2,1,0:T(8,128)S(1)}, f32[2,64,256]{2,1,0:T(8,128)S(1)}, u32[]{:S(2)}, u32[]{:S(2)}) collective-permute-start(f32[2,64,256]{2,1,0:T(8,128)S(1)} %fusion), channel_id=1, source_target_pairs={{0,4},{4,0},{8,12},{12,8},{16,20},{20,16},{24,28},{28,24},{1,5},{5... | collective-permute-start | bytes 393224 | tf_op jit(solution)/shard_map/ppermute | solution.py:241

commit v8 on v7

--- a/solution.py
+++ b/solution.py
@@ -67,8 +67,8 @@
     ones = jnp.ones((16, row_count), BF16)
     for m in range(subs):
         code_hit = mask_bf16(code_iota == live_codes[m : m + 1])
-        out[m, 0:width_sub] = dot_nt(columns[m * width_sub : (m + 1) * width_sub], code_hit)
-        out[m, width_sub:padded] = dot_nt(ones, code_hit)[0 : padded - width_sub]
+        part = jnp.concatenate([columns[m * width_sub : (m + 1) * width_sub], ones], axis=0)
+        out[m] = dot_nt(part, code_hit)[0:padded]
     load.wait()
 
 
@@ -236,6 +236,20 @@
         out[m] = scaled_codes(sums, counts, which)
 
 
+def finish_kernel(width_sub, *refs):
+    parts, out = refs[:-1], refs[-1]
+    for m in range(out.shape[0]):
+        coded = [part[m].astype(I32).astype(F32) for part in parts]
+        sums = sum(
+            code[0:width_sub] * (jnp.exp2(code[width_sub + 2 : width_sub + 3]) * (1.0 / 16384.0))
+            for code in coded
+        )
+        high, low = (
+            sum(code[width_sub + i : width_sub + i + 1] for code in coded) for i in range(2)
+        )
+        out[m] = sums / (256.0 * high + low)
+
+
 def swap(array, axis, step):
     count = lax.axis_size(axis)
     return lax.ppermute(array, axis, [(i, i ^ step) for i in range(count)])
@@ -376,24 +390,15 @@
     )(valid_rows, position, offsets, pieces.reshape(owners * capacity, width))
     row_error, *others = lax.optimization_barrier((row_error, *others))
     core = lax.axis_index("list") % 2
-    parts = [part.astype(F32) for part in (own, *others)]
-    parts = [
-        jnp.where(
-            lax.broadcasted_iota(I32, part.shape, 1) < width_sub,
-            part * (jnp.exp2(part[:, width_sub + 2 : width_sub + 3]) / 16384.0),
-            part,
-        )
-        for part in parts
-    ]
-    sums, high, low = (
-        functools.reduce(jnp.add, [part[:, first:last] for part in parts])
-        for first, last in (
-            (0, width_sub),
-            (width_sub, width_sub + 1),
-            (width_sub + 1, width_sub + 2),
-        )
-    )
-    own = sums / (256.0 * high + low)
+    own = pl.pallas_call(
+        functools.partial(finish_kernel, width_sub),
+        in_specs=[VMEM] * (1 + len(others)),
+        out_specs=VMEM,
+        out_shape=struct(half, width_sub, code_count),
+        compiler_params=params(20),
+        cost_estimate=cost(1000, 1000),
+        name="finish",
+    )(own, *others)
     other = swap(own, "list", 1)
     new_codebook = jnp.concatenate(
         [jnp.where(core == 0, own, other), jnp.where(core == 0, other, own)], axis=0

time: 56.5 us -> 56.1 us (level)
    unnamed x13 -> x10, local copies, waits for them, and re-layouts: 1.65 us -> 1.63 us
  transfers between devices with their start and end apart: 10 -> 10, of which waited for: 7 -> 6; matrix products, arithmetic and copies ran while one was open for 0% -> 0% of each run, Pallas kernels for 18% -> 18%
where the time goes in v8:
time: 56.1 us; the launch traced here: 55.7 us
  Pallas kernels  18.5 us (33%)
  starting transfers between devices  17.3 us (31%)
  waiting for transfers between devices  16 us (29%)
  local copies, waits for them, and re-layouts  1.63 us (3%)
  between operations  1.39 us (2%)
  other arithmetic  0.74 us (1%)
    ppermute x8, waiting for transfers between devices, swap(): return lax.ppermute(array, axis, [(i, i ^ step) for i in range(count)])  9.32 us
    ppermute x8, starting transfers between devices, swap(): return lax.ppermute(array, axis, [(i, i ^ step) for i in range(count)])  8.56 us
    pallas_call x1, Pallas kernels, body(): pl.pallas_call(functools.partial(gather_kernel, subs), in_specs=[VMEM, VM...  6.72 us
    all_to_all x1, starting transfers between devices, body(): requests = lax.all_to_all(requests, 'list', 0, 0, tiled=True)  5.17 us
    all_to_all x1, waiting for transfers between devices, body(): pieces = lax.all_to_all(gathered, 'list', 0, 0, tiled=True)  4.36 us
    pallas_call x1, Pallas kernels, body(): pl.pallas_call(functools.partial(sums_kernel, replicas), in_specs=[VMEM]...  4.32 us
    all_to_all x1, starting transfers between devices, body(): pieces = lax.all_to_all(gathered, 'list', 0, 0, tiled=True)  3.61 us
    pallas_call x1, Pallas kernels, body(): pl.pallas_call(row_sums_kernel, in_specs=[SMEM] + [VMEM] * 2 + [HBM], out...  2.64 us
  transfers between devices with their start and end apart: 10, of which 6 were waited for; matrix products, arithmetic and copies ran while one was open for 0% of the time, Pallas kernels for 18%

profile of v8, /device:TPU:0, one launch (start us, length us, event | category | flops | bytes accessed | tf_op | source)
XLA Modules:
  0.0 55.7 jit_solution(11266033057003288134)
XLA Ops:
  1.3 1.9 %pack.1 = (bf16[8,32,128]{2,1,0:T(8,128)(2,1)}, s32[1,256]{1,0:T(1,128)}) custom-call(s32[1]{0:T(128)S(6)} %copy.9.valid, s32[1,256]{1,0:T(1,128)} %bitcast.17, s32[1,256]{1,0:T(1,128)} %bitcast.18, s32[16,256]{1,0:T(8,128)} %bitcast.13), custom_call_target="tpu_custom_call" | custom-call | flops 1000 | bytes 1000 | tf_op jit(solution)/shard_map/pack/pallas_call | solution.py:282
  3.1 5.2 %all-to-all-start = ((bf16[8,32,128]{2,1,0:T(8,128)(2,1)}), bf16[8,32,128]{2,1,0:T(8,128)(2,1)S(1)}, u32[]{:S(2)}, u32[]{:S(2)}) async-start(bf16[8,32,128]{2,1,0:T(8,128)(2,1)} %get-tuple-element.18), calls=%async_computation | async-start | bytes 131072 | tf_op jit(solution)/shard_map/all_to_all | solution.py:299
  8.3 2.6 %row_sums.1 = (f32[16,72,256]{2,1,0:T(8,128)S(1)}, bf16[1024,1024]{1,0:T(8,128)(2,1)S(1)}) custom-call(s32[1]{0:T(128)S(6)} %copy.9.valid, bf16[256,1024]{1,0:T(8,128)(2,1)} %rows.3, s32[16,256]{1,0:T(8,128)} %bitcast.14, bf16[2048,1024]{1,0:T(8,128)(2,1)} %centres.3), custom_call_target="tpu_custom_call" | custom-call | flops 2147483648 | bytes 4194304 | tf_op jit(solution)/shard_map/row_sums/pallas_call | solution.py:305
  11.0 2.4 %all-to-all-done.requests = bf16[8,32,128]{2,1,0:T(8,128)(2,1)S(1)} async-done(((bf16[8,32,128]{2,1,0:T(8,128)(2,1)}), bf16[8,32,128]{2,1,0:T(8,128)(2,1)S(1)}, u32[]{:S(2)}, u32[]{:S(2)}) %all-to-all-start) | async-done | bytes 65568 | tf_op jit(solution)/shard_map/all_to_all | solution.py:299
  13.3 6.7 %gather.1 = bf16[8,128,1024]{2,1,0:T(8,128)(2,1)} custom-call(bf16[8,32,128]{2,1,0:T(8,128)(2,1)S(1)} %all-to-all-done.requests, bf16[1024,1024]{1,0:T(8,128)(2,1)S(1)} %get-tuple-element.19.held, bf16[2048,1024]{1,0:T(8,128)(2,1)} %centres.3), custom_call_target="tpu_custom_call" | custom-call | flops 4294967296 | bytes 6291456 | tf_op jit(solution)/shard_map/gather/pallas_call | solution.py:327
  20.1 3.6 %all-to-all-start.1 = ((bf16[8,128,1024]{2,1,0:T(8,128)(2,1)}), bf16[8,128,1024]{2,1,0:T(8,128)(2,1)S(1)}, u32[]{:S(2)}, u32[]{:S(2)}) async-start(bf16[8,128,1024]{2,1,0:T(8,128)(2,1)} %gather.1), calls=%async_computation.1 | async-start | bytes 4194304 | tf_op jit(solution)/shard_map/all_to_all | solution.py:342
  23.7 1.6 %copy-done = bf16[8,128,1024]{2,1,0:T(8,128)(2,1)S(1)} copy-done((bf16[8,128,1024]{2,1,0:T(8,128)(2,1)S(1)}, bf16[8,128,1024]{2,1,0:T(8,128)(2,1)}, u32[]{:S(2)}) %copy-start) | copy-done | bytes 2097176
  25.3 4.3 %sums.1 = (f32[4,2,72,256]{3,2,1,0:T(8,128)S(1)}, f32[4,2,72,256]{3,2,1,0:T(8,128)S(1)}) custom-call(bf16[8,32,128]{2,1,0:T(8,128)(2,1)S(1)} %all-to-all-done.requests, bf16[1024,1024]{1,0:T(8,128)(2,1)S(1)} %bitcast.10, f32[16,72,256]{2,1,0:T(8,128)S(1)} %get-tuple-element.20.row_sums), custom_call_target="tpu_custom_call" | custom-call | flops 1000 | bytes 1000 | tf_op jit(solution)/shard_map/sums/pallas_call | solution.py:345
  29.6 0.5 collective-permute-start
  30.1 1.6 %collective-permute-done.got = f32[4,2,72,256]{3,2,1,0:T(8,128)S(1)} collective-permute-done((f32[4,2,72,256]{3,2,1,0:T(8,128)S(1)}, f32[4,2,72,256]{3,2,1,0:T(8,128)S(1)}, u32[]{:S(2)}, u32[]{:S(2)}) %collective-permute-start) | collective-permute-done | bytes 589856 | tf_op jit(solution)/shard_map/ppermute | solution.py:255
  31.9 1.7 %collective-permute-start.1 = (s16[2,72,256]{2,1,0:T(8,128)(2,1)S(1)}, s16[2,72,256]{2,1,0:T(8,128)(2,1)S(1)}, u32[]{:S(2)}, u32[]{:S(2)}) collective-permute-start(s16[2,72,256]{2,1,0:T(8,128)(2,1)S(1)} %get-tuple-element.24), channel_id=1, source_target_pairs={{0,1},{1,0},{2,3},{3,2},{4,5},{5,4},{6,7},{7,6},{8,9},{9,8},{10,11... | collective-permute-start | bytes 221192 | tf_op jit(solution)/shard_map/ppermute | solution.py:255
  33.6 2.6 %collective-permute-start.2 = (s16[2,72,256]{2,1,0:T(8,128)(2,1)S(1)}, s16[2,72,256]{2,1,0:T(8,128)(2,1)S(1)}, u32[]{:S(2)}, u32[]{:S(2)}) collective-permute-start(s16[2,72,256]{2,1,0:T(8,128)(2,1)S(1)} %get-tuple-element.25), channel_id=1, source_target_pairs={{0,2},{1,3},{2,0},{3,1},{4,6},{5,7},{6,4},{7,5},{8,10},{9,11},{10,... | collective-permute-start | bytes 221192 | tf_op jit(solution)/shard_map/ppermute | solution.py:255
  36.1 0.2 collective-permute-start.3
  36.4 0.9 %offsets.1 = f32[256,1024]{1,0:T(8,128)S(1)} custom-call(bf16[256,1024]{1,0:T(8,128)(2,1)S(1)} %copy-done.2, s32[16,256]{1,0:T(8,128)S(1)} %bitcast.15, f32[16,64,256]{2,1,0:T(8,128)S(1)} %bitcast.11), custom_call_target="tpu_custom_call" | custom-call | flops 1000 | bytes 1000 | tf_op jit(solution)/shard_map/offsets/pallas_call | solution.py:318
  37.3 5.2 %collective-permute-done.2.refs_1_ = s16[2,72,256]{2,1,0:T(8,128)(2,1)S(1)} collective-permute-done((s16[2,72,256]{2,1,0:T(8,128)(2,1)S(1)}, s16[2,72,256]{2,1,0:T(8,128)(2,1)S(1)}, u32[]{:S(2)}, u32[]{:S(2)}) %collective-permute-start.2) | collective-permute-done | bytes 73760 | tf_op jit(solution)/shard_map/ppermute | solution.py:255
  42.5 0.3 encode.1.refs_0_
  42.8 1.8 %collective-permute-start.4 = (s16[2,72,256]{2,1,0:T(8,128)(2,1)S(1)}, s16[2,72,256]{2,1,0:T(8,128)(2,1)S(1)}, u32[]{:S(2)}, u32[]{:S(2)}) collective-permute-start(s16[2,72,256]{2,1,0:T(8,128)(2,1)S(1)} %encode.1.refs_0_), channel_id=1, source_target_pairs={{0,8},{4,12},{8,0},{12,4},{16,24},{20,28},{24,16},{28,20},{1,9},{5... | collective-permute-start | bytes 221192 | tf_op jit(solution)/shard_map/ppermute | solution.py:255
  44.7 1.5 %collective-permute-start.5 = (s16[2,72,256]{2,1,0:T(8,128)(2,1)S(1)}, s16[2,72,256]{2,1,0:T(8,128)(2,1)S(1)}, u32[]{:S(2)}, u32[]{:S(2)}) collective-permute-start(s16[2,72,256]{2,1,0:T(8,128)(2,1)S(1)} %encode.1.refs_0_), channel_id=1, source_target_pairs={{0,16},{4,20},{8,24},{12,28},{16,0},{20,4},{24,8},{28,12},{1,17},{... | collective-permute-start | bytes 221192 | tf_op jit(solution)/shard_map/ppermute | solution.py:255
  46.2 0.2 collective-permute-start.6
  46.4 4.4 %all-to-all-done.1 = bf16[8,128,1024]{2,1,0:T(8,128)(2,1)S(1)} async-done(((bf16[8,128,1024]{2,1,0:T(8,128)(2,1)}), bf16[8,128,1024]{2,1,0:T(8,128)(2,1)S(1)}, u32[]{:S(2)}, u32[]{:S(2)}) %all-to-all-start.1) | async-done | bytes 2097184 | tf_op jit(solution)/shard_map/all_to_all | solution.py:342
  50.8 1.6 %errors.1 = f32[1,256]{1,0:T(1,128)} custom-call(s32[1]{0:T(128)S(6)} %copy.9.valid, s32[1,256]{1,0:T(1,128)S(1)} %copy-done.4, f32[256,1024]{1,0:T(8,128)S(1)} %offsets.1, bf16[1024,1024]{1,0:T(8,128)(2,1)S(1)} %bitcast.9), custom_call_target="tpu_custom_call" | custom-call | flops 1000 | bytes 1000 | tf_op jit(solution)/shard_map/errors/pallas_call | solution.py:382
  52.3 1.1 %collective-permute-done.6.refs_3_ = s16[2,72,256]{2,1,0:T(8,128)(2,1)S(1)} collective-permute-done((s16[2,72,256]{2,1,0:T(8,128)(2,1)S(1)}, s16[2,72,256]{2,1,0:T(8,128)(2,1)S(1)}, u32[]{:S(2)}, u32[]{:S(2)}) %collective-permute-start.6) | collective-permute-done | bytes 73760 | tf_op jit(solution)/shard_map/ppermute | solution.py:255
  53.6 1.3 %collective-permute-done.7 = f32[2,64,256]{2,1,0:T(8,128)S(1)} collective-permute-done((f32[2,64,256]{2,1,0:T(8,128)S(1)}, f32[2,64,256]{2,1,0:T(8,128)S(1)}, u32[]{:S(2)}, u32[]{:S(2)}) %collective-permute-start.7) | collective-permute-done | bytes 131104 | tf_op jit(solution)/shard_map/ppermute | solution.py:255
  55.0 0.7 %maximum_bitcast_fusion = f32[4,256,64]{1,2,0:T(8,128)} fusion(f32[2,64,256]{2,1,0:T(8,128)S(1)} %get-tuple-element.35, f32[2,64,256]{2,1,0:T(8,128)S(1)} %get-tuple-element.34), kind=kLoop, calls=%fused_computation | loop fusion | flops 65536 | bytes 524288 | tf_op jit(solution)/shard_map/transpose | solution.py:406
  (17 shorter events, 0.4 us)
Async XLA Ops:
  3.1 10.2 %all-to-all-start = ((bf16[8,32,128]{2,1,0:T(8,128)(2,1)}), bf16[8,32,128]{2,1,0:T(8,128)(2,1)S(1)}, u32[]{:S(2)}, u32[]{:S(2)}) async-start(bf16[8,32,128]{2,1,0:T(8,128)(2,1)} %get-tuple-element.18), calls=%async_computation | async-start | bytes 131072 | tf_op jit(solution)/shard_map/all_to_all | solution.py:299
  20.1 30.7 %all-to-all-start.1 = ((bf16[8,128,1024]{2,1,0:T(8,128)(2,1)}), bf16[8,128,1024]{2,1,0:T(8,128)(2,1)S(1)}, u32[]{:S(2)}, u32[]{:S(2)}) async-start(bf16[8,128,1024]{2,1,0:T(8,128)(2,1)} %gather.1), calls=%async_computation.1 | async-start | bytes 4194304 | tf_op jit(solution)/shard_map/all_to_all | solution.py:342
  23.7 1.6 %copy-start = (bf16[8,128,1024]{2,1,0:T(8,128)(2,1)S(1)}, bf16[8,128,1024]{2,1,0:T(8,128)(2,1)}, u32[]{:S(2)}) copy-start(bf16[8,128,1024]{2,1,0:T(8,128)(2,1)} %gather.1) | copy-start | bytes 6291460
  25.3 11.1 %copy-start.1 = (f32[16,256,64]{1,2,0:T(8,128)S(1)}, f32[16,256,64]{1,2,0:T(8,128)}, u32[]{:S(2)}) copy-start(f32[16,256,64]{1,2,0:T(8,128)} %param.13) | copy-start | bytes 3145732
  25.3 11.1 %copy-start.2 = (bf16[256,1024]{1,0:T(8,128)(2,1)S(1)}, bf16[256,1024]{1,0:T(8,128)(2,1)}, u32[]{:S(2)}) copy-start(bf16[256,1024]{1,0:T(8,128)(2,1)} %rows.3) | copy-start | bytes 1572868
  25.3 11.1 %copy-start.3 = (s32[256,16]{0,1:T(8,128)S(1)}, s32[256,16]{0,1:T(8,128)}, u32[]{:S(2)}) copy-start(s32[256,16]{0,1:T(8,128)} %param.10) | copy-start | bytes 49156
  29.6 2.1 %collective-permute-start = (f32[4,2,72,256]{3,2,1,0:T(8,128)S(1)}, f32[4,2,72,256]{3,2,1,0:T(8,128)S(1)}, u32[]{:S(2)}, u32[]{:S(2)}) collective-permute-start(f32[4,2,72,256]{3,2,1,0:T(8,128)S(1)} %get-tuple-element.22), channel_id=1, source_target_pairs={{0,4},{4,0},{8,12},{12,8},{16,20},{20,16},{24,28},{28,24},{1,5},{5... | collective-permute-start | bytes 1769480 | tf_op jit(solution)/shard_map/ppermute | solution.py:255
  31.9 18.9 %copy-start.4 = (s32[1,256]{1,0:T(1,128)S(1)}, s32[1,256]{1,0:T(1,128)}, u32[]{:S(2)}) copy-start(s32[1,256]{1,0:T(1,128)} %get-tuple-element.28.position) | copy-start | bytes 3076
  31.9 5.4 %collective-permute-start.1 = (s16[2,72,256]{2,1,0:T(8,128)(2,1)S(1)}, s16[2,72,256]{2,1,0:T(8,128)(2,1)S(1)}, u32[]{:S(2)}, u32[]{:S(2)}) collective-permute-start(s16[2,72,256]{2,1,0:T(8,128)(2,1)S(1)} %get-tuple-element.24), channel_id=1, source_target_pairs={{0,1},{1,0},{2,3},{3,2},{4,5},{5,4},{6,7},{7,6},{8,9},{9,8},{10,11... | collective-permute-start | bytes 221192 | tf_op jit(solution)/shard_map/ppermute | solution.py:255
  33.6 9.0 %collective-permute-start.2 = (s16[2,72,256]{2,1,0:T(8,128)(2,1)S(1)}, s16[2,72,256]{2,1,0:T(8,128)(2,1)S(1)}, u32[]{:S(2)}, u32[]{:S(2)}) collective-permute-start(s16[2,72,256]{2,1,0:T(8,128)(2,1)S(1)} %get-tuple-element.25), channel_id=1, source_target_pairs={{0,2},{1,3},{2,0},{3,1},{4,6},{5,7},{6,4},{7,5},{8,10},{9,11},{10,... | collective-permute-start | bytes 221192 | tf_op jit(solution)/shard_map/ppermute | solution.py:255
  36.1 6.4 %collective-permute-start.3 = (s16[2,72,256]{2,1,0:T(8,128)(2,1)S(1)}, s16[2,72,256]{2,1,0:T(8,128)(2,1)S(1)}, u32[]{:S(2)}, u32[]{:S(2)}) collective-permute-start(s16[2,72,256]{2,1,0:T(8,128)(2,1)S(1)} %get-tuple-element.26), channel_id=1, source_target_pairs={{0,3},{1,2},{2,1},{3,0},{4,7},{5,6},{6,5},{7,4},{8,11},{9,10},{10,... | collective-permute-start | bytes 221192 | tf_op jit(solution)/shard_map/ppermute | solution.py:255
  42.8 9.5 %collective-permute-start.4 = (s16[2,72,256]{2,1,0:T(8,128)(2,1)S(1)}, s16[2,72,256]{2,1,0:T(8,128)(2,1)S(1)}, u32[]{:S(2)}, u32[]{:S(2)}) collective-permute-start(s16[2,72,256]{2,1,0:T(8,128)(2,1)S(1)} %encode.1.refs_0_), channel_id=1, source_target_pairs={{0,8},{4,12},{8,0},{12,4},{16,24},{20,28},{24,16},{28,20},{1,9},{5... | collective-permute-start | bytes 221192 | tf_op jit(solution)/shard_map/ppermute | solution.py:255
  44.7 7.7 %collective-permute-start.5 = (s16[2,72,256]{2,1,0:T(8,128)(2,1)S(1)}, s16[2,72,256]{2,1,0:T(8,128)(2,1)S(1)}, u32[]{:S(2)}, u32[]{:S(2)}) collective-permute-start(s16[2,72,256]{2,1,0:T(8,128)(2,1)S(1)} %encode.1.refs_0_), channel_id=1, source_target_pairs={{0,16},{4,20},{8,24},{12,28},{16,0},{20,4},{24,8},{28,12},{1,17},{... | collective-permute-start | bytes 221192 | tf_op jit(solution)/shard_map/ppermute | solution.py:255
  46.2 7.3 %collective-permute-start.6 = (s16[2,72,256]{2,1,0:T(8,128)(2,1)S(1)}, s16[2,72,256]{2,1,0:T(8,128)(2,1)S(1)}, u32[]{:S(2)}, u32[]{:S(2)}) collective-permute-start(s16[2,72,256]{2,1,0:T(8,128)(2,1)S(1)} %encode.1.refs_0_), channel_id=1, source_target_pairs={{0,24},{4,28},{8,16},{12,20},{16,8},{20,12},{24,0},{28,4},{1,25},{... | collective-permute-start | bytes 221192 | tf_op jit(solution)/shard_map/ppermute | solution.py:255
  53.5 1.4 %collective-permute-start.7 = (f32[2,64,256]{2,1,0:T(8,128)S(1)}, f32[2,64,256]{2,1,0:T(8,128)S(1)}, u32[]{:S(2)}, u32[]{:S(2)}) collective-permute-start(f32[2,64,256]{2,1,0:T(8,128)S(1)} %finish.1), channel_id=1, source_target_pairs={{0,4},{4,0},{8,12},{12,8},{16,20},{20,16},{24,28},{28,24},{1,5},{5... | collective-permute-start | bytes 393224 | tf_op jit(solution)/shard_map/ppermute | solution.py:255

commit v9 on v8

--- a/solution.py
+++ b/solution.py
@@ -321,7 +321,7 @@
         out_specs=VMEM,
         out_shape=struct(row_count, width),
         compiler_params=params(48),
-        cost_estimate=cost(1000, 1000),
+        cost_estimate=cost(1 << 30, 2 << 20),
         name="offsets",
     )(memory_rows, codes, book)
     gathered = pl.pallas_call(
@@ -348,7 +348,7 @@
         out_specs=[VMEM] * 2,
         out_shape=[half_shape] * 2,
         compiler_params=params(20),
-        cost_estimate=cost(1000, 1000),
+        cost_estimate=cost(4 << 30, 4 << 20),
         name="sums",
     )(requests, gathered.reshape(owners * capacity, width), row_sums)
 

time: 56.1 us -> 56.1 us (level)
  no operation moved by 1% of the time
where the time goes in v9:
time: 56.1 us; the launch traced here: 55.7 us
  Pallas kernels  18.5 us (33%)
  starting transfers between devices  17.3 us (31%)
  waiting for transfers between devices  16.1 us (29%)
  local copies, waits for them, and re-layouts  1.63 us (3%)
  between operations  1.39 us (2%)
  other arithmetic  0.74 us (1%)
    ppermute x8, waiting for transfers between devices, swap(): return lax.ppermute(array, axis, [(i, i ^ step) for i in range(count)])  9.32 us
    ppermute x8, starting transfers between devices, swap(): return lax.ppermute(array, axis, [(i, i ^ step) for i in range(count)])  8.56 us
    pallas_call x1, Pallas kernels, body(): pl.pallas_call(functools.partial(gather_kernel, subs), in_specs=[VMEM, VM...  6.72 us
    all_to_all x1, starting transfers between devices, body(): requests = lax.all_to_all(requests, 'list', 0, 0, tiled=True)  5.17 us
    all_to_all x1, waiting for transfers between devices, body(): pieces = lax.all_to_all(gathered, 'list', 0, 0, tiled=True)  4.38 us
    pallas_call x1, Pallas kernels, body(): pl.pallas_call(functools.partial(sums_kernel, replicas), in_specs=[VMEM]...  4.32 us
    all_to_all x1, starting transfers between devices, body(): pieces = lax.all_to_all(gathered, 'list', 0, 0, tiled=True)  3.61 us
    pallas_call x1, Pallas kernels, body(): pl.pallas_call(row_sums_kernel, in_specs=[SMEM] + [VMEM] * 2 + [HBM], out...  2.64 us
  transfers between devices with their start and end apart: 10, of which 6 were waited for; matrix products, arithmetic and copies ran while one was open for 0% of the time, Pallas kernels for 18%

profile of v9, /device:TPU:0, one launch (start us, length us, event | category | flops | bytes accessed | tf_op | source)
XLA Modules:
  0.0 55.7 jit_solution(12123085756218271791)
XLA Ops:
  1.3 1.9 %pack.1 = (bf16[8,32,128]{2,1,0:T(8,128)(2,1)}, s32[1,256]{1,0:T(1,128)}) custom-call(s32[1]{0:T(128)S(6)} %copy.9.valid, s32[1,256]{1,0:T(1,128)} %bitcast.17, s32[1,256]{1,0:T(1,128)} %bitcast.18, s32[16,256]{1,0:T(8,128)} %bitcast.13), custom_call_target="tpu_custom_call" | custom-call | flops 1000 | bytes 1000 | tf_op jit(solution)/shard_map/pack/pallas_call | solution.py:282
  3.1 5.2 %all-to-all-start = ((bf16[8,32,128]{2,1,0:T(8,128)(2,1)}), bf16[8,32,128]{2,1,0:T(8,128)(2,1)S(1)}, u32[]{:S(2)}, u32[]{:S(2)}) async-start(bf16[8,32,128]{2,1,0:T(8,128)(2,1)} %get-tuple-element.18), calls=%async_computation | async-start | bytes 131072 | tf_op jit(solution)/shard_map/all_to_all | solution.py:299
  8.3 2.6 %row_sums.1 = (f32[16,72,256]{2,1,0:T(8,128)S(1)}, bf16[1024,1024]{1,0:T(8,128)(2,1)S(1)}) custom-call(s32[1]{0:T(128)S(6)} %copy.9.valid, bf16[256,1024]{1,0:T(8,128)(2,1)} %rows.3, s32[16,256]{1,0:T(8,128)} %bitcast.14, bf16[2048,1024]{1,0:T(8,128)(2,1)} %centres.3), custom_call_target="tpu_custom_call" | custom-call | flops 2147483648 | bytes 4194304 | tf_op jit(solution)/shard_map/row_sums/pallas_call | solution.py:305
  11.0 2.4 %all-to-all-done.requests = bf16[8,32,128]{2,1,0:T(8,128)(2,1)S(1)} async-done(((bf16[8,32,128]{2,1,0:T(8,128)(2,1)}), bf16[8,32,128]{2,1,0:T(8,128)(2,1)S(1)}, u32[]{:S(2)}, u32[]{:S(2)}) %all-to-all-start) | async-done | bytes 65568 | tf_op jit(solution)/shard_map/all_to_all | solution.py:299
  13.3 6.7 %gather.1 = bf16[8,128,1024]{2,1,0:T(8,128)(2,1)} custom-call(bf16[8,32,128]{2,1,0:T(8,128)(2,1)S(1)} %all-to-all-done.requests, bf16[1024,1024]{1,0:T(8,128)(2,1)S(1)} %get-tuple-element.19.held, bf16[2048,1024]{1,0:T(8,128)(2,1)} %centres.3), custom_call_target="tpu_custom_call" | custom-call | flops 4294967296 | bytes 6291456 | tf_op jit(solution)/shard_map/gather/pallas_call | solution.py:327
  20.1 3.6 %all-to-all-start.1 = ((bf16[8,128,1024]{2,1,0:T(8,128)(2,1)}), bf16[8,128,1024]{2,1,0:T(8,128)(2,1)S(1)}, u32[]{:S(2)}, u32[]{:S(2)}) async-start(bf16[8,128,1024]{2,1,0:T(8,128)(2,1)} %gather.1), calls=%async_computation.1 | async-start | bytes 4194304 | tf_op jit(solution)/shard_map/all_to_all | solution.py:342
  23.7 1.6 %copy-done = bf16[8,128,1024]{2,1,0:T(8,128)(2,1)S(1)} copy-done((bf16[8,128,1024]{2,1,0:T(8,128)(2,1)S(1)}, bf16[8,128,1024]{2,1,0:T(8,128)(2,1)}, u32[]{:S(2)}) %copy-start) | copy-done | bytes 2097176
  25.3 4.3 %sums.1 = (f32[4,2,72,256]{3,2,1,0:T(8,128)S(1)}, f32[4,2,72,256]{3,2,1,0:T(8,128)S(1)}) custom-call(bf16[8,32,128]{2,1,0:T(8,128)(2,1)S(1)} %all-to-all-done.requests, bf16[1024,1024]{1,0:T(8,128)(2,1)S(1)} %bitcast.10, f32[16,72,256]{2,1,0:T(8,128)S(1)} %get-tuple-element.20.row_sums), custom_call_target="tpu_custom_call" | custom-call | flops 4294967296 | bytes 4194304 | tf_op jit(solution)/shard_map/sums/pallas_call | solution.py:345
  29.6 0.5 collective-permute-start
  30.1 1.6 %collective-permute-done.got = f32[4,2,72,256]{3,2,1,0:T(8,128)S(1)} collective-permute-done((f32[4,2,72,256]{3,2,1,0:T(8,128)S(1)}, f32[4,2,72,256]{3,2,1,0:T(8,128)S(1)}, u32[]{:S(2)}, u32[]{:S(2)}) %collective-permute-start) | collective-permute-done | bytes 589856 | tf_op jit(solution)/shard_map/ppermute | solution.py:255
  31.9 1.7 %collective-permute-start.1 = (s16[2,72,256]{2,1,0:T(8,128)(2,1)S(1)}, s16[2,72,256]{2,1,0:T(8,128)(2,1)S(1)}, u32[]{:S(2)}, u32[]{:S(2)}) collective-permute-start(s16[2,72,256]{2,1,0:T(8,128)(2,1)S(1)} %get-tuple-element.24), channel_id=1, source_target_pairs={{0,1},{1,0},{2,3},{3,2},{4,5},{5,4},{6,7},{7,6},{8,9},{9,8},{10,11... | collective-permute-start | bytes 221192 | tf_op jit(solution)/shard_map/ppermute | solution.py:255
  33.6 2.6 %collective-permute-start.2 = (s16[2,72,256]{2,1,0:T(8,128)(2,1)S(1)}, s16[2,72,256]{2,1,0:T(8,128)(2,1)S(1)}, u32[]{:S(2)}, u32[]{:S(2)}) collective-permute-start(s16[2,72,256]{2,1,0:T(8,128)(2,1)S(1)} %get-tuple-element.25), channel_id=1, source_target_pairs={{0,2},{1,3},{2,0},{3,1},{4,6},{5,7},{6,4},{7,5},{8,10},{9,11},{10,... | collective-permute-start | bytes 221192 | tf_op jit(solution)/shard_map/ppermute | solution.py:255
  36.1 0.2 collective-permute-start.3
  36.4 0.9 %offsets.1 = f32[256,1024]{1,0:T(8,128)S(1)} custom-call(bf16[256,1024]{1,0:T(8,128)(2,1)S(1)} %copy-done.4, s32[16,256]{1,0:T(8,128)S(1)} %bitcast.15, f32[16,64,256]{2,1,0:T(8,128)S(1)} %bitcast.11), custom_call_target="tpu_custom_call" | custom-call | flops 1073741824 | bytes 2097152 | tf_op jit(solution)/shard_map/offsets/pallas_call | solution.py:318
  37.3 5.2 %collective-permute-done.2.refs_1_ = s16[2,72,256]{2,1,0:T(8,128)(2,1)S(1)} collective-permute-done((s16[2,72,256]{2,1,0:T(8,128)(2,1)S(1)}, s16[2,72,256]{2,1,0:T(8,128)(2,1)S(1)}, u32[]{:S(2)}, u32[]{:S(2)}) %collective-permute-start.2) | collective-permute-done | bytes 73760 | tf_op jit(solution)/shard_map/ppermute | solution.py:255
  42.5 0.3 encode.1.refs_0_
  42.8 1.8 %collective-permute-start.4 = (s16[2,72,256]{2,1,0:T(8,128)(2,1)S(1)}, s16[2,72,256]{2,1,0:T(8,128)(2,1)S(1)}, u32[]{:S(2)}, u32[]{:S(2)}) collective-permute-start(s16[2,72,256]{2,1,0:T(8,128)(2,1)S(1)} %encode.1.refs_0_), channel_id=1, source_target_pairs={{0,8},{4,12},{8,0},{12,4},{16,24},{20,28},{24,16},{28,20},{1,9},{5... | collective-permute-start | bytes 221192 | tf_op jit(solution)/shard_map/ppermute | solution.py:255
  44.6 1.5 %collective-permute-start.5 = (s16[2,72,256]{2,1,0:T(8,128)(2,1)S(1)}, s16[2,72,256]{2,1,0:T(8,128)(2,1)S(1)}, u32[]{:S(2)}, u32[]{:S(2)}) collective-permute-start(s16[2,72,256]{2,1,0:T(8,128)(2,1)S(1)} %encode.1.refs_0_), channel_id=1, source_target_pairs={{0,16},{4,20},{8,24},{12,28},{16,0},{20,4},{24,8},{28,12},{1,17},{... | collective-permute-start | bytes 221192 | tf_op jit(solution)/shard_map/ppermute | solution.py:255
  46.1 0.2 collective-permute-start.6
  46.4 4.4 %all-to-all-done.1 = bf16[8,128,1024]{2,1,0:T(8,128)(2,1)S(1)} async-done(((bf16[8,128,1024]{2,1,0:T(8,128)(2,1)}), bf16[8,128,1024]{2,1,0:T(8,128)(2,1)S(1)}, u32[]{:S(2)}, u32[]{:S(2)}) %all-to-all-start.1) | async-done | bytes 2097184 | tf_op jit(solution)/shard_map/all_to_all | solution.py:342
  50.8 1.5 %errors.1 = f32[1,256]{1,0:T(1,128)} custom-call(s32[1]{0:T(128)S(6)} %copy.9.valid, s32[1,256]{1,0:T(1,128)S(1)} %copy-done.3, f32[256,1024]{1,0:T(8,128)S(1)} %offsets.1, bf16[1024,1024]{1,0:T(8,128)(2,1)S(1)} %bitcast.9), custom_call_target="tpu_custom_call" | custom-call | flops 1000 | bytes 1000 | tf_op jit(solution)/shard_map/errors/pallas_call | solution.py:382
  52.3 1.1 %collective-permute-done.6.refs_3_ = s16[2,72,256]{2,1,0:T(8,128)(2,1)S(1)} collective-permute-done((s16[2,72,256]{2,1,0:T(8,128)(2,1)S(1)}, s16[2,72,256]{2,1,0:T(8,128)(2,1)S(1)}, u32[]{:S(2)}, u32[]{:S(2)}) %collective-permute-start.6) | collective-permute-done | bytes 73760 | tf_op jit(solution)/shard_map/ppermute | solution.py:255
  53.6 1.3 %collective-permute-done.7 = f32[2,64,256]{2,1,0:T(8,128)S(1)} collective-permute-done((f32[2,64,256]{2,1,0:T(8,128)S(1)}, f32[2,64,256]{2,1,0:T(8,128)S(1)}, u32[]{:S(2)}, u32[]{:S(2)}) %collective-permute-start.7) | collective-permute-done | bytes 131104 | tf_op jit(solution)/shard_map/ppermute | solution.py:255
  55.0 0.7 %maximum_bitcast_fusion = f32[4,256,64]{1,2,0:T(8,128)} fusion(f32[2,64,256]{2,1,0:T(8,128)S(1)} %get-tuple-element.35, f32[2,64,256]{2,1,0:T(8,128)S(1)} %get-tuple-element.34), kind=kLoop, calls=%fused_computation | loop fusion | flops 65536 | bytes 524288 | tf_op jit(solution)/shard_map/transpose | solution.py:406
  (17 shorter events, 0.4 us)
Async XLA Ops:
  3.1 10.2 %all-to-all-start = ((bf16[8,32,128]{2,1,0:T(8,128)(2,1)}), bf16[8,32,128]{2,1,0:T(8,128)(2,1)S(1)}, u32[]{:S(2)}, u32[]{:S(2)}) async-start(bf16[8,32,128]{2,1,0:T(8,128)(2,1)} %get-tuple-element.18), calls=%async_computation | async-start | bytes 131072 | tf_op jit(solution)/shard_map/all_to_all | solution.py:299
  20.1 30.7 %all-to-all-start.1 = ((bf16[8,128,1024]{2,1,0:T(8,128)(2,1)}), bf16[8,128,1024]{2,1,0:T(8,128)(2,1)S(1)}, u32[]{:S(2)}, u32[]{:S(2)}) async-start(bf16[8,128,1024]{2,1,0:T(8,128)(2,1)} %gather.1), calls=%async_computation.1 | async-start | bytes 4194304 | tf_op jit(solution)/shard_map/all_to_all | solution.py:342
  23.7 1.6 %copy-start = (bf16[8,128,1024]{2,1,0:T(8,128)(2,1)S(1)}, bf16[8,128,1024]{2,1,0:T(8,128)(2,1)}, u32[]{:S(2)}) copy-start(bf16[8,128,1024]{2,1,0:T(8,128)(2,1)} %gather.1) | copy-start | bytes 6291460
  25.3 11.1 %copy-start.1 = (f32[16,256,64]{1,2,0:T(8,128)S(1)}, f32[16,256,64]{1,2,0:T(8,128)}, u32[]{:S(2)}) copy-start(f32[16,256,64]{1,2,0:T(8,128)} %param.13) | copy-start | bytes 3145732
  25.3 11.1 %copy-start.2 = (s32[256,16]{0,1:T(8,128)S(1)}, s32[256,16]{0,1:T(8,128)}, u32[]{:S(2)}) copy-start(s32[256,16]{0,1:T(8,128)} %param.10) | copy-start | bytes 49156
  25.3 11.1 %copy-start.4 = (bf16[256,1024]{1,0:T(8,128)(2,1)S(1)}, bf16[256,1024]{1,0:T(8,128)(2,1)}, u32[]{:S(2)}) copy-start(bf16[256,1024]{1,0:T(8,128)(2,1)} %rows.3) | copy-start | bytes 1572868
  29.6 2.1 %collective-permute-start = (f32[4,2,72,256]{3,2,1,0:T(8,128)S(1)}, f32[4,2,72,256]{3,2,1,0:T(8,128)S(1)}, u32[]{:S(2)}, u32[]{:S(2)}) collective-permute-start(f32[4,2,72,256]{3,2,1,0:T(8,128)S(1)} %get-tuple-element.22), channel_id=1, source_target_pairs={{0,4},{4,0},{8,12},{12,8},{16,20},{20,16},{24,28},{28,24},{1,5},{5... | collective-permute-start | bytes 1769480 | tf_op jit(solution)/shard_map/ppermute | solution.py:255
  31.9 5.4 %collective-permute-start.1 = (s16[2,72,256]{2,1,0:T(8,128)(2,1)S(1)}, s16[2,72,256]{2,1,0:T(8,128)(2,1)S(1)}, u32[]{:S(2)}, u32[]{:S(2)}) collective-permute-start(s16[2,72,256]{2,1,0:T(8,128)(2,1)S(1)} %get-tuple-element.24), channel_id=1, source_target_pairs={{0,1},{1,0},{2,3},{3,2},{4,5},{5,4},{6,7},{7,6},{8,9},{9,8},{10,11... | collective-permute-start | bytes 221192 | tf_op jit(solution)/shard_map/ppermute | solution.py:255
  33.6 9.0 %collective-permute-start.2 = (s16[2,72,256]{2,1,0:T(8,128)(2,1)S(1)}, s16[2,72,256]{2,1,0:T(8,128)(2,1)S(1)}, u32[]{:S(2)}, u32[]{:S(2)}) collective-permute-start(s16[2,72,256]{2,1,0:T(8,128)(2,1)S(1)} %get-tuple-element.25), channel_id=1, source_target_pairs={{0,2},{1,3},{2,0},{3,1},{4,6},{5,7},{6,4},{7,5},{8,10},{9,11},{10,... | collective-permute-start | bytes 221192 | tf_op jit(solution)/shard_map/ppermute | solution.py:255
  36.1 6.4 %collective-permute-start.3 = (s16[2,72,256]{2,1,0:T(8,128)(2,1)S(1)}, s16[2,72,256]{2,1,0:T(8,128)(2,1)S(1)}, u32[]{:S(2)}, u32[]{:S(2)}) collective-permute-start(s16[2,72,256]{2,1,0:T(8,128)(2,1)S(1)} %get-tuple-element.26), channel_id=1, source_target_pairs={{0,3},{1,2},{2,1},{3,0},{4,7},{5,6},{6,5},{7,4},{8,11},{9,10},{10,... | collective-permute-start | bytes 221192 | tf_op jit(solution)/shard_map/ppermute | solution.py:255
  36.4 14.4 %copy-start.3 = (s32[1,256]{1,0:T(1,128)S(1)}, s32[1,256]{1,0:T(1,128)}, u32[]{:S(2)}) copy-start(s32[1,256]{1,0:T(1,128)} %get-tuple-element.28.position) | copy-start | bytes 3076
  42.8 9.5 %collective-permute-start.4 = (s16[2,72,256]{2,1,0:T(8,128)(2,1)S(1)}, s16[2,72,256]{2,1,0:T(8,128)(2,1)S(1)}, u32[]{:S(2)}, u32[]{:S(2)}) collective-permute-start(s16[2,72,256]{2,1,0:T(8,128)(2,1)S(1)} %encode.1.refs_0_), channel_id=1, source_target_pairs={{0,8},{4,12},{8,0},{12,4},{16,24},{20,28},{24,16},{28,20},{1,9},{5... | collective-permute-start | bytes 221192 | tf_op jit(solution)/shard_map/ppermute | solution.py:255
  44.6 7.7 %collective-permute-start.5 = (s16[2,72,256]{2,1,0:T(8,128)(2,1)S(1)}, s16[2,72,256]{2,1,0:T(8,128)(2,1)S(1)}, u32[]{:S(2)}, u32[]{:S(2)}) collective-permute-start(s16[2,72,256]{2,1,0:T(8,128)(2,1)S(1)} %encode.1.refs_0_), channel_id=1, source_target_pairs={{0,16},{4,20},{8,24},{12,28},{16,0},{20,4},{24,8},{28,12},{1,17},{... | collective-permute-start | bytes 221192 | tf_op jit(solution)/shard_map/ppermute | solution.py:255
  46.1 7.3 %collective-permute-start.6 = (s16[2,72,256]{2,1,0:T(8,128)(2,1)S(1)}, s16[2,72,256]{2,1,0:T(8,128)(2,1)S(1)}, u32[]{:S(2)}, u32[]{:S(2)}) collective-permute-start(s16[2,72,256]{2,1,0:T(8,128)(2,1)S(1)} %encode.1.refs_0_), channel_id=1, source_target_pairs={{0,24},{4,28},{8,16},{12,20},{16,8},{20,12},{24,0},{28,4},{1,25},{... | collective-permute-start | bytes 221192 | tf_op jit(solution)/shard_map/ppermute | solution.py:255
  53.5 1.4 %collective-permute-start.7 = (f32[2,64,256]{2,1,0:T(8,128)S(1)}, f32[2,64,256]{2,1,0:T(8,128)S(1)}, u32[]{:S(2)}, u32[]{:S(2)}) collective-permute-start(f32[2,64,256]{2,1,0:T(8,128)S(1)} %finish.1), channel_id=1, source_target_pairs={{0,4},{4,0},{8,12},{12,8},{16,20},{20,16},{24,28},{28,24},{1,5},{5... | collective-permute-start | bytes 393224 | tf_op jit(solution)/shard_map/ppermute | solution.py:255
